TPU v7x, 32 devices: a whole 2x2x4 slice. The times are simulated.
32 devices in a mesh: blk: 16 (over z, y, x), mp: 2 (over core).
Axes of the slice: x: 2, y: 2, z: 4, core: 2. Of those that a mesh axis runs over, the one named last changes fastest.
Arguments:
- tokens: bfloat16 [4096, 1536], P('blk'), may hold values from -6 to 6
- cotangent: bfloat16 [4096, 1536], P('blk'), may hold values from -6 to 6
- norm_gain: bfloat16 [1536], replicated, may hold values from 0.5 to 1.5
- w_query: bfloat16 [1536, 1536], P('blk', 'mp'), may hold values from -0.15625 to 0.15625
- b_query: bfloat16 [1536], P('mp'), may hold values from -3 to 3
- w_key: bfloat16 [1536, 256], P('blk', 'mp'), may hold values from -0.15625 to 0.15625
- b_key: bfloat16 [256], P('mp'), may hold values from -3 to 3
- w_value: bfloat16 [1536, 256], P('blk', 'mp'), may hold values from -0.15625 to 0.15625
- b_value: bfloat16 [256], P('mp'), may hold values from -3 to 3
- w_out: bfloat16 [1536, 1536], P('mp', 'blk'), may hold values from -2 to 2
- ffn_gain: bfloat16 [1536], replicated, may hold values from 0.5 to 1.5
- w_gate: bfloat16 [1536, 8960], P('blk', 'mp'), may hold values from -0.15625 to 0.15625
- w_up: bfloat16 [1536, 8960], P('blk', 'mp'), may hold values from -0.15625 to 0.15625
- w_down: bfloat16 [8960, 1536], P('mp', 'blk'), may hold values from -0.125 to 0.125
- unit_seq: int32 [4], replicated, may hold values from 0 to 2, as said below
- block_map: int32 [16], replicated, may hold values from 0 to 15, as said below
Outputs:
- mixed: bfloat16 [4096, 1536], P('blk')
- g_tokens: float32 [4096, 1536], P('blk')
- g_norm_gain: float32 [1536], replicated
- g_query: float32 [1536, 1536], P('blk', 'mp')
- g_query_bias: float32 [1536], P('mp')
- g_key: float32 [1536, 256], P('blk', 'mp')
- g_key_bias: float32 [256], P('mp')
- g_value: float32 [1536, 256], P('blk', 'mp')
- g_value_bias: float32 [256], P('mp')
- g_out: float32 [1536, 1536], P('mp', 'blk')
- g_ffn_gain: float32 [1536], replicated
- g_gate: float32 [1536, 8960], P('blk', 'mp')
- g_up: float32 [1536, 8960], P('blk', 'mp')
- g_down: float32 [8960, 1536], P('mp', 'blk')
Inputs may be any that keep to these rules, and one draw needn't show every extreme that they name: `unit_seq`: starts at 0 and rises by 0 or 1 from unit to unit; one sequence, at a place drawn from the seed, covers exactly 2 consecutive units, every other sequence 1 or 4 units. `block_map`: A permutation of the logical token blocks; index 0 of blk holds the block with the first token of the sequence of 2 units and the last index the block with its last token.
All inputs are finite; a program needn't handle non-finite values.
Results may differ from a plain program's by a relative error of at most 0.039.
Values may be sent and summed in bfloat16 or wider, within the bound.
No kernel may reach another device: no remote copies, remote signals or barrier semaphores. Data moves between devices by JAX's collectives and lax.ppermute only.
A program may use at most 320 MiB of HBM per device.

v0:
```python
import jax
import jax.numpy as jnp
from jax import lax
from jax.sharding import PartitionSpec as P

HD = 128
SEG = 1024


epsilon = 1e-06


def rotate(value, cosine, sine):
    half = value.shape[-1] // 2
    first = value[..., :half]
    second = value[..., half:]
    return jnp.concatenate(
        [first * cosine - second * sine, second * cosine + first * sine], axis=-1
    )


def rope_tables(position):
    freq = jnp.power(10000.0, -(jnp.arange(HD // 2, dtype=jnp.float32) * (2.0 / HD)))
    angle = position.astype(jnp.float32)[:, None] * freq[None, :]
    return (jnp.cos(angle)[:, None, :], jnp.sin(angle)[:, None, :])


def token_tables(index, unit_seq, block_map, block_rows):
    count = block_map.shape[0]
    source = index // block_rows
    places = jnp.arange(count, dtype=jnp.int32)
    owner = jnp.sum(jnp.where(source[:, None] == places[None, :], block_map[None, :], 0), axis=1)
    logical = owner * block_rows + index % block_rows
    units = jnp.arange(unit_seq.shape[0], dtype=jnp.int32)
    previous = jnp.concatenate([jnp.full((1,), -1, jnp.int32), unit_seq[:-1]])
    first = lax.cummax(jnp.where(unit_seq != previous, units, 0), axis=0)
    which = (logical // SEG)[:, None] == units[None, :]
    seq = jnp.sum(jnp.where(which, unit_seq[None, :], 0), axis=1)
    begin = jnp.sum(jnp.where(which, first[None, :], 0), axis=1)
    return (seq, logical, logical - begin * SEG)


def block_size(count):
    size = count
    while size > 1536 and size % 2 == 0:
        size = size // 2
    return size


def norm_back(grad, value, inverse, gain):
    scaled = grad * gain
    grad_gain = jnp.sum(grad * value * inverse, axis=0)
    mean_term = jnp.mean(scaled * value, axis=-1, keepdims=True)
    grad_value = inverse * scaled - value * (inverse * inverse * inverse) * mean_term
    return (grad_value, grad_gain)


def shards(
    tokens,
    cotangent,
    norm_gain,
    w_query,
    b_query,
    w_key,
    b_key,
    w_value,
    b_value,
    w_out,
    ffn_gain,
    w_gate,
    w_up,
    w_down,
    unit_seq,
    block_map,
):
    block_rows = tokens.shape[0]
    blocks = lax.axis_size("blk")
    scale = HD ** (-0.5)
    here = lax.axis_index("blk") * block_rows + jnp.arange(block_rows, dtype=jnp.int32)
    query_seq, query_log, query_pos = token_tables(here, unit_seq, block_map, block_rows)
    cosine, sine = rope_tables(query_pos)
    heads = w_query.shape[1] // HD
    query_full, key_full, value_full, gate_full, up_full = (
        lax.all_gather(w_query, "blk", axis=0, tiled=True),
        lax.all_gather(w_key, "blk", axis=0, tiled=True),
        lax.all_gather(w_value, "blk", axis=0, tiled=True),
        lax.all_gather(w_gate, "blk", axis=0, tiled=True),
        lax.all_gather(w_up, "blk", axis=0, tiled=True),
    )
    out_full, down_full = (
        lax.all_gather(w_out, "blk", axis=1, tiled=True),
        lax.all_gather(w_down, "blk", axis=1, tiled=True),
    )
    inputs = tokens.astype(jnp.float32)
    gain_one = norm_gain.astype(jnp.float32)
    inverse_one = lax.rsqrt(jnp.mean(inputs * inputs, axis=-1, keepdims=True) + epsilon)
    normed = (inputs * inverse_one * gain_one).astype(jnp.bfloat16)
    query_lin = jnp.dot(normed, query_full, preferred_element_type=jnp.float32) + b_query.astype(
        jnp.float32
    )
    key_lin = jnp.dot(normed, key_full, preferred_element_type=jnp.float32) + b_key.astype(
        jnp.float32
    )
    value_low = (
        jnp.dot(normed, value_full, preferred_element_type=jnp.float32)
        + b_value.astype(jnp.float32)
    ).astype(jnp.bfloat16)
    query_rot = rotate(query_lin.reshape(block_rows, heads, HD), cosine, sine).astype(jnp.bfloat16)
    query_heads = query_rot.transpose(1, 0, 2)
    key_rot = (
        rotate(key_lin.reshape(block_rows, 1, HD), cosine, sine)
        .reshape(block_rows, HD)
        .astype(jnp.bfloat16)
    )

    def key_blocks(piece):
        keys, values = piece
        count = keys.shape[0]
        size = block_size(count)
        index = jnp.arange(count, dtype=jnp.int32)
        key_seq, key_log, key_place = token_tables(index, unit_seq, block_map, block_rows)
        shape = (count // size, size)
        return (
            keys.reshape(shape + (HD,)),
            values.reshape(shape + (HD,)),
            key_seq.reshape(shape),
            key_log.reshape(shape),
            index.reshape(shape),
        )

    def visible(block_seq, block_log):
        return (query_seq[:, None] == block_seq[None, :]) & (
            block_log[None, :] <= query_log[:, None]
        )

    start_state = (
        jnp.full((heads, block_rows), -1e30, jnp.float32),
        jnp.zeros((heads, block_rows), jnp.float32),
        jnp.zeros((heads, block_rows, HD), jnp.float32),
    )

    def step(state, block):
        key_part, value_part, block_seq, block_log, block_index = block
        mask = visible(block_seq, block_log)

        def compute(inner):
            best, total, accum = inner
            scores = (
                jnp.einsum("hqd,kd->hqk", query_heads, key_part, preferred_element_type=jnp.float32)
                * scale
            )
            scores = jnp.where(mask[None], scores, -1e30)
            new_best = jnp.maximum(best, jnp.max(scores, axis=-1))
            factor = jnp.exp(best - new_best)
            weights = jnp.exp(scores - new_best[..., None])
            total = total * factor + jnp.sum(weights, axis=-1)
            accum = accum * factor[..., None] + jnp.einsum(
                "hqk,kd->hqd",
                weights.astype(jnp.bfloat16),
                value_part,
                preferred_element_type=jnp.float32,
            )
            return (new_best, total, accum)

        return (lax.cond(jnp.any(mask), compute, lambda inner: inner, state), None)

    result, unused = lax.scan(
        step,
        start_state,
        key_blocks(
            (
                lax.all_gather(key_rot, "blk", axis=0, tiled=True),
                lax.all_gather(value_low, "blk", axis=0, tiled=True),
            )
        ),
    )
    best, total, accum = result
    log_total = best + jnp.log(total)
    attended_heads = accum / total[..., None]
    attended_low = (
        attended_heads.transpose(1, 0, 2).reshape(block_rows, heads * HD).astype(jnp.bfloat16)
    )
    attn = lax.psum(
        jnp.dot(attended_low, out_full, preferred_element_type=jnp.float32).astype(jnp.bfloat16),
        "mp",
    ).astype(jnp.float32)
    middle = inputs + attn
    gain_two = ffn_gain.astype(jnp.float32)
    inverse_two = lax.rsqrt(jnp.mean(middle * middle, axis=-1, keepdims=True) + epsilon)
    normed_two = (middle * inverse_two * gain_two).astype(jnp.bfloat16)
    gate = jnp.dot(normed_two, gate_full, preferred_element_type=jnp.float32)
    up = jnp.dot(normed_two, up_full, preferred_element_type=jnp.float32)
    sigmoid_gate = jax.nn.sigmoid(gate)
    silu_gate = gate * sigmoid_gate
    hidden = (silu_gate * up).astype(jnp.bfloat16)
    ffn = lax.psum(
        jnp.dot(hidden, down_full, preferred_element_type=jnp.float32).astype(jnp.bfloat16), "mp"
    ).astype(jnp.float32)
    mixed = (middle + ffn).astype(jnp.bfloat16)
    query_back, key_back, value_back, gate_back, up_back = (
        lax.all_gather(w_query, "blk", axis=0, tiled=True),
        lax.all_gather(w_key, "blk", axis=0, tiled=True),
        lax.all_gather(w_value, "blk", axis=0, tiled=True),
        lax.all_gather(w_gate, "blk", axis=0, tiled=True),
        lax.all_gather(w_up, "blk", axis=0, tiled=True),
    )
    out_back, down_back = (
        lax.all_gather(w_out, "blk", axis=1, tiled=True),
        lax.all_gather(w_down, "blk", axis=1, tiled=True),
    )
    grad_out = cotangent.astype(jnp.float32)
    grad_down_t = jnp.dot(cotangent.T, hidden, preferred_element_type=jnp.float32)
    grad_hidden = jnp.dot(cotangent, down_back.T, preferred_element_type=jnp.float32)
    grad_gate = (grad_hidden * up * sigmoid_gate * (1.0 + gate * (1.0 - sigmoid_gate))).astype(
        jnp.bfloat16
    )
    grad_up = (grad_hidden * silu_gate).astype(jnp.bfloat16)
    grad_gate_w = jnp.dot(normed_two.T, grad_gate, preferred_element_type=jnp.float32)
    grad_up_w = jnp.dot(normed_two.T, grad_up, preferred_element_type=jnp.float32)
    grad_normed_two = jnp.dot(grad_gate, gate_back.T, preferred_element_type=jnp.float32) + jnp.dot(
        grad_up, up_back.T, preferred_element_type=jnp.float32
    )
    grad_normed_two = lax.psum(grad_normed_two.astype(jnp.bfloat16), "mp").astype(jnp.float32)
    grad_middle_norm, grad_gain_two = norm_back(grad_normed_two, middle, inverse_two, gain_two)
    grad_middle = grad_out + grad_middle_norm
    grad_attn = grad_middle.astype(jnp.bfloat16)
    grad_out_t = jnp.dot(grad_attn.T, attended_low, preferred_element_type=jnp.float32)
    grad_attended = jnp.dot(grad_attn, out_back.T, preferred_element_type=jnp.float32).astype(
        jnp.bfloat16
    )
    grad_heads = grad_attended.reshape(block_rows, heads, HD).transpose(1, 0, 2)
    delta = jnp.sum(grad_heads.astype(jnp.float32) * attended_heads, axis=-1)
    back_state = (
        jnp.zeros((heads, block_rows, HD), jnp.float32),
        jnp.zeros((block_rows * blocks, 2 * HD), jnp.float32),
    )

    def step(state, block):
        key_part, value_part, block_seq, block_log, block_index = block
        mask = visible(block_seq, block_log)

        def compute(inner):
            grad_query, grad_kv = inner
            scores = (
                jnp.einsum("hqd,kd->hqk", query_heads, key_part, preferred_element_type=jnp.float32)
                * scale
            )
            scores = jnp.where(mask[None], scores, -1e30)
            probs = jnp.exp(scores - log_total[..., None])
            grad_value = jnp.einsum(
                "hqk,hqd->kd",
                probs.astype(jnp.bfloat16),
                grad_heads,
                preferred_element_type=jnp.float32,
            )
            grad_probs = jnp.einsum(
                "hqd,kd->hqk", grad_heads, value_part, preferred_element_type=jnp.float32
            )
            grad_scores = (probs * (grad_probs - delta[..., None])).astype(jnp.bfloat16)
            grad_query = (
                grad_query
                + jnp.einsum(
                    "hqk,kd->hqd", grad_scores, key_part, preferred_element_type=jnp.float32
                )
                * scale
            )
            grad_key = (
                jnp.einsum(
                    "hqk,hqd->kd", grad_scores, query_heads, preferred_element_type=jnp.float32
                )
                * scale
            )
            update = jnp.concatenate([grad_key, grad_value], axis=1)
            grad_kv = lax.dynamic_update_slice(grad_kv, update, (block_index[0], jnp.int32(0)))
            return (grad_query, grad_kv)

        return (lax.cond(jnp.any(mask), compute, lambda inner: inner, state), None)

    result, unused = lax.scan(
        step,
        back_state,
        key_blocks(
            (
                lax.all_gather(key_rot, "blk", axis=0, tiled=True),
                lax.all_gather(value_low, "blk", axis=0, tiled=True),
            )
        ),
    )
    grad_query_heads, grad_kv_all = result
    grad_kv_mine = lax.psum_scatter(grad_kv_all, "blk", scatter_dimension=0, tiled=True)
    grad_key_mine = grad_kv_mine[:, :HD]
    grad_value_mine = grad_kv_mine[:, HD:]
    grad_q = (
        rotate(grad_query_heads.transpose(1, 0, 2), cosine, -sine)
        .reshape(block_rows, heads * HD)
        .astype(jnp.bfloat16)
    )
    grad_k = (
        rotate(grad_key_mine.reshape(block_rows, 1, HD), cosine, -sine)
        .reshape(block_rows, HD)
        .astype(jnp.bfloat16)
    )
    grad_v = grad_value_mine.astype(jnp.bfloat16)
    grad_query_w = jnp.dot(normed.T, grad_q, preferred_element_type=jnp.float32)
    grad_key_w = jnp.dot(normed.T, grad_k, preferred_element_type=jnp.float32)
    grad_value_w = jnp.dot(normed.T, grad_v, preferred_element_type=jnp.float32)
    grad_normed = jnp.dot(grad_q, query_back.T, preferred_element_type=jnp.float32)
    grad_normed = grad_normed + jnp.dot(grad_k, key_back.T, preferred_element_type=jnp.float32)
    grad_normed = grad_normed + jnp.dot(grad_v, value_back.T, preferred_element_type=jnp.float32)
    grad_normed = lax.psum(grad_normed.astype(jnp.bfloat16), "mp").astype(jnp.float32)
    grad_input_norm, grad_gain_one = norm_back(grad_normed, inputs, inverse_one, gain_one)
    grad_tokens = grad_middle + grad_input_norm
    bias_query = jnp.sum(grad_q.astype(jnp.float32), axis=0)
    bias_key = jnp.sum(grad_k.astype(jnp.float32), axis=0)
    bias_value = jnp.sum(grad_v.astype(jnp.float32), axis=0)
    gain_one_sum, gain_two_sum, bias_query_sum, bias_key_sum, bias_value_sum = lax.psum(
        (grad_gain_one, grad_gain_two, bias_query, bias_key, bias_value), "blk"
    )
    query_part, key_part_w, value_part_w, gate_part, up_part, out_part, down_part = (
        lax.psum_scatter(grad_query_w, "blk", scatter_dimension=0, tiled=True),
        lax.psum_scatter(grad_key_w, "blk", scatter_dimension=0, tiled=True),
        lax.psum_scatter(grad_value_w, "blk", scatter_dimension=0, tiled=True),
        lax.psum_scatter(grad_gate_w, "blk", scatter_dimension=0, tiled=True),
        lax.psum_scatter(grad_up_w, "blk", scatter_dimension=0, tiled=True),
        lax.psum_scatter(grad_out_t, "blk", scatter_dimension=0, tiled=True),
        lax.psum_scatter(grad_down_t, "blk", scatter_dimension=0, tiled=True),
    )
    return (
        mixed,
        grad_tokens,
        gain_one_sum,
        query_part,
        bias_query_sum,
        key_part_w,
        bias_key_sum,
        value_part_w,
        bias_value_sum,
        out_part.T,
        gain_two_sum,
        gate_part,
        up_part,
        down_part.T,
    )


def solution(mesh):
    placed = (
        P("blk", None),
        P("blk", None),
        P(),
        P("blk", "mp"),
        P("mp"),
        P("blk", "mp"),
        P("mp"),
        P("blk", "mp"),
        P("mp"),
        P("mp", "blk"),
        P(),
        P("blk", "mp"),
        P("blk", "mp"),
        P("mp", "blk"),
        P(),
        P(),
    )
    return jax.shard_map(
        shards,
        mesh=mesh,
        in_specs=placed,
        out_specs=(
            P("blk", None),
            P("blk", None),
            P(),
            P("blk", "mp"),
            P("mp"),
            P("blk", "mp"),
            P("mp"),
            P("blk", "mp"),
            P("mp"),
            P("mp", "blk"),
            P(),
            P("blk", "mp"),
            P("blk", "mp"),
            P("mp", "blk"),
        ),
        check_vma=False,
    )
```

profile of v0, /device:TPU:0, one launch (start us, length us, event | category | flops | bytes accessed | tf_op | source)
XLA Modules:
  0.0 2824.5 jit_solution(5199652343332069117)
XLA Ops:
  8.1 44.7 %all_gather.36 = bf16[1536,128]{1,0:T(8,128)(2,1)S(1)} all-gather(bf16[96,128]{1,0:T(8,128)(2,1)} %param.29), channel_id=1, replica_groups=mesh['blk'=16,'mp'=2] {'blk'}, dimensions={0}, use_global_device_ids=true | all-gather | bytes 417792 | tf_op jit(solution)/shard_map/all_gather | solution.py:85
  61.3 37.8 %all_gather.39 = bf16[1536,128]{1,0:T(8,128)(2,1)S(1)} all-gather(bf16[96,128]{1,0:T(8,128)(2,1)S(1)} %copy-done.43), channel_id=1, replica_groups=mesh['blk'=16,'mp'=2] {'blk'}, dimensions={0}, use_global_device_ids=true | all-gather | bytes 417792 | tf_op jit(solution)/shard_map/all_gather | solution.py:86
  114.4 61.7 %all-gather.9.cloned.1.call-done = bf16[1536,768]{1,0:T(8,128)(2,1)} async-done(((bf16[96,768]{1,0:T(8,128)(2,1)}), bf16[1536,768]{1,0:T(8,128)(2,1)}) %all-gather.9.cloned.1.call-update) | async-done | bytes 2359312 | tf_op jit(solution)/shard_map/all_gather | solution.py:84
  179.3 54.3 %all-gather.11.cloned.1.call-done = bf16[4096,128]{1,0:T(8,128)(2,1)} async-done(((bf16[256,128]{1,0:T(8,128)(2,1)}), bf16[4096,128]{1,0:T(8,128)(2,1)}) %all-gather.11.cloned.1.call-update) | async-done | bytes 1048592 | tf_op jit(solution)/shard_map/all_gather | solution.py:173
  233.6 14.3 while.27
  250.6 46.7 %all-gather.13.cloned.1.call-done = bf16[768,1536]{0,1:T(8,128)(2,1)} async-done(((bf16[768,96]{0,1:T(8,128)(2,1)}), bf16[768,1536]{0,1:T(8,128)(2,1)}) %all-gather.13.cloned.1.call-update) | async-done | bytes 2359312 | tf_op jit(solution)/shard_map/all_gather | solution.py:91
  303.4 15.5 all-reduce.6.cloned.1.call-done
  322.4 163.9 %all-gather.15.cloned.1.call-done = bf16[1536,4480]{1,0:T(8,128)(2,1)} async-done(((bf16[96,4480]{1,0:T(8,128)(2,1)}), bf16[1536,4480]{1,0:T(8,128)(2,1)}) %all-gather.15.cloned.1.call-update) | async-done | bytes 13762576 | tf_op jit(solution)/shard_map/all_gather | solution.py:87
  496.7 154.2 %all-gather.17.cloned.1.call-done = bf16[1536,4480]{1,0:T(8,128)(2,1)} async-done(((bf16[96,4480]{1,0:T(8,128)(2,1)}), bf16[1536,4480]{1,0:T(8,128)(2,1)}) %all-gather.17.cloned.1.call-update) | async-done | bytes 13762576 | tf_op jit(solution)/shard_map/all_gather | solution.py:88
  661.2 154.2 %all-gather.19.cloned.1.call-done = bf16[4480,1536]{0,1:T(8,128)(2,1)} async-done(((bf16[4480,96]{0,1:T(8,128)(2,1)}), bf16[4480,1536]{0,1:T(8,128)(2,1)}) %all-gather.19.cloned.1.call-update) | async-done | bytes 13762576 | tf_op jit(solution)/shard_map/all_gather | solution.py:92
  847.7 16.7 all-reduce.8.cloned.1.call-done
  876.5 31.4 %while.28 = (s32[]{:T(128)}, f32[6,256,128]{2,1,0:T(8,128)S(1)}, f32[4096,256]{0,1:T(8,128)}, s32[256]{0:T(256)S(1)}, s32[4,1024]{1,0:T(4,128)}, /*index=5*/s32[...) while((s32[]{:T(128)}, f32[6,256,128]{2,1,0:T(8,128)S(1)}, ...), condition=%wide.region_24.25_spmd.clone, body=%wide.region_20.24_spmd.clone.sunk | while | flops 2030829568 | bytes 38352736 | solution.py:279
  879.2 20.4 conditional.6
  922.4 142.6 %reduce-scatter.11.cloned.1.call-done = f32[256,256]{0,1:T(8,128)} async-done(((f32[4096,256]{0,1:T(8,128)}), f32[256,256]{0,1:T(8,128)}) %reduce-scatter.11.cloned.1.call-update) | async-done | bytes 262160 | tf_op jit(solution)/shard_map/reduce_scatter | solution.py:290
  1082.1 14.9 fusion.125
  1097.4 15.1 fusion.126
  1125.7 27.6 copy.92
  1155.1 75.7 %all-reduce = (f32[1536]{0:T(1024)}, f32[768]{0:T(1024)}, f32[128]{0:T(128)}, f32[128]{0:T(128)}, f32[1536]{0:T(1024)}) all-reduce(f32[1536]{0:T(1024)S(1)} %get-tuple-element.540, f32[768]{0:T(1024)S(1)} %bitcast.156, f32[128]{0:T(128)S(1)} %convert_reduce_fusion.2, ...), channel_id=1, replica_groups=mesh['blk'=16,'mp'=2] {'blk'}, use_global_device_ids=true, to_apply=%region_29.30 | all-reduce | flops 4096 | bytes 32768 | tf_op jit(solution)/shard_map/psum | solution.py:316
  1234.8 141.4 %reduce-scatter.19.cloned.1.call-done = f32[96,768]{1,0:T(8,128)} async-done(((f32[1536,768]{1,0:T(8,128)}), f32[96,768]{1,0:T(8,128)}) %reduce-scatter.19.cloned.1.call-update) | async-done | bytes 294928 | tf_op jit(solution)/shard_map/reduce_scatter | solution.py:325
  1376.1 127.2 %reduce-scatter.15.cloned.1.call-done = f32[96,128]{1,0:T(8,128)} async-done(((f32[1536,128]{1,0:T(8,128)}), f32[96,128]{1,0:T(8,128)}) %reduce-scatter.15.cloned.1.call-update) | async-done | bytes 49168 | tf_op jit(solution)/shard_map/reduce_scatter | solution.py:321
  1503.3 127.1 %reduce-scatter.17.cloned.1.call-done = f32[96,128]{1,0:T(8,128)} async-done(((f32[1536,128]{1,0:T(8,128)}), f32[96,128]{1,0:T(8,128)}) %reduce-scatter.17.cloned.1.call-update) | async-done | bytes 49168 | tf_op jit(solution)/shard_map/reduce_scatter | solution.py:322
  1630.5 396.0 %reduce-scatter.21.cloned.1.call-done = f32[96,4480]{1,0:T(8,128)} async-done(((f32[1536,4480]{1,0:T(8,128)}), f32[96,4480]{1,0:T(8,128)}) %reduce-scatter.21.cloned.1.call-update) | async-done | bytes 1720336 | tf_op jit(solution)/shard_map/reduce_scatter | solution.py:323
  2026.5 394.8 %reduce-scatter.23.cloned.1.call-done = f32[96,4480]{1,0:T(8,128)} async-done(((f32[1536,4480]{1,0:T(8,128)}), f32[96,4480]{1,0:T(8,128)}) %reduce-scatter.23.cloned.1.call-update) | async-done | bytes 1720336 | tf_op jit(solution)/shard_map/reduce_scatter | solution.py:324
  2421.3 395.9 %reduce-scatter.25.cloned.1.call-done = f32[96,4480]{1,0:T(8,128)} async-done(((f32[1536,4480]{1,0:T(8,128)}), f32[96,4480]{1,0:T(8,128)}) %reduce-scatter.25.cloned.1.call-update) | async-done | bytes 1720336
  (280 shorter events, 199.6 us)
Async XLA Ops:
  7.2 104.9 %all-gather.21.cloned.1.call-start = ((), (), s32[]{:S(2)}) async-start(), calls=%async_computation.23 | async-start | bytes 1114112 | tf_op jit(solution)/shard_map/all_gather | solution.py:172
  60.4 115.6 %all-gather.9.cloned.1.call-start = ((), (), s32[]{:S(2)}) async-start(), calls=%async_computation.8 | async-start | bytes 2506752 | tf_op jit(solution)/shard_map/all_gather | solution.py:84
  61.2 172.3 %all-gather.11.cloned.1.call-start = ((), (), s32[]{:S(2)}) async-start(), calls=%async_computation.9 | async-start | bytes 1114112 | tf_op jit(solution)/shard_map/all_gather | solution.py:173
  100.9 196.4 %all-gather.13.cloned.1.call-start = ((), (), s32[]{:S(2)}) async-start(), calls=%async_computation.10 | async-start | bytes 2506752 | tf_op jit(solution)/shard_map/all_gather | solution.py:91
  101.5 217.4 %all-reduce.6.cloned.1.call-start = ((), (), s32[]{:S(2)}) async-start(), calls=%async_computation.11 | async-start | bytes 1572864 | tf_op jit(solution)/shard_map/psum | solution.py:183
  300.7 185.6 %all-gather.15.cloned.1.call-start = ((), (), s32[]{:S(2)}) async-start(), calls=%async_computation.12 | async-start | bytes 14622720 | tf_op jit(solution)/shard_map/all_gather | solution.py:87
  301.3 349.6 %all-gather.17.cloned.1.call-start = ((), (), s32[]{:S(2)}) async-start(), calls=%async_computation.13 | async-start | bytes 14622720 | tf_op jit(solution)/shard_map/all_gather | solution.py:88
  302.1 513.4 %all-gather.19.cloned.1.call-start = ((), (), s32[]{:S(2)}) async-start(), calls=%async_computation.14 | async-start | bytes 14622720 | tf_op jit(solution)/shard_map/all_gather | solution.py:92
  302.8 561.6 %all-reduce.8.cloned.1.call-start = ((), (), s32[]{:S(2)}) async-start(), calls=%async_computation.15 | async-start | bytes 1572864 | tf_op jit(solution)/shard_map/psum | solution.py:223
  303.4 183.0 %copy-start.27 = (f32[1536]{0:T(1024)}, f32[1536]{0:T(1024)S(1)}, u32[]{:S(2)}) copy-start(f32[1536]{0:T(1024)S(1)} %convert_element_type.153) | copy-start | bytes 18436
  321.0 165.4 %copy-start.40 = (f32[256]{0:T(256)}, f32[256]{0:T(256)S(1)}, u32[]{:S(2)}) copy-start(f32[256]{0:T(256)S(1)} %get-tuple-element.638) | copy-start | bytes 3076
  322.4 328.5 %copy-start.7 = (bf16[256,1536]{1,0:T(8,128)(2,1)}, bf16[256,1536]{1,0:T(8,128)(2,1)S(1)}, u32[]{:S(2)}) copy-start(bf16[256,1536]{1,0:T(8,128)(2,1)S(1)} %multiply_convert_fusion.3) | copy-start | bytes 2359300
  496.7 318.8 %copy-start.5 = (bf16[256,1536]{1,0:T(8,128)(2,1)S(1)}, bf16[256,1536]{1,0:T(8,128)(2,1)}, u32[]{:S(2)}) copy-start(bf16[256,1536]{1,0:T(8,128)(2,1)} %param.25) | copy-start | bytes 2359300
  846.8 218.1 %reduce-scatter.11.cloned.1.call-start = ((), (), s32[]{:S(2)}) async-start(), calls=%async_computation.16 | async-start | bytes 4456448 | tf_op jit(solution)/shard_map/reduce_scatter | solution.py:290
  908.0 245.5 %all-reduce.10.cloned.1.call-start = ((), (), s32[]{:S(2)}) async-start(), calls=%async_computation.25 | async-start | bytes 3145728 | tf_op jit(solution)/shard_map/psum | solution.py:196
  919.8 146.8 %copy-start.54 = (f32[64]{0:T(128)S(1)}, f32[64]{0:T(128)}, u32[]{:S(2)}) copy-start(f32[64]{0:T(128)} %copy-done.53) | copy-start | bytes 772
  919.8 147.7 %copy-start.13 = (bf16[1536,128]{1,0:T(8,128)(2,1)S(1)}, bf16[1536,128]{1,0:T(8,128)(2,1)}, u32[]{:S(2)}) copy-start(bf16[1536,128]{1,0:T(8,128)(2,1)} %copy-done.12) | copy-start | bytes 1179652
  1069.3 165.5 %reduce-scatter.13.cloned.1.call-start = ((), (), s32[]{:S(2)}) async-start(), calls=%async_computation.17 | async-start | bytes 5013504 | tf_op jit(solution)/shard_map/reduce_scatter | solution.py:320
  1072.6 303.6 %reduce-scatter.19.cloned.1.call-start = ((), (), s32[]{:S(2)}) async-start(), calls=%async_computation.20 | async-start | bytes 5013504 | tf_op jit(solution)/shard_map/reduce_scatter | solution.py:325
  1078.4 424.9 %reduce-scatter.15.cloned.1.call-start = ((), (), s32[]{:S(2)}) async-start(), calls=%async_computation.18 | async-start | bytes 835584 | tf_op jit(solution)/shard_map/reduce_scatter | solution.py:321
  1080.5 549.9 %reduce-scatter.17.cloned.1.call-start = ((), (), s32[]{:S(2)}) async-start(), calls=%async_computation.19 | async-start | bytes 835584 | tf_op jit(solution)/shard_map/reduce_scatter | solution.py:322
  1082.0 944.4 %reduce-scatter.21.cloned.1.call-start = ((), (), s32[]{:S(2)}) async-start(), calls=%async_computation.21 | async-start | bytes 29245440 | tf_op jit(solution)/shard_map/reduce_scatter | solution.py:323
  1097.0 1324.2 %reduce-scatter.23.cloned.1.call-start = ((), (), s32[]{:S(2)}) async-start(), calls=%async_computation.22 | async-start | bytes 29245440 | tf_op jit(solution)/shard_map/reduce_scatter | solution.py:324
  1112.5 1704.7 %reduce-scatter.25.cloned.1.call-start = ((), (), s32[]{:S(2)}) async-start(), calls=%async_computation.24 | async-start | bytes 29245440
  (55 other events, 1624.4 us)
Sparse Core Ops, SparseCore 0:
  60.6 51.5 all-gather.20
  114.9 61.1 all-gather.8
  179.4 54.0 all-gather.10
  236.2 61.0 all-gather.12
  300.9 18.0 all-reduce.5
  322.0 164.3 all-gather.14
  489.5 161.3 all-gather.16
  654.1 161.3 all-gather.18
  847.0 17.3 all-reduce.7
  908.1 156.7 reduce-scatter.10
  1069.4 20.0 all-reduce.9
  1095.9 138.5 reduce-scatter.12
  1240.3 135.8 reduce-scatter.18
  1382.0 121.3 reduce-scatter.14
  1509.1 121.2 reduce-scatter.16
  1637.9 388.4 reduce-scatter.20
  2032.9 388.3 reduce-scatter.22
  2428.8 388.4 reduce-scatter.24
where the time goes:
time: 2830 us; the launch traced here: 2820 us
  waiting for transfers between devices  2400 us (85%)
  blocking collectives  158 us (6%)
  matrix products  148 us (5%)
  local copies, waits for them, and re-layouts  51 us (2%)
  other arithmetic  37.7 us (1%)
    unnamed x19, waiting for transfers between devices  399 us
    reduce_scatter x1, waiting for transfers between devices, shards(): lax.psum_scatter(grad_gate_w, 'blk', scatter_dimension=0, tiled=True)  396 us
    reduce_scatter x1, waiting for transfers between devices, shards(): lax.psum_scatter(grad_up_w, 'blk', scatter_dimension=0, tiled=True)  395 us
    all_gather x1, waiting for transfers between devices, shards(): lax.all_gather(w_gate, 'blk', axis=0, tiled=True)  164 us
    all_gather x1, waiting for transfers between devices, shards(): lax.all_gather(w_down, 'blk', axis=1, tiled=True)  154 us
    all_gather x1, waiting for transfers between devices, shards(): lax.all_gather(w_up, 'blk', axis=0, tiled=True)  154 us
    reduce_scatter x1, waiting for transfers between devices, shards(): lax.psum_scatter(grad_kv_all, 'blk', scatter_dimension=0, tiled=True)  143 us
    reduce_scatter x1, waiting for transfers between devices, shards(): lax.psum_scatter(grad_out_t, 'blk', scatter_dimension=0, tiled=True)  141 us
  transfers between devices with their start and end apart: 18, of which 16 were waited for; matrix products, arithmetic and copies ran while one was open for 5% of the time, Pallas kernels for 0%

commit v1 on v0

v1 whole, which is shorter than its diff:
```python
import functools

import jax
import jax.numpy as jnp
from jax import lax
from jax.experimental import pallas as pl
from jax.experimental.pallas import tpu as pltpu
from jax.sharding import Mesh
from jax.sharding import PartitionSpec as P

HD = 128
SEG = 1024
LOG2E = 1.4426950408889634
BIG = -1e30
BF = jnp.bfloat16
F32 = jnp.float32

epsilon = 1e-06


def bit_axis(bit):
    return ("x", "y", "a")[bit] if bit < 3 else "h", 1 if bit < 3 else 1 << (bit - 3)


def flip(value, bit):
    axis, mask = bit_axis(bit)
    return lax.ppermute(value, axis, [(i, i ^ mask) for i in range(lax.axis_size(axis))])


def mine(bit):
    axis, mask = bit_axis(bit)
    return (lax.axis_index(axis) // mask) % 2


def swap_mp(value):
    return lax.ppermute(value, "mp", [(0, 1), (1, 0)])


def halves(value, which):
    return lax.dynamic_index_in_dim(value, which, 0, keepdims=False)


def gather_bits(value, order):
    rows, width = value.shape
    have = []
    for bit in order:
        at = sum(1 for b in have if b > bit)
        other = flip(value, bit)
        value = jnp.where(
            mine(bit) == 0, jnp.stack([value, other], at), jnp.stack([other, value], at)
        )
        have.append(bit)
    return value.reshape(-1, width)


def scatter_bits(value, order, blocks):
    width = value.shape[-1]
    have = sorted(order, reverse=True)
    value = value.reshape((2,) * len(order) + (-1, width))
    for bit in order:
        at = have.index(bit)
        me = mine(bit)
        keep = lax.dynamic_index_in_dim(value, me, at, keepdims=False)
        send = lax.dynamic_index_in_dim(value, 1 - me, at, keepdims=False)
        value = (keep.astype(F32) + flip(send, bit).astype(F32)).astype(BF)
        have.remove(bit)
    return value


CUBE = ((0, 1, 2), (1, 2, 0), (2, 0, 1))


def cube_parts(rows):
    units = rows // 8
    sizes = [(units + 2 - i) // 3 * 8 for i in range(3)]
    return sizes


def cube_gather(value):
    parts, at = [], 0
    for size in cube_parts(value.shape[0]):
        parts.append(value[at : at + size])
        at += size
    for step in range(3):
        parts = [
            jnp.concatenate([part, flip(part, order[step])], 0) for part, order in zip(parts, CUBE)
        ]
    return jnp.concatenate(parts, 0)


def cube_scatter(value, rows):
    parts, at = [], 0
    for size in cube_parts(rows):
        parts.append(value[at : at + 8 * size])
        at += 8 * size
    for step in range(3):
        new = []
        for part, order in zip(parts, CUBE):
            half = part.shape[0] // 2
            other = flip(part[half:], order[2 - step])
            total = part[:half].astype(F32) + other.astype(F32)
            new.append(total if step == 2 else total.astype(BF))
        parts = new
    return jnp.concatenate(parts, 0)


def slot_gather(value, order):
    for bit in order:
        value = jnp.concatenate([value, flip(value, bit)], 0)
    return value


def slot_scatter(value, order):
    for bit in order:
        half = value.shape[0] // 2
        value = value[:half].astype(F32) + flip(value[half:], bit).astype(F32)
        if bit != order[-1]:
            value = value.astype(BF)
    return value


def slot_places(order):
    places = [0]
    for bit in order:
        places = places + [p ^ (1 << bit) for p in places]
    return places


def rotate(value, cosine, sine):
    half = value.shape[-1] // 2
    first = value[..., :half]
    second = value[..., half:]
    return jnp.concatenate(
        [first * cosine - second * sine, second * cosine + first * sine], axis=-1
    )


def rope_tables(position):
    freq = jnp.power(10000.0, -(jnp.arange(HD // 2, dtype=F32) * (2.0 / HD)))
    angle = position.astype(F32)[:, None] * freq[None, :]
    return (jnp.cos(angle)[:, None, :], jnp.sin(angle)[:, None, :])


def look(table, index):
    places = jnp.arange(table.shape[0], dtype=jnp.int32)
    return jnp.sum(jnp.where(index[:, None] == places[None, :], table[None, :], 0), axis=1)


def norm_back(grad, value, inverse, gain):
    scaled = grad * gain
    grad_gain = jnp.sum(grad * value * inverse, axis=0)
    mean_term = jnp.mean(scaled * value, axis=-1, keepdims=True)
    grad_value = inverse * scaled - value * (inverse * inverse * inverse) * mean_term
    return (grad_value, grad_gain)


NT = (((1,), (1,)), ((), ()))
TN = (((0,), (0,)), ((), ()))


def dot(left, right, dims=(((1,), (0,)), ((), ()))):
    return lax.dot_general(left, right, dims, preferred_element_type=F32)


def attend_kernel(vis, vat, q_ref, k_ref, v_ref, o_ref, low_ref, lse_ref, acc, top, tot):
    rows, width = q_ref.shape
    heads = width // HD
    factor = HD ** (-0.5) * LOG2E

    def block(place, first):
        key = k_ref[place]
        value = v_ref[vat[place]]
        if first:
            mask = lax.broadcasted_iota(jnp.int32, (rows, rows), 0) >= lax.broadcasted_iota(
                jnp.int32, (rows, rows), 1
            )
        for h in range(heads):
            cols = slice(h * HD, (h + 1) * HD)
            scores = dot(q_ref[:, cols], key, NT) * factor
            if first:
                scores = jnp.where(mask, scores, BIG)
                best = jnp.max(scores, axis=1, keepdims=True)
                weights = jnp.exp2(scores - best)
                tot[h] = jnp.sum(weights, axis=1, keepdims=True)
                acc[:, cols] = dot(weights.astype(BF), value)
            else:
                old = top[h]
                best = jnp.maximum(old, jnp.max(scores, axis=1, keepdims=True))
                weights = jnp.exp2(scores - best)
                scale = jnp.exp2(old - best)
                tot[h] = tot[h] * scale + jnp.sum(weights, axis=1, keepdims=True)
                acc[:, cols] = acc[:, cols] * scale + dot(weights.astype(BF), value)
            top[h] = best

    block(0, True)

    def step(place, carry):
        @pl.when(vis[place] == 1)
        def _():
            block(place, False)

        return carry

    lax.fori_loop(1, k_ref.shape[0], step, 0)
    for h in range(heads):
        cols = slice(h * HD, (h + 1) * HD)
        total = tot[h]
        out = acc[:, cols] / total
        o_ref[:, cols] = out
        low_ref[:, cols] = out.astype(BF)
        lse_ref[:, cols] = jnp.broadcast_to(top[h] + jnp.log(total) * LOG2E, (rows, HD))


def attend(vis, vat, query, keys, values):
    rows, width = query.shape
    heads = width // HD
    smem = pl.BlockSpec(memory_space=pltpu.SMEM)
    vmem = pl.BlockSpec(memory_space=pltpu.VMEM)
    return pl.pallas_call(
        attend_kernel,
        out_shape=(
            jax.ShapeDtypeStruct((rows, width), F32),
            jax.ShapeDtypeStruct((rows, width), BF),
            jax.ShapeDtypeStruct((rows, width), F32),
        ),
        in_specs=[smem, smem, vmem, vmem, vmem],
        out_specs=(vmem, vmem, vmem),
        scratch_shapes=[
            pltpu.VMEM((rows, width), F32),
            pltpu.VMEM((heads, rows, 1), F32),
            pltpu.VMEM((heads, rows, 1), F32),
        ],
        compiler_params=pltpu.CompilerParams(vmem_limit_bytes=40 * 2**20),
        cost_estimate=pl.CostEstimate(
            flops=4 * rows * width * 2048, bytes_accessed=8 * 2**20, transcendentals=rows * 6 * 2048
        ),
    )(vis, vat, query, keys, values)


def attend_back_kernel(
    vis, vat, q_ref, k_ref, v_ref, do_ref, o_ref, lse_ref, dq_ref, dk_ref, dv_ref, delta
):
    rows, width = q_ref.shape
    heads = width // HD
    scale = HD ** (-0.5)
    for h in range(heads):
        cols = slice(h * HD, (h + 1) * HD)
        delta[h] = jnp.sum(do_ref[:, cols].astype(F32) * o_ref[:, cols], axis=1, keepdims=True)
    dk_ref[...] = jnp.zeros_like(dk_ref)
    dv_ref[...] = jnp.zeros_like(dv_ref)

    def block(place, first):
        key = k_ref[place]
        value = v_ref[vat[place]]
        if first:
            mask = lax.broadcasted_iota(jnp.int32, (rows, rows), 0) >= lax.broadcasted_iota(
                jnp.int32, (rows, rows), 1
            )
        dk = jnp.zeros((rows, HD), F32)
        dv = jnp.zeros((rows, HD), F32)
        for h in range(heads):
            cols = slice(h * HD, (h + 1) * HD)
            query = q_ref[:, cols]
            grad = do_ref[:, cols]
            probs = jnp.exp2(
                dot(query, key, NT) * (scale * LOG2E) - lse_ref[:, h * HD : h * HD + 1]
            )
            if first:
                probs = jnp.where(mask, probs, 0.0)
            dv = dv + dot(probs.astype(BF), grad, TN)
            dprobs = dot(grad, value, NT)
            dscores = (probs * (dprobs - delta[h])).astype(BF)
            dk = dk + dot(dscores, query, TN)
            dq = dot(dscores, key) * scale
            if first:
                dq_ref[:, cols] = dq
            else:
                dq_ref[:, cols] = dq_ref[:, cols] + dq
        dk_ref[place] = (dk * scale).astype(BF)
        dv_ref[vat[place]] = dv.astype(BF)

    block(0, True)

    def step(place, carry):
        @pl.when(vis[place] == 1)
        def _():
            block(place, False)

        return carry

    lax.fori_loop(1, k_ref.shape[0], step, 0)


def attend_back(vis, vat, query, keys, values, grad, out, lse):
    rows, width = query.shape
    heads = width // HD
    smem = pl.BlockSpec(memory_space=pltpu.SMEM)
    vmem = pl.BlockSpec(memory_space=pltpu.VMEM)
    return pl.pallas_call(
        attend_back_kernel,
        out_shape=(
            jax.ShapeDtypeStruct((rows, width), F32),
            jax.ShapeDtypeStruct(keys.shape, BF),
            jax.ShapeDtypeStruct(values.shape, BF),
        ),
        in_specs=[smem, smem] + [vmem] * 6,
        out_specs=(vmem, vmem, vmem),
        scratch_shapes=[pltpu.VMEM((heads, rows, 1), F32)],
        compiler_params=pltpu.CompilerParams(vmem_limit_bytes=48 * 2**20),
        cost_estimate=pl.CostEstimate(
            flops=10 * rows * width * 2048,
            bytes_accessed=16 * 2**20,
            transcendentals=rows * 6 * 2048,
        ),
    )(vis, vat, query, keys, values, grad, out, lse)


def shards(
    tokens,
    cotangent,
    norm_gain,
    w_query,
    b_query,
    w_key,
    b_key,
    w_value,
    b_value,
    w_out,
    ffn_gain,
    w_gate,
    w_up,
    w_down,
    unit_seq,
    block_map,
):
    rows, model = tokens.shape
    blocks = block_map.shape[0]
    bits = blocks.bit_length() - 1
    high = list(range(3, bits))
    low_rows = rows // 2
    width = w_query.shape[1]
    heads = width // HD
    hidden_here = w_gate.shape[1]
    slab = w_gate.shape[0]
    part = -(-hidden_here // 512) * 128
    core = lax.axis_index("mp")
    cube_a = lax.axis_index("a")
    cross = [(1, 2), (2, 1)]
    me = lax.axis_index(("h", "a", "y", "x"))

    order_k = tuple(reversed(high)) + (2, 0, 1)
    order_v = tuple(reversed(high)) + (2, 1, 0)
    place_k = slot_places(order_k)
    place_v = slot_places(order_v)
    vat = jnp.array([place_v.index(s) for s in place_k], jnp.int32)
    per_unit = SEG // rows
    units = jnp.arange(unit_seq.shape[0], dtype=jnp.int32)
    previous = jnp.concatenate([jnp.full((1,), -1, jnp.int32), unit_seq[:-1]])
    first_unit = lax.cummax(jnp.where(unit_seq != previous, units, 0), axis=0)
    others = jnp.bitwise_xor(me, jnp.array(place_k, jnp.int32))
    logical = look(block_map, others)
    seqs = look(unit_seq, logical // per_unit)
    vis = ((seqs == seqs[0]) & (logical < logical[0])).astype(jnp.int32)
    begin = look(first_unit, logical[:1] // per_unit)
    position = logical[0] * rows - begin[0] * SEG + jnp.arange(rows, dtype=jnp.int32)
    cosine, sine = rope_tables(position)

    w_one = w_query[:, : width - 2 * HD]
    w_two = jnp.concatenate([w_query[:, width - 2 * HD :], w_key, w_value], axis=1)
    order_w1 = tuple(reversed(high)) + (2, 0, 1)
    order_w2 = tuple(reversed(high)) + (2, 1, 0)
    w_one = gather_bits(w_one, order_w1)
    w_two = gather_bits(w_two, order_w2)
    out_t = w_out.T
    half_out = width // 2
    out_one = gather_bits(out_t[:, :half_out], order_w1)
    out_two = gather_bits(out_t[:, half_out:], order_w2)
    out_full = jnp.concatenate([out_one, out_two], axis=1)

    def quarter(weight):
        weight = jnp.pad(weight, ((0, 0), (0, 4 * part - hidden_here)))
        return weight.reshape(slab, 4, part).transpose(1, 0, 2)

    def spread(pack):
        other = lax.ppermute(pack, ("a", "mp"), cross)
        pack = jnp.where(cube_a == core, pack, other)
        pack = lax.all_to_all(pack, ("y", "x"), 0, 0, tiled=True)
        pack = pack.reshape(1, -1, pack.shape[-1])
        for bit in high:
            other = flip(pack, bit)
            pack = jnp.where(
                mine(bit) == 0,
                jnp.concatenate([pack, other], 0),
                jnp.concatenate([other, pack], 0),
            )
        other = swap_mp(pack)
        pack = jnp.where(
            core == 0, jnp.stack([pack, other], 1), jnp.stack([other, pack], 1)
        )
        return pack.reshape(-1, pack.shape[-1])

    def collect(grad):
        n = grad.shape[-1]
        grad = grad.reshape(blocks // 8, 2, 4 * slab, n)
        keep = lax.dynamic_index_in_dim(grad, core, 1, keepdims=False)
        send = lax.dynamic_index_in_dim(grad, 1 - core, 1, keepdims=False)
        grad = (keep.astype(F32) + swap_mp(send).astype(F32)).astype(BF)
        for bit in reversed(high):
            grad = grad.reshape(2, -1, 4 * slab, n)
            keep = halves(grad, mine(bit))
            send = halves(grad, 1 - mine(bit))
            grad = (keep.astype(F32) + flip(send, bit).astype(F32)).astype(BF)
        grad = grad.reshape(4, slab, n)
        grad = lax.all_to_all(grad, ("y", "x"), 0, 0, tiled=True)
        other = lax.ppermute(grad, ("a", "mp"), cross)
        return jnp.where(cube_a == core, grad, other)

    def unpack(grad):
        return grad.transpose(1, 0, 2).reshape(slab, 4 * part)[:, :hidden_here].astype(F32)

    gate_up = spread(jnp.concatenate([quarter(w_gate), quarter(w_up)], axis=2))
    down_t = spread(quarter(w_down.T))

    def my_half(value):
        return halves(value.reshape((2, low_rows) + value.shape[1:]), core)

    cot_cube = cube_gather(my_half(cotangent))

    inputs = tokens.astype(F32)
    gain_one = norm_gain.astype(F32)
    inverse_one = lax.rsqrt(jnp.mean(inputs * inputs, axis=-1, keepdims=True) + epsilon)
    normed = (inputs * inverse_one * gain_one).astype(BF)
    lin_two = dot(normed, w_two)
    key_lin = lin_two[:, 2 * HD : 3 * HD] + b_key.astype(F32)
    value_low = (lin_two[:, 3 * HD :] + b_value.astype(F32)).astype(BF)
    key_rot = rotate(key_lin, cosine[:, 0], sine[:, 0]).astype(BF)
    keys = slot_gather(key_rot[None], order_k)
    values = slot_gather(value_low[None], order_v)
    lin_one = dot(normed, w_one)
    query_lin = jnp.concatenate([lin_one, lin_two[:, : 2 * HD]], axis=1) + b_query.astype(F32)
    query = (
        rotate(query_lin.reshape(rows, heads, HD), cosine, sine).reshape(rows, width).astype(BF)
    )
    attended, attended_low, lse = attend(vis, vat, query, keys, values)
    attn = dot(attended_low, out_full, NT).astype(BF).reshape(2, low_rows, model)
    attn = halves(attn, core).astype(F32) + swap_mp(halves(attn, 1 - core)).astype(F32)
    middle = my_half(tokens).astype(F32) + attn
    gain_two = ffn_gain.astype(F32)
    inverse_two = lax.rsqrt(jnp.mean(middle * middle, axis=-1, keepdims=True) + epsilon)
    normed_two = (middle * inverse_two * gain_two).astype(BF)

    cube_two = cube_gather(normed_two)
    grad_hidden = dot(cot_cube, down_t)
    both = dot(cube_two, gate_up)
    gate = both[:, :part]
    up = both[:, part:]
    sigmoid_gate = jax.nn.sigmoid(gate)
    silu_gate = gate * sigmoid_gate
    hidden = (silu_gate * up).astype(BF)
    grad_gate = (grad_hidden * up * sigmoid_gate * (1.0 + gate * (1.0 - sigmoid_gate))).astype(BF)
    grad_up = (grad_hidden * silu_gate).astype(BF)
    grad_both = jnp.concatenate([grad_gate, grad_up], axis=1)
    grad_two = cube_scatter(dot(grad_both, gate_up, NT).astype(BF), low_rows)
    ffn = cube_scatter(dot(hidden, down_t, NT).astype(BF), low_rows)
    mixed_half = (middle + ffn).astype(BF)

    def whole(own):
        other = swap_mp(own)
        return jnp.where(
            core == 0, jnp.concatenate([own, other], 0), jnp.concatenate([other, own], 0)
        )

    mixed = whole(mixed_half)
    grads_down = collect(dot(cot_cube, hidden, TN).astype(BF))
    grads_both = collect(dot(cube_two, grad_both, TN).astype(BF))

    cot_half = my_half(cotangent).astype(F32)
    grad_middle_norm, grad_gain_two = norm_back(grad_two, middle, inverse_two, gain_two)
    grad_middle_half = cot_half + grad_middle_norm
    grad_attn = whole(grad_middle_half.astype(BF))
    grad_middle = whole(grad_middle_half)
    grad_attended = dot(grad_attn, out_full).astype(BF)
    grad_query_rot, grad_keys, grad_values = attend_back(
        vis, vat, query, keys, values, grad_attended, attended, lse
    )
    back_k = tuple(reversed(order_k))
    back_v = tuple(reversed(order_v))
    grad_key_mine = slot_scatter(grad_keys, back_k)[0]
    grad_value_mine = slot_scatter(grad_values, back_v)[0]
    grad_q = (
        rotate(grad_query_rot.reshape(rows, heads, HD), cosine, -sine)
        .reshape(rows, width)
        .astype(BF)
    )
    grad_k = rotate(grad_key_mine, cosine[:, 0], -sine[:, 0]).astype(BF)
    grad_v = grad_value_mine.astype(BF)

    def scatter_two(grad):
        at = grad.shape[1] // 2
        return jnp.concatenate(
            [
                scatter_bits(grad[:, :at], tuple(reversed(order_w1)), blocks),
                scatter_bits(grad[:, at:], tuple(reversed(order_w2)), blocks),
            ],
            axis=1,
        ).astype(F32)

    out_part = scatter_two(dot(grad_attn, attended_low, TN).astype(BF))
    query_part = scatter_two(dot(normed, grad_q, TN).astype(BF))
    grad_kv = jnp.concatenate([grad_k, grad_v], axis=1)
    kv_part = scatter_two(dot(normed, grad_kv, TN).astype(BF))
    at = width - 2 * HD
    grad_normed = dot(grad_q[:, :at], w_one, NT) + dot(
        jnp.concatenate([grad_q[:, at:], grad_kv], axis=1), w_two, NT
    )
    grad_normed = grad_normed.astype(BF)
    grad_normed = grad_normed.astype(F32) + swap_mp(grad_normed).astype(F32)
    grad_input_norm, grad_gain_one = norm_back(grad_normed, inputs, inverse_one, gain_one)
    grad_tokens = grad_middle + grad_input_norm
    bias_query = jnp.sum(grad_q.astype(F32), axis=0)
    bias_kv = jnp.sum(grad_kv.astype(F32), axis=0)

    gain_two_sum = grad_gain_two + swap_mp(grad_gain_two)
    small = jnp.concatenate([grad_gain_one, gain_two_sum, bias_query, bias_kv]).reshape(-1, 128)
    for bit in range(bits):
        small = small + flip(small, bit)
    small = small.reshape(-1)
    gain_one_sum = small[:model]
    gain_two_sum = small[model : 2 * model]
    bias_query_sum = small[2 * model : 2 * model + width]
    bias_key_sum = small[2 * model + width : 2 * model + width + HD]
    bias_value_sum = small[2 * model + width + HD :]
    return (
        mixed,
        grad_tokens,
        gain_one_sum,
        query_part,
        bias_query_sum,
        kv_part[:, :HD],
        bias_key_sum,
        kv_part[:, HD:],
        bias_value_sum,
        out_part.T,
        gain_two_sum,
        unpack(grads_both[:, :, :part]),
        unpack(grads_both[:, :, part:]),
        unpack(grads_down).T,
    )


def solution(mesh):
    blocks, cores = mesh.devices.shape
    mesh = Mesh(
        mesh.devices.reshape(blocks // 8, 2, 2, 2, cores), ("h", "a", "y", "x", "mp")
    )
    blk = ("h", "a", "y", "x")
    placed = (
        P(blk, None),
        P(blk, None),
        P(),
        P(blk, "mp"),
        P("mp"),
        P(blk, "mp"),
        P("mp"),
        P(blk, "mp"),
        P("mp"),
        P("mp", blk),
        P(),
        P(blk, "mp"),
        P(blk, "mp"),
        P("mp", blk),
        P(),
        P(),
    )
    return jax.shard_map(
        shards,
        mesh=mesh,
        in_specs=placed,
        out_specs=(
            P(blk, None),
            P(blk, None),
            P(),
            P(blk, "mp"),
            P("mp"),
            P(blk, "mp"),
            P("mp"),
            P(blk, "mp"),
            P("mp"),
            P("mp", blk),
            P(),
            P(blk, "mp"),
            P(blk, "mp"),
            P("mp", blk),
        ),
        check_vma=False,
    )
```

time: 2830 us -> 826 us (0.29)
  the two profiles are of different devices: /device:TPU:0 before, /device:TPU:1 now
where the time goes in v1:
time: 826 us; the launch traced here: 814 us
  waiting for transfers between devices  382 us (46%)
  starting transfers between devices  193 us (23%)
  other arithmetic  100 us (12%)
  local copies, waits for them, and re-layouts  69.8 us (8%)
  matrix products  57.7 us (7%)
    ppermute x100, waiting for transfers between devices, flip(): lax.ppermute(value, axis, [(i, i ^ mask) for i in range(lax.axis_size(axi...  376 us
    ppermute x100, starting transfers between devices, flip(): lax.ppermute(value, axis, [(i, i ^ mask) for i in range(lax.axis_size(axi...  131 us
    dot_general x15, matrix products, dot(): return lax.dot_general(left, right, dims, preferred_element_type=F32)  57.7 us
    ppermute x10, starting transfers between devices, swap_mp(): return lax.ppermute(value, 'mp', [(0, 1), (1, 0)])  30.4 us
    unnamed x183, local copies, waits for them, and re-layouts  21.5 us
    select_n x28, other arithmetic, gather_bits(): jnp.where(mine(bit) == 0, jnp.stack([value, other], at), jnp.stack([other...  17.2 us
  transfers between devices with their start and end apart: 118, of which 45 were waited for; matrix products, arithmetic and copies ran while one was open for 20% of the time, Pallas kernels for 1%

profile of v1, /device:TPU:1, one launch (start us, length us, event | category | flops | bytes accessed | tf_op | source)
XLA Modules:
  0.0 813.8 jit_solution(13320751096991394731)
XLA Ops:
  51.4 25.1 %collective-permute-done.21 = bf16[2,96,384]{2,1,0:T(8,128)(2,1)S(1)} collective-permute-done((bf16[2,96,384]{2,1,0:T(8,128)(2,1)S(1)}, bf16[2,96,384]{2,1,0:T(8,128)(2,1)S(1)}, u32[]{:S(2)}, u32[]{:S(2)}) %collective-permute-start.21) | collective-permute-done | bytes 147488 | tf_op jit(solution)/shard_map/ppermute | solution.py:27
  94.9 7.5 collective-permute-done.6
  121.8 24.2 %collective-permute-done.53 = bf16[40,1536]{1,0:T(8,128)(2,1)S(1)} collective-permute-done((bf16[40,1536]{1,0:T(8,128)(2,1)S(1)}, bf16[40,1536]{1,0:T(8,128)(2,1)S(1)}, u32[]{:S(2)}, u32[]{:S(2)}) %collective-permute-start.53) | collective-permute-done | bytes 122912 | tf_op jit(solution)/shard_map/ppermute | solution.py:27
  194.1 17.5 %collective-permute-done.15 = bf16[8,256,128]{2,1,0:T(8,128)(2,1)S(1)} collective-permute-done((bf16[8,256,128]{2,1,0:T(8,128)(2,1)S(1)}, bf16[8,256,128]{2,1,0:T(8,128)(2,1)S(1)}, u32[]{:S(2)}, u32[]{:S(2)}) %collective-permute-start.15) | collective-permute-done | bytes 524320 | tf_op jit(solution)/shard_map/ppermute | solution.py:27
  226.4 11.8 %collective-permute-start.58 = (bf16[160,1536]{1,0:T(8,128)(2,1)}, bf16[160,1536]{1,0:T(8,128)(2,1)}, u32[]{:S(2)}, u32[]{:S(2)}) collective-permute-start(bf16[160,1536]{1,0:T(8,128)(2,1)} %pad_maximum_fusion.22), channel_id=1, source_target_pairs={{0,4},{4,0},{1,5},{5,1},{2,6},{6,2},{3,7},{7,3},{8,12},{12,8},{9,1... | collective-permute-start | bytes 1474568 | tf_op jit(solution)/shard_map/ppermute | solution.py:27
  259.9 7.9 collective-permute-start.27
  271.3 36.3 %collective-permute-done.27 = bf16[192,1536]{1,0:T(8,128)(2,1)S(1)} collective-permute-done((bf16[192,1536]{1,0:T(8,128)(2,1)S(1)}, bf16[192,1536]{1,0:T(8,128)(2,1)S(1)}, u32[]{:S(2)}, u32[]{:S(2)}) %collective-permute-start.27) | collective-permute-done | bytes 589856 | tf_op jit(solution)/shard_map/ppermute | solution.py:27
  314.2 21.6 %collective-permute-done.35 = bf16[1,384,2304]{2,1,0:T(8,128)(2,1)S(1)} collective-permute-done((bf16[1,384,2304]{2,1,0:T(8,128)(2,1)}, bf16[1,384,2304]{2,1,0:T(8,128)(2,1)S(1)}, u32[]{:S(2)}, u32[]{:S(2)}) %collective-permute-start.35) | collective-permute-done | bytes 1769504 | tf_op jit(solution)/shard_map/ppermute | solution.py:27
  348.4 9.0 %collective-permute-done.30 = bf16[160,1536]{1,0:T(8,128)(2,1)S(1)} collective-permute-done((bf16[160,1536]{1,0:T(8,128)(2,1)S(1)}, bf16[160,1536]{1,0:T(8,128)(2,1)S(1)}, u32[]{:S(2)}, u32[]{:S(2)}) %collective-permute-start.30) | collective-permute-done | bytes 491552 | tf_op jit(solution)/shard_map/ppermute | solution.py:27
  364.1 9.8 %fusion.100 = f32[1024,2304]{1,0:T(8,128)} fusion(bf16[1024,1536]{1,0:T(8,128)(2,1)S(1)} %constant_dynamic-update-slice_fusion.10, bf16[1536,2304]{1,0:T(8,128)(2,1)S(1)} %bitcast.358), kind=kOutput, calls=%fused_computation.385 | convolution fusion | flops 7247757312 | bytes 19660800 | tf_op jit(solution)/shard_map/dot_general | solution.py:162
  373.9 9.5 %multiply_convert_fusion.1 = (bf16[1024,1152]{1,0:T(8,128)(2,1)S(1)}, bf16[1024,1152]{1,0:T(8,128)(2,1)}, bf16[1024,1152]{1,0:T(8,128)(2,1)S(1)}) fusion(f32[1024,2304]{1,0:T(8,128)} %fusion.100, bf16[1024,1536]{1,0:T(8,128)(2,1)S(1)} %constant_dynamic-update-slice_fusion.22, bf16[1536,1152]{1,0:T(8,128)(2,1)S(1)} %bitcast.368), kind=kOutput, calls=%fused_computation.7 | convolution fusion | flops 3641573376 | bytes 23199744 | tf_op jit(solution)/shard_map/dot_general | solution.py:162
  396.5 8.3 %convolution_convert_fusion = bf16[1536,2304]{1,0:T(8,128)(2,1)S(1)} fusion(bf16[1024,1536]{1,0:T(8,128)(2,1)S(1)} %constant_dynamic-update-slice_fusion.10, bf16[1024,1152]{1,0:T(8,128)(2,1)S(1)} %copy-done.74, bf16[1024,1152]{1,0:T(8,128)(2,1)S(1)} %get-tuple-element.46), kind=kOutput, calls=%fused_computation | convolution fusion | flops 7260733440 | bytes 14942208 | tf_op jit(solution)/shard_map/dot_general | solution.py:162
  404.8 11.3 %convolution_convert_fusion.2 = bf16[1024,1536]{1,0:T(8,128)(2,1)} fusion(bf16[1536,2304]{1,0:T(8,128)(2,1)S(1)} %bitcast.359, bf16[1024,1152]{1,0:T(8,128)(2,1)} %get-tuple-element.47, bf16[1024,1152]{1,0:T(8,128)(2,1)S(1)} %get-tuple-element.46), kind=kOutput, calls=%fused_computation.11 | convolution fusion | flops 7258767360 | bytes 14942208 | tf_op jit(solution)/shard_map/dot_general | solution.py:162
  420.9 11.0 %collective-permute-done.43 = bf16[160,1536]{1,0:T(8,128)(2,1)S(1)} collective-permute-done((bf16[160,1536]{1,0:T(8,128)(2,1)S(1)}, bf16[160,1536]{1,0:T(8,128)(2,1)S(1)}, u32[]{:S(2)}, u32[]{:S(2)}) %collective-permute-start.43) | collective-permute-done | bytes 491552 | tf_op jit(solution)/shard_map/ppermute | solution.py:27
  432.4 11.5 %collective-permute-done.62 = bf16[160,1536]{1,0:T(8,128)(2,1)S(1)} collective-permute-done((bf16[160,1536]{1,0:T(8,128)(2,1)S(1)}, bf16[160,1536]{1,0:T(8,128)(2,1)S(1)}, u32[]{:S(2)}, u32[]{:S(2)}) %collective-permute-start.62) | collective-permute-done | bytes 491552 | tf_op jit(solution)/shard_map/ppermute | solution.py:27
  456.3 8.2 %collective-permute-done.45 = bf16[40,1536]{1,0:T(8,128)(2,1)S(1)} collective-permute-done((bf16[40,1536]{1,0:T(8,128)(2,1)S(1)}, bf16[40,1536]{1,0:T(8,128)(2,1)S(1)}, u32[]{:S(2)}, u32[]{:S(2)}) %collective-permute-start.45) | collective-permute-done | bytes 122912 | tf_op jit(solution)/shard_map/ppermute | solution.py:27
  494.2 8.1 collective-permute-start.70
  530.1 13.1 %collective-permute-done.72 = bf16[2,256,128]{2,1,0:T(8,128)(2,1)S(1)} collective-permute-done((bf16[2,256,128]{2,1,0:T(8,128)(2,1)S(1)}, bf16[2,256,128]{2,1,0:T(8,128)(2,1)S(1)}, u32[]{:S(2)}, u32[]{:S(2)}) %collective-permute-start.72) | collective-permute-done | bytes 131104 | tf_op jit(solution)/shard_map/ppermute | solution.py:27
  543.3 7.2 collective-permute-start.73
  553.5 12.9 %collective-permute-done.73 = bf16[1,256,128]{2,1,0:T(8,128)(2,1)S(1)} collective-permute-done((bf16[1,256,128]{2,1,0:T(8,128)(2,1)S(1)}, bf16[1,256,128]{2,1,0:T(8,128)(2,1)S(1)}, u32[]{:S(2)}, u32[]{:S(2)}) %collective-permute-start.73) | collective-permute-done | bytes 65568 | tf_op jit(solution)/shard_map/ppermute | solution.py:27
  582.8 10.9 %collective-permute-done.92 = bf16[2,2,2,96,128]{4,3,0,1,2:T(8,128)(2,1)S(1)} collective-permute-done((bf16[2,2,2,96,128]{4,3,0,1,2:T(8,128)(2,1)S(1)}, bf16[2,2,2,96,128]{4,3,0,1,2:T(8,128)(2,1)S(1)}, u32[]{:S(2)}, u32[]{:S(2)}) %collective-permute-start.92) | collective-permute-done | bytes 196640 | tf_op jit(solution)/shard_map/ppermute | solution.py:27
  635.8 13.7 %collective-permute-start.78 = (bf16[256,1536]{1,0:T(8,128)(2,1)S(1)}, bf16[256,1536]{1,0:T(8,128)(2,1)S(1)}, u32[]{:S(2)}, u32[]{:S(2)}) collective-permute-start(bf16[256,1536]{1,0:T(8,128)(2,1)S(1)} %fusion.3), channel_id=1, source_target_pairs={{0,1},{1,0},{2,3},{3,2},{4,5},{5,4},{6,7},{7,6},{8,9},{9,8},{10,11... | collective-permute-start | bytes 2359304 | tf_op jit(solution)/shard_map/ppermute | solution.py:36
  684.0 70.5 %collective-permute-done.109 = bf16[1,384,2304]{2,1,0:T(8,128)(2,1)S(1)} collective-permute-done((bf16[1,384,2304]{2,1,0:T(8,128)(2,1)S(1)}, bf16[1,384,2304]{2,1,0:T(8,128)(2,1)S(1)}, u32[]{:S(2)}, u32[]{:S(2)}) %collective-permute-start.109) | collective-permute-done | bytes 1769504 | tf_op jit(solution)/shard_map/ppermute | solution.py:27
  786.9 18.0 %collective-permute-done.91 = bf16[96,384]{1,0:T(8,128)(2,1)S(1)} collective-permute-done((bf16[96,384]{1,0:T(8,128)(2,1)S(1)}, bf16[96,384]{1,0:T(8,128)(2,1)S(1)}, u32[]{:S(2)}, u32[]{:S(2)}) %collective-permute-start.91) | collective-permute-done | bytes 73760 | tf_op jit(solution)/shard_map/ppermute | solution.py:27
  (680 shorter events, 424.4 us)
Async XLA Ops:
  2.4 48.2 %collective-permute-start.50 = (bf16[48,1536]{1,0:T(8,128)(2,1)S(1)}, bf16[48,1536]{1,0:T(8,128)(2,1)S(1)}, u32[]{:S(2)}, u32[]{:S(2)}) collective-permute-start(bf16[48,1536]{1,0:T(8,128)(2,1)S(1)} %get-tuple-element.39), channel_id=1, source_target_pairs={{0,2},{2,0},{1,3},{3,1},{4,6},{6,4},{5,7},{7,5},{8,10},{10,8},{9,1... | collective-permute-start | bytes 442376 | tf_op jit(solution)/shard_map/ppermute | solution.py:27
  33.7 142.0 %collective-permute-start.34 = (bf16[4,96,2304]{2,0,1:T(4,128)(2,1)}, bf16[4,96,2304]{2,0,1:T(4,128)(2,1)}, u32[]{:S(2)}, u32[]{:S(2)}) collective-permute-start(bf16[4,96,2304]{2,0,1:T(4,128)(2,1)} %pad_maximum_fusion.4), channel_id=1, source_target_pairs={{1,8},{8,1},{3,10},{10,3},{5,12},{12,5},{7,14},{14,7},{17,24},{24,... | collective-permute-start | bytes 5308424 | tf_op jit(solution)/shard_map/ppermute | solution.py:385
  40.9 66.4 %collective-permute-start.37 = (bf16[4,96,1152]{2,0,1:T(4,128)(2,1)}, bf16[4,96,1152]{2,0,1:T(4,128)(2,1)S(1)}, u32[]{:S(2)}, u32[]{:S(2)}) collective-permute-start(bf16[4,96,1152]{2,0,1:T(4,128)(2,1)} %bitcast.373), channel_id=1, source_target_pairs={{1,8},{8,1},{3,10},{10,3},{5,12},{12,5},{7,14},{14,7},{17,24},{24,... | collective-permute-start | bytes 2654216 | tf_op jit(solution)/shard_map/ppermute | solution.py:385
  103.8 42.3 %collective-permute-start.23 = (bf16[2,2,2,96,384]{4,3,0,1,2:T(8,128)(2,1)}, bf16[2,2,2,96,384]{4,3,0,1,2:T(8,128)(2,1)}, u32[]{:S(2)}, u32[]{:S(2)}) collective-permute-start(bf16[2,2,2,96,384]{4,3,0,1,2:T(8,128)(2,1)} %maximum_select_fusion.18), channel_id=1, source_target_pairs={{0,2},{2,0},{1,3},{3,1},{4,6},{6,4},{5,7},{7,5},{8,10},{10,8},{9,1... | collective-permute-start | bytes 1769480 | tf_op jit(solution)/shard_map/ppermute | solution.py:27
  107.3 46.6 %collective-permute-start.7 = (bf16[2,2,2,96,512]{4,3,0,1,2:T(8,128)(2,1)}, bf16[2,2,2,96,512]{4,3,0,1,2:T(8,128)(2,1)}, u32[]{:S(2)}, u32[]{:S(2)}) collective-permute-start(bf16[2,2,2,96,512]{4,3,0,1,2:T(8,128)(2,1)} %maximum_select_fusion.13), channel_id=1, source_target_pairs={{0,2},{2,0},{1,3},{3,1},{4,6},{6,4},{5,7},{7,5},{8,10},{10,8},{9,1... | collective-permute-start | bytes 2359304 | tf_op jit(solution)/shard_map/ppermute | solution.py:27
  110.0 57.9 %all-to-all-start.1 = ((bf16[4,96,1152]{2,1,0:T(8,128)(2,1)}), bf16[4,96,1152]{2,1,0:T(8,128)(2,1)}, u32[]{:S(2)}, u32[]{:S(2)}) async-start(bf16[4,96,1152]{2,1,0:T(8,128)(2,1)} %copy.290), calls=%async_computation.1 | async-start | bytes 1769472 | tf_op jit(solution)/shard_map/all_to_all | solution.py:387
  114.4 46.3 %collective-permute-start.3 = (bf16[2,2,2,96,512]{4,3,2,1,0:T(8,128)(2,1)}, bf16[2,2,2,96,512]{4,3,2,1,0:T(8,128)(2,1)S(1)}, u32[]{:S(2)}, u32[]{:S(2)}) collective-permute-start(bf16[2,2,2,96,512]{4,3,2,1,0:T(8,128)(2,1)} %maximum_select_fusion.11), channel_id=1, source_target_pairs={{0,4},{4,0},{1,5},{5,1},{2,6},{6,2},{3,7},{7,3},{8,12},{12,8},{9,1... | collective-permute-start | bytes 2359304 | tf_op jit(solution)/shard_map/ppermute | solution.py:27
  167.9 84.1 %collective-permute-start.38 = (bf16[1,384,1152]{2,1,0:T(8,128)(2,1)}, bf16[1,384,1152]{2,1,0:T(8,128)(2,1)}, u32[]{:S(2)}, u32[]{:S(2)}) collective-permute-start(bf16[1,384,1152]{2,1,0:T(8,128)(2,1)} %bitcast.76), channel_id=1, source_target_pairs={{0,16},{16,0},{1,17},{17,1},{2,18},{18,2},{3,19},{19,3},{4,20},{20... | collective-permute-start | bytes 2654216 | tf_op jit(solution)/shard_map/ppermute | solution.py:27
  180.3 76.2 %all-to-all-start = ((bf16[4,96,2304]{2,1,0:T(8,128)(2,1)}), bf16[4,96,2304]{2,1,0:T(8,128)(2,1)}, u32[]{:S(2)}, u32[]{:S(2)}) async-start(bf16[4,96,2304]{2,1,0:T(8,128)(2,1)} %copy.289), calls=%async_computation | async-start | bytes 3538944 | tf_op jit(solution)/shard_map/all_to_all | solution.py:387
  226.4 81.9 %collective-permute-start.58 = (bf16[160,1536]{1,0:T(8,128)(2,1)}, bf16[160,1536]{1,0:T(8,128)(2,1)}, u32[]{:S(2)}, u32[]{:S(2)}) collective-permute-start(bf16[160,1536]{1,0:T(8,128)(2,1)} %pad_maximum_fusion.22), channel_id=1, source_target_pairs={{0,4},{4,0},{1,5},{5,1},{2,6},{6,2},{3,7},{7,3},{8,12},{12,8},{9,1... | collective-permute-start | bytes 1474568 | tf_op jit(solution)/shard_map/ppermute | solution.py:27
  255.6 90.0 %collective-permute-start.39 = (bf16[2,384,1152]{2,1,0:T(8,128)(2,1)}, bf16[2,384,1152]{2,1,0:T(8,128)(2,1)}, u32[]{:S(2)}, u32[]{:S(2)}) collective-permute-start(bf16[2,384,1152]{2,1,0:T(8,128)(2,1)} %maximum_select_fusion.5), channel_id=1, source_target_pairs={{0,1},{1,0},{2,3},{3,2},{4,5},{5,4},{6,7},{7,6},{8,9},{9,8},{10,11... | collective-permute-start | bytes 5308424 | tf_op jit(solution)/shard_map/ppermute | solution.py:36
  256.5 79.3 %collective-permute-start.35 = (bf16[1,384,2304]{2,1,0:T(8,128)(2,1)}, bf16[1,384,2304]{2,1,0:T(8,128)(2,1)S(1)}, u32[]{:S(2)}, u32[]{:S(2)}) collective-permute-start(bf16[1,384,2304]{2,1,0:T(8,128)(2,1)} %bitcast.69), channel_id=1, source_target_pairs={{0,16},{16,0},{1,17},{17,1},{2,18},{18,2},{3,19},{19,3},{4,20},{20... | collective-permute-start | bytes 5308424 | tf_op jit(solution)/shard_map/ppermute | solution.py:27
  259.9 47.7 %collective-permute-start.27 = (bf16[192,1536]{1,0:T(8,128)(2,1)S(1)}, bf16[192,1536]{1,0:T(8,128)(2,1)S(1)}, u32[]{:S(2)}, u32[]{:S(2)}) collective-permute-start(bf16[192,1536]{1,0:T(8,128)(2,1)S(1)} %pad_maximum_fusion.15), channel_id=1, source_target_pairs={{0,8},{8,0},{1,9},{9,1},{2,10},{10,2},{3,11},{11,3},{4,12},{12,4},... | collective-permute-start | bytes 1769480 | tf_op jit(solution)/shard_map/ppermute | solution.py:27
  417.5 94.3 %collective-permute-start.111 = (bf16[2,384,1152]{2,1,0:T(8,128)(2,1)}, bf16[2,384,1152]{2,1,0:T(8,128)(2,1)}, u32[]{:S(2)}, u32[]{:S(2)}) collective-permute-start(bf16[2,384,1152]{2,1,0:T(8,128)(2,1)} %dynamic-slice_bitcast_fusion.1), channel_id=1, source_target_pairs={{0,1},{1,0},{2,3},{3,2},{4,5},{5,4},{6,7},{7,6},{8,9},{9,8},{10,11... | collective-permute-start | bytes 5308424 | tf_op jit(solution)/shard_map/ppermute | solution.py:36
  486.1 186.9 %collective-permute-start.108 = (bf16[2,384,2304]{2,1,0:T(8,128)(2,1)}, bf16[2,384,2304]{2,1,0:T(8,128)(2,1)}, u32[]{:S(2)}, u32[]{:S(2)}) collective-permute-start(bf16[2,384,2304]{2,1,0:T(8,128)(2,1)} %dynamic-slice_bitcast_fusion), channel_id=1, source_target_pairs={{0,1},{1,0},{2,3},{3,2},{4,5},{5,4},{6,7},{7,6},{8,9},{9,8},{10,11... | collective-permute-start | bytes 10616840 | tf_op jit(solution)/shard_map/ppermute | solution.py:36
  486.7 180.3 %collective-permute-start.68 = (f32[128,1536]{1,0:T(8,128)}, f32[128,1536]{1,0:T(8,128)}, u32[]{:S(2)}, u32[]{:S(2)}) collective-permute-start(f32[128,1536]{1,0:T(8,128)} %get-tuple-element.33), channel_id=1, source_target_pairs={{0,1},{1,0},{2,3},{3,2},{4,5},{5,4},{6,7},{7,6},{8,9},{9,8},{10,11... | collective-permute-start | bytes 2359304 | tf_op jit(solution)/shard_map/ppermute | solution.py:36
  522.1 77.1 %collective-permute-start.112 = (bf16[1,384,1152]{2,1,0:T(8,128)(2,1)}, bf16[1,384,1152]{2,1,0:T(8,128)(2,1)}, u32[]{:S(2)}, u32[]{:S(2)}) collective-permute-start(bf16[1,384,1152]{2,1,0:T(8,128)(2,1)} %constant_dynamic-slice_fusion), channel_id=1, source_target_pairs={{0,16},{16,0},{1,17},{17,1},{2,18},{18,2},{3,19},{19,3},{4,20},{20... | collective-permute-start | bytes 2654216 | tf_op jit(solution)/shard_map/ppermute | solution.py:27
  576.5 57.9 %collective-permute-start.100 = (bf16[2,2,2,96,384]{4,3,0,1,2:T(8,128)(2,1)}, bf16[2,2,2,96,384]{4,3,0,1,2:T(8,128)(2,1)}, u32[]{:S(2)}, u32[]{:S(2)}) collective-permute-start(bf16[2,2,2,96,384]{4,3,0,1,2:T(8,128)(2,1)} %bitcast.339), channel_id=1, source_target_pairs={{0,4},{4,0},{1,5},{5,1},{2,6},{6,2},{3,7},{7,3},{8,12},{12,8},{9,1... | collective-permute-start | bytes 1769480 | tf_op jit(solution)/shard_map/ppermute | solution.py:27
  602.8 153.4 %all-to-all-start.3 = ((bf16[4,96,1152]{2,1,0:T(8,128)(2,1)}), bf16[4,96,1152]{2,1,0:T(8,128)(2,1)S(1)}, u32[]{:S(2)}, u32[]{:S(2)}) async-start(bf16[4,96,1152]{2,1,0:T(8,128)(2,1)} %bitcast.160), calls=%async_computation.3 | async-start | bytes 1769472 | tf_op jit(solution)/shard_map/all_to_all | solution.py:414
  676.1 78.4 %collective-permute-start.109 = (bf16[1,384,2304]{2,1,0:T(8,128)(2,1)S(1)}, bf16[1,384,2304]{2,1,0:T(8,128)(2,1)S(1)}, u32[]{:S(2)}, u32[]{:S(2)}) collective-permute-start(bf16[1,384,2304]{2,1,0:T(8,128)(2,1)S(1)} %constant_dynamic-slice_fusion.1), channel_id=1, source_target_pairs={{0,16},{16,0},{1,17},{17,1},{2,18},{18,2},{3,19},{19,3},{4,20},{20... | collective-permute-start | bytes 5308424 | tf_op jit(solution)/shard_map/ppermute | solution.py:27
  679.1 88.3 %collective-permute-start.102 = (bf16[2,96,384]{2,1,0:T(8,128)(2,1)}, bf16[2,96,384]{2,1,0:T(8,128)(2,1)}, u32[]{:S(2)}, u32[]{:S(2)}) collective-permute-start(bf16[2,96,384]{2,1,0:T(8,128)(2,1)} %dynamic-slice_bitcast_fusion.9), channel_id=1, source_target_pairs={{0,8},{8,0},{1,9},{9,1},{2,10},{10,2},{3,11},{11,3},{4,12},{12,4},... | collective-permute-start | bytes 442376 | tf_op jit(solution)/shard_map/ppermute | solution.py:27
  680.9 88.2 %collective-permute-start.106 = (bf16[2,96,384]{2,1,0:T(8,128)(2,1)}, bf16[2,96,384]{2,1,0:T(8,128)(2,1)}, u32[]{:S(2)}, u32[]{:S(2)}) collective-permute-start(bf16[2,96,384]{2,1,0:T(8,128)(2,1)} %dynamic-slice_bitcast_fusion.8), channel_id=1, source_target_pairs={{0,8},{8,0},{1,9},{9,1},{2,10},{10,2},{3,11},{11,3},{4,12},{12,4},... | collective-permute-start | bytes 442376 | tf_op jit(solution)/shard_map/ppermute | solution.py:27
  682.1 90.9 %collective-permute-start.86 = (bf16[2,96,384]{2,1,0:T(8,128)(2,1)}, bf16[2,96,384]{2,1,0:T(8,128)(2,1)}, u32[]{:S(2)}, u32[]{:S(2)}) collective-permute-start(bf16[2,96,384]{2,1,0:T(8,128)(2,1)} %dynamic-slice_bitcast_fusion.11), channel_id=1, source_target_pairs={{0,8},{8,0},{1,9},{9,1},{2,10},{10,2},{3,11},{11,3},{4,12},{12,4},... | collective-permute-start | bytes 442376 | tf_op jit(solution)/shard_map/ppermute | solution.py:27
  762.2 43.4 %collective-permute-start.113 = (bf16[4,96,1152]{2,0,1:T(4,128)(2,1)}, bf16[4,96,1152]{2,0,1:T(4,128)(2,1)}, u32[]{:S(2)}, u32[]{:S(2)}) collective-permute-start(bf16[4,96,1152]{2,0,1:T(4,128)(2,1)} %copy.314), channel_id=1, source_target_pairs={{1,8},{8,1},{3,10},{10,3},{5,12},{12,5},{7,14},{14,7},{17,24},{24,... | collective-permute-start | bytes 2654216 | tf_op jit(solution)/shard_map/ppermute | solution.py:415
  (171 other events, 2657.7 us)

commit v2 on v1

v2 whole, which is shorter than its diff:
```python
import functools

import jax
import jax.numpy as jnp
from jax import lax
from jax.experimental import pallas as pl
from jax.experimental.pallas import tpu as pltpu
from jax.sharding import Mesh
from jax.sharding import PartitionSpec as P

HD = 128
SEG = 1024
LOG2E = 1.4426950408889634
BIG = -1e30
BF = jnp.bfloat16
F32 = jnp.float32

epsilon = 1e-06


BLK = ("h", "a", "y", "x")
CUBE_AXES = ("a", "y", "x")


def bit_axis(bit):
    return ("x", "y", "a")[bit] if bit < 3 else "h", 1 if bit < 3 else 1 << (bit - 3)


def flip(value, bit):
    axis, mask = bit_axis(bit)
    return lax.ppermute(value, axis, [(i, i ^ mask) for i in range(lax.axis_size(axis))])


def mine(bit):
    axis, mask = bit_axis(bit)
    return (lax.axis_index(axis) // mask) % 2


def swap_mp(value):
    return lax.ppermute(value, "mp", [(0, 1), (1, 0)])


def halves(value, which):
    return lax.dynamic_index_in_dim(value, which, 0, keepdims=False)


def trade(value, axes, dim=0):
    return lax.all_to_all(value, axes, dim, dim, tiled=True)


def after(value, *others):
    return lax.optimization_barrier((value,) + others)[0]


def together(values):
    return list(lax.optimization_barrier(tuple(values)))


class Gather:
    def __init__(self, value):
        self.value, self.have = value, []

    def step(self, bit):
        at = sum(1 for b in self.have if b > bit)
        other = flip(self.value, bit)
        self.last = other
        self.value = jnp.where(
            mine(bit) == 0,
            jnp.stack([self.value, other], at),
            jnp.stack([other, self.value], at),
        )
        self.have.append(bit)
        return self

    def split(self, count):
        parts = []
        for value in jnp.split(self.value, count, axis=-1):
            part = Gather(value)
            part.have = list(self.have)
            parts.append(part)
        return parts

    def rows(self):
        return self.value.reshape((-1, self.value.shape[-1]))


class Scatter:
    def __init__(self, value, bits):
        self.have = list(range(bits))[::-1]
        self.value = value.reshape((2,) * bits + (-1, value.shape[-1]))

    def step(self, bit, *others):
        at = self.have.index(bit)
        me = mine(bit)
        keep = lax.dynamic_index_in_dim(self.value, me, at, keepdims=False)
        send = lax.dynamic_index_in_dim(self.value, 1 - me, at, keepdims=False)
        self.last = flip(send, bit)
        if others:
            self.last = after(self.last, *others)
        self.value = keep.astype(F32) + self.last.astype(F32)
        self.have.remove(bit)
        if self.have:
            self.value = self.value.astype(BF)
        return self


def joined(parts):
    one = Gather(jnp.concatenate([p.value for p in parts], axis=-1))
    one.have = list(parts[0].have)
    return one


CUBE = ((0, 1, 2), (1, 2, 0), (2, 0, 1))


def cube_parts(rows):
    units = rows // 8
    sizes = [(units + 2 - i) // 3 * 8 for i in range(3)]
    return sizes


def cube_gather(value):
    parts, at = [], 0
    for size in cube_parts(value.shape[0]):
        parts.append(value[at : at + size])
        at += size
    for step in range(3):
        came = together([flip(part, order[step]) for part, order in zip(parts, CUBE)])
        parts = [jnp.concatenate(both, 0) for both in zip(parts, came)]
    return jnp.concatenate(parts, 0), came


class Cube:
    def __init__(self, value):
        self.value, self.size, self.have = value, value.shape[0], [0]

    def step(self, bit):
        self.last = flip(self.value, bit)
        self.value = jnp.concatenate([self.value, self.last], 0)
        self.have = self.have + [h ^ (1 << bit) for h in self.have]
        return self

    def done(self):
        slots = self.value.reshape((8, self.size) + self.value.shape[1:])
        pieces, at = [], 0
        for rows, order in zip(cube_parts(self.size), CUBE):
            wanted = [0]
            for bit in order:
                wanted = wanted + [w ^ (1 << bit) for w in wanted]
            pieces += [slots[self.have.index(w), at : at + rows] for w in wanted]
            at += rows
        return jnp.concatenate(pieces, 0)


class CubeBack:
    def __init__(self, value, rows):
        have = [0]
        for bit in (2, 0, 1):
            have = have + [h ^ (1 << bit) for h in have]
        pieces, at = {}, 0
        for size, order in zip(cube_parts(rows), CUBE):
            wanted = [0]
            for bit in order:
                wanted = wanted + [w ^ (1 << bit) for w in wanted]
            for w in wanted:
                pieces.setdefault(w, []).append(value[at : at + size])
                at += size
        self.value = jnp.concatenate([p for w in have for p in pieces[w]], 0)

    def step(self, bit, *others):
        half = self.value.shape[0] // 2
        other = flip(self.value[half:], bit)
        if others:
            other = after(other, *others)
        self.value = self.value[:half].astype(F32) + other.astype(F32)
        if bit != 2:
            self.value = self.value.astype(BF)
        return self


def cube_scatter(value, rows):
    parts, at, came = [], 0, []
    for size in cube_parts(rows):
        parts.append(value[at : at + 8 * size])
        at += 8 * size
    for step in range(3):
        half = [part.shape[0] // 2 for part in parts]
        sent = [flip(p[n:], order[2 - step]) for p, n, order in zip(parts, half, CUBE)]
        came.append(together(sent))
        parts = [p[:n].astype(F32) + v.astype(F32) for p, n, v in zip(parts, half, came[-1])]
        if step < 2:
            parts = [p.astype(BF) for p in parts]
    return jnp.concatenate(parts, 0), came


def rotate(value, cosine, sine):
    half = value.shape[-1] // 2
    return value * cosine + jnp.concatenate([value[:, half:], value[:, :half]], axis=1) * sine


def rope_tables(position):
    freq = jnp.power(10000.0, -(jnp.arange(HD // 2, dtype=F32) * (2.0 / HD)))
    angle = position.astype(F32)[:, None] * freq[None, :]
    cosine, sine = jnp.cos(angle), jnp.sin(angle)
    return (jnp.concatenate([cosine, cosine], 1), jnp.concatenate([-sine, sine], 1))


def look(table, index):
    places = jnp.arange(table.shape[0], dtype=jnp.int32)
    return jnp.sum(jnp.where(index[:, None] == places[None, :], table[None, :], 0), axis=1)


def norm_back(grad, value, inverse, gain):
    scaled = grad * gain
    grad_gain = jnp.sum(grad * value * inverse, axis=0)
    mean_term = jnp.mean(scaled * value, axis=-1, keepdims=True)
    grad_value = inverse * scaled - value * (inverse * inverse * inverse) * mean_term
    return (grad_value, grad_gain)


NT = (((1,), (1,)), ((), ()))
TN = (((0,), (0,)), ((), ()))


def dot(left, right, dims=(((1,), (0,)), ((), ()))):
    return lax.dot_general(left, right, dims, preferred_element_type=F32)


def own_mask(rows):
    return lax.broadcasted_iota(jnp.int32, (rows, rows), 0) >= lax.broadcasted_iota(
        jnp.int32, (rows, rows), 1
    )


def attend_kernel(vis, q_ref, kv_ref, o_ref, low_ref, lse_ref, acc, top, tot):
    rows, width = q_ref.shape
    heads = width // HD
    blocks = kv_ref.shape[0]
    factor = HD ** (-0.5) * LOG2E

    def block(place, first):
        key = kv_ref[place, :, :HD]
        value = kv_ref[place, :, HD:]
        if first:
            mask = own_mask(rows)
        for h in range(heads):
            cols = slice(h * HD, (h + 1) * HD)
            scores = dot(q_ref[:, cols], key, NT) * factor
            if first:
                scores = jnp.where(mask, scores, BIG)
                best = jnp.max(scores, axis=1, keepdims=True)
                weights = jnp.exp2(scores - best)
                tot[h] = jnp.sum(weights, axis=1, keepdims=True)
                acc[:, cols] = dot(weights.astype(BF), value)
            else:
                old = top[h]
                best = jnp.maximum(old, jnp.max(scores, axis=1, keepdims=True))
                weights = jnp.exp2(scores - best)
                scale = jnp.exp2(old - best)
                tot[h] = tot[h] * scale + jnp.sum(weights, axis=1, keepdims=True)
                acc[:, cols] = acc[:, cols] * scale + dot(weights.astype(BF), value)
            top[h] = best

    block(vis[blocks], True)

    def step(place, carry):
        @pl.when(vis[place] == 1)
        def _():
            block(place, False)

        return carry

    lax.fori_loop(0, blocks, step, 0)
    for h in range(heads):
        cols = slice(h * HD, (h + 1) * HD)
        total = tot[h]
        out = acc[:, cols] / total
        o_ref[:, cols] = out
        low_ref[:, cols] = out.astype(BF)
        lse_ref[:, cols] = jnp.broadcast_to(top[h] + jnp.log(total) * LOG2E, (rows, HD))


def attend(vis, query, keyval):
    rows, width = query.shape
    heads = width // HD
    smem = pl.BlockSpec(memory_space=pltpu.SMEM)
    vmem = pl.BlockSpec(memory_space=pltpu.VMEM)
    return pl.pallas_call(
        attend_kernel,
        out_shape=(
            jax.ShapeDtypeStruct((rows, width), F32),
            jax.ShapeDtypeStruct((rows, width), BF),
            jax.ShapeDtypeStruct((rows, width), F32),
        ),
        in_specs=[smem, vmem, vmem],
        out_specs=(vmem, vmem, vmem),
        scratch_shapes=[
            pltpu.VMEM((rows, width), F32),
            pltpu.VMEM((heads, rows, 1), F32),
            pltpu.VMEM((heads, rows, 1), F32),
        ],
        compiler_params=pltpu.CompilerParams(vmem_limit_bytes=40 * 2**20),
        cost_estimate=pl.CostEstimate(
            flops=4 * rows * width * 2048, bytes_accessed=8 * 2**20, transcendentals=rows * 6 * 2048
        ),
    )(vis, query, keyval)


def attend_back_kernel(
    vis, q_ref, kv_ref, do_ref, o_ref, lse_ref, cos_ref, sin_ref, out_ref, dkv_ref, dq_ref, delta
):
    rows, width = q_ref.shape
    heads = width // HD
    blocks = kv_ref.shape[0]
    scale = HD ** (-0.5)
    for h in range(heads):
        cols = slice(h * HD, (h + 1) * HD)
        delta[h] = jnp.sum(do_ref[:, cols].astype(F32) * o_ref[:, cols], axis=1, keepdims=True)

    def block(place, first):
        key = kv_ref[place, :, :HD]
        value = kv_ref[place, :, HD:]
        if first:
            mask = own_mask(rows)
        dk = jnp.zeros((rows, HD), F32)
        dv = jnp.zeros((rows, HD), F32)
        for h in range(heads):
            cols = slice(h * HD, (h + 1) * HD)
            query = q_ref[:, cols]
            grad = do_ref[:, cols]
            probs = jnp.exp2(
                dot(query, key, NT) * (scale * LOG2E) - lse_ref[:, h * HD : h * HD + 1]
            )
            if first:
                probs = jnp.where(mask, probs, 0.0)
            dv = dv + dot(probs.astype(BF), grad, TN)
            dprobs = dot(grad, value, NT)
            dscores = (probs * (dprobs - delta[h])).astype(BF)
            dk = dk + dot(dscores, query, TN)
            dq = dot(dscores, key) * scale
            if first:
                dq_ref[:, cols] = dq
            else:
                dq_ref[:, cols] = dq_ref[:, cols] + dq
        dkv_ref[place, :, :HD] = (dk * scale).astype(BF)
        dkv_ref[place, :, HD:] = dv.astype(BF)

    block(vis[blocks], True)

    def step(place, carry):
        @pl.when(vis[place] == 1)
        def _():
            block(place, False)

        @pl.when((vis[place] == 0) & (place != vis[blocks]))
        def _():
            dkv_ref[place] = jnp.zeros((rows, 2 * HD), BF)

        return carry

    lax.fori_loop(0, blocks, step, 0)
    for h in range(heads):
        cols = slice(h * HD, (h + 1) * HD)
        out_ref[:, cols] = turn(dq_ref[:, cols], cos_ref[...], -sin_ref[...]).astype(BF)


def attend_back(vis, query, keyval, grad, out, lse, cosine, sine):
    rows, width = query.shape
    heads = width // HD
    smem = pl.BlockSpec(memory_space=pltpu.SMEM)
    vmem = pl.BlockSpec(memory_space=pltpu.VMEM)
    return pl.pallas_call(
        attend_back_kernel,
        out_shape=(
            jax.ShapeDtypeStruct((rows, width), BF),
            jax.ShapeDtypeStruct(keyval.shape, BF),
        ),
        in_specs=[smem] + [vmem] * 7,
        out_specs=(vmem, vmem),
        scratch_shapes=[
            pltpu.VMEM((rows, width), F32),
            pltpu.VMEM((heads, rows, 1), F32),
        ],
        compiler_params=pltpu.CompilerParams(vmem_limit_bytes=48 * 2**20),
        cost_estimate=pl.CostEstimate(
            flops=10 * rows * width * 2048,
            bytes_accessed=16 * 2**20,
            transcendentals=rows * 6 * 2048,
        ),
    )(vis, query, keyval, grad, out, lse, cosine, sine)


def turn(value, cosine, sine):
    return value * cosine + pltpu.roll(value, HD // 2, 1) * sine


def project_kernel(turned, x_ref, w_ref, b_ref, cos_ref, sin_ref, o_ref):
    lin = dot(x_ref[...], w_ref[...]) + b_ref[...]
    for h in range(lin.shape[1] // HD):
        cols = slice(h * HD, (h + 1) * HD)
        head = lin[:, cols]
        if h < turned:
            head = turn(head, cos_ref[...], sin_ref[...])
        o_ref[:, cols] = head.astype(BF)


def project(normed, weight, bias, cosine, sine, turned):
    rows = normed.shape[0]
    width = weight.shape[1]
    vmem = pl.BlockSpec(memory_space=pltpu.VMEM)
    return pl.pallas_call(
        functools.partial(project_kernel, turned),
        out_shape=jax.ShapeDtypeStruct((rows, width), BF),
        in_specs=[vmem] * 5,
        out_specs=vmem,
        compiler_params=pltpu.CompilerParams(vmem_limit_bytes=24 * 2**20),
        cost_estimate=pl.CostEstimate(
            flops=2 * rows * width * normed.shape[1],
            bytes_accessed=2 * normed.shape[1] * (rows + width),
            transcendentals=0,
        ),
    )(normed, weight, bias.astype(F32)[None], cosine, sine)


def share(tiles, chip):
    at = (chip * tiles) // 8
    return at, ((chip + 1) * tiles) // 8 - at


def pack_kernel(tiles, part, gate_ref, up_ref, down_ref, both_out, down_out):
    at, count = share(tiles, pl.program_id(0))
    cols = pl.ds(pl.multiple_of(at * 128, 128), part)
    keep = lax.broadcasted_iota(jnp.int32, (gate_ref.shape[0], part), 1) < count * 128

    def kept(value):
        return jnp.where(keep, value.astype(F32), 0.0).astype(BF)

    both_out[0, :, :part] = kept(gate_ref[:, cols])
    both_out[0, :, part:] = kept(up_ref[:, cols])
    down_out[0] = kept(down_ref[cols, :].astype(F32).T)


def pack(w_gate, w_up, w_down, part):
    slab, hidden = w_gate.shape
    vmem = pl.BlockSpec(memory_space=pltpu.VMEM)
    return pl.pallas_call(
        functools.partial(pack_kernel, hidden // 128, part),
        grid=(8,),
        out_shape=(
            jax.ShapeDtypeStruct((8, slab, 2 * part), BF),
            jax.ShapeDtypeStruct((8, slab, part), BF),
        ),
        in_specs=[vmem] * 3,
        out_specs=(
            pl.BlockSpec((1, slab, 2 * part), lambda c: (c, 0, 0)),
            pl.BlockSpec((1, slab, part), lambda c: (c, 0, 0)),
        ),
        compiler_params=pltpu.CompilerParams(vmem_limit_bytes=24 * 2**20),
        cost_estimate=pl.CostEstimate(flops=0, bytes_accessed=8 * 2**20, transcendentals=0),
    )(w_gate, w_up, w_down)


def unpack_kernel(tiles, gate_ref, up_ref, down_ref, gate_out, up_out, down_out):
    for c in range(8):
        at, size = share(tiles, c)
        here, width = slice(at * 128, (at + size) * 128), size * 128
        gate_out[:, here] = gate_ref[c, :, :width].astype(F32)
        up_out[:, here] = up_ref[c, :, :width].astype(F32)
        down_out[here, :] = down_ref[c, :, :width].astype(F32).T


def unpack(gate, up, down, hidden):
    slab = down.shape[1]
    vmem = pl.BlockSpec(memory_space=pltpu.VMEM)
    return pl.pallas_call(
        functools.partial(unpack_kernel, hidden // 128),
        out_shape=(
            jax.ShapeDtypeStruct((slab, hidden), F32),
            jax.ShapeDtypeStruct((slab, hidden), F32),
            jax.ShapeDtypeStruct((hidden, slab), F32),
        ),
        in_specs=[vmem] * 3,
        out_specs=(vmem,) * 3,
        compiler_params=pltpu.CompilerParams(vmem_limit_bytes=40 * 2**20),
        cost_estimate=pl.CostEstimate(flops=0, bytes_accessed=10 * 2**20, transcendentals=0),
    )(gate, up, down)


def shards(
    tokens,
    cotangent,
    norm_gain,
    w_query,
    b_query,
    w_key,
    b_key,
    w_value,
    b_value,
    w_out,
    ffn_gain,
    w_gate,
    w_up,
    w_down,
    unit_seq,
    block_map,
):
    rows, model = tokens.shape
    blocks = block_map.shape[0]
    low_rows = rows // 2
    width = w_query.shape[1]
    heads = width // HD
    slab = w_gate.shape[0]
    tiles = w_gate.shape[1] // 128
    part = -(-tiles // 8) * 128
    core = lax.axis_index("mp")
    me = lax.axis_index(BLK)

    def my_half(value):
        return halves(value.reshape((2, low_rows) + value.shape[1:]), core)

    bits = blocks.bit_length() - 1
    high = list(range(3, bits))[::-1]

    both_send, down_send = pack(w_gate, w_up, w_down, part)
    w_kv = Gather(jnp.concatenate([w_key, w_value], axis=1))
    w_q = Gather(w_query)
    w_out_all = Gather(w_out.T)
    cot_half = my_half(cotangent)
    cot_cube = Cube(cot_half)
    for bit in high:
        w_kv.step(bit)
        w_q.step(bit)
        w_out_all.step(bit)
    cot_cube.step(1)
    both_cube = trade(after(both_send, w_kv.last, w_q.last), CUBE_AXES)
    down_cube = trade(after(down_send, both_cube), CUBE_AXES)
    both_own = lax.all_gather(both_cube.reshape(8 * slab, -1), "h", axis=0, tiled=True)
    down_own = lax.all_gather(down_cube.reshape(8 * slab, -1), "h", axis=0, tiled=True)
    block_map = after(block_map, both_send)
    inputs = after(tokens, both_send).astype(F32)
    per_unit = SEG // rows
    units = jnp.arange(unit_seq.shape[0], dtype=jnp.int32)
    previous = jnp.concatenate([jnp.full((1,), -1, jnp.int32), unit_seq[:-1]])
    first_unit = lax.cummax(jnp.where(unit_seq != previous, units, 0), axis=0)
    seqs = look(unit_seq, block_map // per_unit)
    own_place = jnp.arange(blocks, dtype=jnp.int32) == me
    my_block = jnp.sum(jnp.where(own_place, block_map, 0))
    my_seq = jnp.sum(jnp.where(own_place, seqs, 0))
    vis = ((seqs == my_seq) & (block_map < my_block)).astype(jnp.int32)
    vis = jnp.concatenate([vis, me[None].astype(jnp.int32)])
    begin = look(first_unit, (my_block // per_unit)[None])
    position = my_block * rows - begin[0] * SEG + jnp.arange(rows, dtype=jnp.int32)
    cosine, sine = rope_tables(position)

    gain_one = norm_gain.astype(F32)
    inverse_one = lax.rsqrt(jnp.mean(inputs * inputs, axis=-1, keepdims=True) + epsilon)
    normed = (inputs * inverse_one * gain_one).astype(BF)
    w_kv.value = after(w_kv.value, both_cube, cosine, vis, normed, cot_cube.last, w_out_all.last)
    w_q.value = after(w_q.value, both_cube)
    w_kv.step(2)
    w_q.step(2)
    one, two = w_q.split(2)
    w_kv.step(1)
    one.step(0)
    two.step(1)
    cot_cube.value = after(cot_cube.value, w_q.last)
    cot_cube.step(2)
    w_kv = w_kv.step(0).rows()
    w_q = joined([one.step(1), two.step(0)]).rows()

    keyval = Gather(project(normed, w_kv, jnp.concatenate([b_key, b_value]), cosine, sine, 1))

    w_out_all.value = after(w_out_all.value, w_kv)
    for bit in high:
        keyval.step(bit)
    w_out_all.step(2)
    keyval.value = after(keyval.value, down_cube, w_out_all.last, cot_cube.last)
    keyval.step(2)
    w_out_all.step(0)
    key_part, value_part = keyval.split(2)
    key_part.value = after(key_part.value, w_out_all.last)
    key_part.step(0)
    value_part.step(1)
    key_part.step(1)
    value_part.step(0)
    w_out_all.value = after(w_out_all.value, key_part.last, value_part.last)
    cot_cube.value = after(cot_cube.value, key_part.last, value_part.last)
    keyval = joined([key_part, value_part]).value.reshape(blocks, rows, 2 * HD)
    out_full = w_out_all.step(1).rows()
    cot_cube.step(0)
    query = project(normed, w_q, b_query, cosine, sine, heads)
    attended, attended_low, lse = attend(vis, query, keyval)
    attended_low = after(attended_low, cot_cube.last)
    cot_cube = cot_cube.done()
    attn = dot(attended_low, out_full, NT).astype(BF).reshape(2, low_rows, model)
    attn = halves(attn, core).astype(F32) + swap_mp(halves(attn, 1 - core)).astype(F32)
    middle = my_half(tokens).astype(F32) + attn
    gain_two = ffn_gain.astype(F32)
    inverse_two = lax.rsqrt(jnp.mean(middle * middle, axis=-1, keepdims=True) + epsilon)
    normed_two = (middle * inverse_two * gain_two).astype(BF)
    cube_two, came = cube_gather(normed_two)
    both_w = (both_own, swap_mp(both_own))
    down_w = (down_own, swap_mp(down_own))

    def collect(mine, theirs):
        return (mine + swap_mp(theirs.astype(BF)).astype(F32)).astype(BF)

    def over_high_back(value):
        return lax.psum_scatter(value, "h", scatter_dimension=0, tiled=True)

    lins, hiddens, grads = [], [], []
    for both in both_w:
        lin = dot(cube_two, both)
        gate, up = lin[:, :part], lin[:, part:]
        sigmoid_gate = jax.nn.sigmoid(gate)
        silu_gate = gate * sigmoid_gate
        hiddens.append((silu_gate * up).astype(BF))
        lins.append((gate, up, sigmoid_gate, silu_gate))
    down_back = collect(dot(cot_cube, hiddens[0], TN), dot(cot_cube, hiddens[1], TN))
    down_high = over_high_back(down_back)
    for (gate, up, sigmoid_gate, silu_gate), down in zip(lins, down_w):
        grad_hidden = dot(cot_cube, down)
        grad_gate = grad_hidden * up * sigmoid_gate * (1.0 + gate * (1.0 - sigmoid_gate))
        grad_up = grad_hidden * silu_gate
        grads.append(jnp.concatenate([grad_gate.astype(BF), grad_up.astype(BF)], axis=1))
    grad_two = dot(grads[0], both_w[0], NT) + dot(grads[1], both_w[1], NT)
    grad_two = grad_two.astype(BF)
    grads = [after(v, grad_two) for v in grads]
    both_mine, both_theirs = dot(cube_two, grads[0], TN), dot(cube_two, grads[1], TN)
    both_theirs = swap_mp(both_theirs.astype(BF)).astype(F32)
    gate_back = (both_mine[:, :part] + both_theirs[:, :part]).astype(BF)
    up_back = (both_mine[:, part:] + both_theirs[:, part:]).astype(BF)
    gate_high = over_high_back(gate_back)
    up_high = over_high_back(up_back)
    kept = [after(v, grad_two) for v in hiddens]
    grad_two, came = cube_scatter(grad_two, low_rows)
    grad_two = after(grad_two, down_back, gate_back, up_back)
    ffn = dot(kept[0], down_w[0], NT) + dot(kept[1], down_w[1], NT)
    ffn = CubeBack(after(ffn.astype(BF), *came[2]), low_rows)

    def whole(own):
        other = swap_mp(own)
        return jnp.where(
            core == 0, jnp.concatenate([own, other], 0), jnp.concatenate([other, own], 0)
        )

    grad_middle_norm, grad_gain_two = norm_back(grad_two, middle, inverse_two, gain_two)
    grad_middle_half = cot_half.astype(F32) + grad_middle_norm
    grad_attn = whole(grad_middle_half.astype(BF))
    grad_middle = whole(grad_middle_half)
    grad_attended = dot(grad_attn, out_full).astype(BF)
    out_grad = dot(grad_attn, attended_low, TN).astype(BF)
    grad_q, grad_kv_all = attend_back(
        vis, query, keyval, grad_attended, attended, lse, cosine, sine
    )
    low = [2] + high[::-1]

    def pair(grad):
        n = grad.shape[1] // 2
        return [Scatter(grad[:, :n], bits), Scatter(grad[:, n:], bits)]

    def merge(parts):
        parts[0].value = jnp.concatenate([p.value for p in parts], axis=-1)
        return parts[0]

    def hold(parts, *others):
        for p in parts:
            p.value = after(p.value, *others)

    ffn.step(1, grad_q)
    out_sum = pair(out_grad)
    out_sum[0].step(0, grad_q)
    out_sum[1].step(1, grad_q)
    kv_sum = pair(grad_kv_all.reshape(blocks * rows, 2 * HD))
    kv_sum[0].step(0)
    kv_sum[1].step(1)
    hold(out_sum, kv_sum[0].last, kv_sum[1].last)
    kv_sum[0].step(1)
    kv_sum[1].step(0)
    kv_sum = merge(kv_sum)
    out_sum[0].step(1)
    out_sum[1].step(0)
    out_sum = merge(out_sum)
    query_sum = pair(dot(normed, grad_q, TN).astype(BF))
    hold(query_sum, kv_sum.last)
    hold([ffn], kv_sum.last)
    query_sum[0].step(0)
    query_sum[1].step(1)
    ffn.step(0)
    kv_sum.step(2)
    out_sum.step(2)
    hold([kv_sum], query_sum[0].last, query_sum[1].last, out_sum.last)
    for bit in high[::-1]:
        kv_sum.step(bit)
        out_sum.step(bit)
    kv_mine = kv_sum.value
    hold(query_sum, kv_sum.last)
    hold([ffn], kv_sum.last)
    query_sum[0].step(1)
    query_sum[1].step(0)
    query_sum = merge(query_sum)
    ffn.step(2)
    mixed = whole((middle + ffn.value).astype(BF))
    grad_k = rotate(kv_mine[:, :HD], cosine, -sine).astype(BF)
    grad_v = kv_mine[:, HD:].astype(BF)
    grad_kv = jnp.concatenate([grad_k, grad_v], axis=1)
    last = Scatter(dot(normed, grad_kv, TN).astype(BF), bits)
    grad_normed = (dot(grad_q, w_q, NT) + dot(grad_kv, w_kv, NT)).astype(BF)
    other_normed = swap_mp(grad_normed)
    last.step(1)
    grad_normed = grad_normed.astype(F32) + other_normed.astype(F32)
    grad_input_norm, grad_gain_one = norm_back(grad_normed, inputs, inverse_one, gain_one)
    bias_query = jnp.sum(grad_q.astype(F32), axis=0)
    bias_kv = jnp.sum(grad_kv.astype(F32), axis=0)
    gain_two_sum = grad_gain_two + swap_mp(grad_gain_two)
    small = jnp.concatenate([grad_gain_one, gain_two_sum, bias_query, bias_kv]).reshape(-1, 128)
    hold([last], query_sum.last, other_normed)
    last.step(0)
    query_sum.step(2)
    came = flip(small, 0)
    small = small + came
    hold([last], came)
    last.step(2)
    came = flip(small, 1)
    small = small + came
    hold([last], came)
    for bit in high[::-1]:
        query_sum.step(bit)
        last.step(bit)
    for bit in range(2, bits):
        small = small + flip(small, bit)
    small = small.reshape(-1)
    out_part, query_part, kv_part = out_sum.value, query_sum.value, last.value

    def home(value, *others):
        return trade(after(value, *others).reshape(8, slab, part), CUBE_AXES)

    down_back = home(down_high)
    gate_back = home(gate_high, down_back)
    up_back = home(up_high, gate_back)
    gate_part, up_part, down_part = unpack(gate_back, up_back, down_back, w_gate.shape[1])
    grad_tokens = grad_middle + grad_input_norm
    gain_one_sum = small[:model]
    gain_two_sum = small[model : 2 * model]
    bias_query_sum = small[2 * model : 2 * model + width]
    bias_key_sum = small[2 * model + width : 2 * model + width + HD]
    bias_value_sum = small[2 * model + width + HD :]
    return (
        mixed,
        grad_tokens,
        gain_one_sum,
        query_part,
        bias_query_sum,
        kv_part[:, :HD],
        bias_key_sum,
        kv_part[:, HD:],
        bias_value_sum,
        out_part.T,
        gain_two_sum,
        gate_part,
        up_part,
        down_part,
    )


def solution(mesh):
    blocks, cores = mesh.devices.shape
    mesh = Mesh(
        mesh.devices.reshape(blocks // 8, 2, 2, 2, cores), ("h", "a", "y", "x", "mp")
    )
    blk = ("h", "a", "y", "x")
    placed = (
        P(blk, None),
        P(blk, None),
        P(),
        P(blk, "mp"),
        P("mp"),
        P(blk, "mp"),
        P("mp"),
        P(blk, "mp"),
        P("mp"),
        P("mp", blk),
        P(),
        P(blk, "mp"),
        P(blk, "mp"),
        P("mp", blk),
        P(),
        P(),
    )
    return jax.shard_map(
        shards,
        mesh=mesh,
        in_specs=placed,
        out_specs=(
            P(blk, None),
            P(blk, None),
            P(),
            P(blk, "mp"),
            P("mp"),
            P(blk, "mp"),
            P("mp"),
            P(blk, "mp"),
            P("mp"),
            P("mp", blk),
            P(),
            P(blk, "mp"),
            P(blk, "mp"),
            P("mp", blk),
        ),
        check_vma=False,
    )
```

time: 826 us -> 636 us (0.77)
  the two profiles are of different devices: /device:TPU:1 before, /device:TPU:0 now
where the time goes in v2:
time: 636 us; the launch traced here: 626 us
  waiting for transfers between devices  302 us (47%)
  starting transfers between devices  113 us (18%)
  matrix products  70 us (11%)
  other arithmetic  62.2 us (10%)
  local copies, waits for them, and re-layouts  44 us (7%)
  between operations  20.1 us (3%)
  Pallas kernels  14.5 us (2%)
    ppermute x70, waiting for transfers between devices, flip(): lax.ppermute(value, axis, [(i, i ^ mask) for i in range(lax.axis_size(axi...  237 us
    ppermute x70, starting transfers between devices, flip(): lax.ppermute(value, axis, [(i, i ^ mask) for i in range(lax.axis_size(axi...  90.2 us
    dot_general x19, matrix products, dot(): return lax.dot_general(left, right, dims, preferred_element_type=F32)  70 us
    all_gather x1, waiting for transfers between devices, shards(): lax.all_gather(both_cube.reshape(8 * slab, -1), 'h', axis=0, tiled=True)  40 us
    unnamed x167, local copies, waits for them, and re-layouts  31.2 us
    all_to_all x5, waiting for transfers between devices, trade(): return lax.all_to_all(value, axes, dim, dim, tiled=True)  24.5 us
    all_to_all x5, starting transfers between devices, trade(): return lax.all_to_all(value, axes, dim, dim, tiled=True)  20.8 us
  transfers between devices with their start and end apart: 90, of which 43 were waited for; matrix products, arithmetic and copies ran while one was open for 24% of the time, Pallas kernels for 2%

profile of v2, /device:TPU:0, one launch (start us, length us, event | category | flops | bytes accessed | tf_op | source)
XLA Modules:
  0.0 626.4 jit_solution(3490304330998177699)
XLA Ops:
  30.9 21.1 %all-to-all-done = bf16[8,96,1280]{2,1,0:T(8,128)(2,1)} async-done(((bf16[8,96,1280]{2,1,0:T(8,128)(2,1)}), bf16[8,96,1280]{2,1,0:T(8,128)(2,1)}, u32[]{:S(2)}, u32[]{:S(2)}) %all-to-all-start) | async-done | bytes 1966112 | tf_op jit(solution)/shard_map/all_to_all | solution.py:48
  89.0 6.6 %collective-permute-start.11 = (bf16[2,2,2,96,256]{4,3,0,1,2:T(8,128)(2,1)}, bf16[2,2,2,96,256]{4,3,0,1,2:T(8,128)(2,1)}, u32[]{:S(2)}, u32[]{:S(2)}) collective-permute-start(bf16[2,2,2,96,256]{4,3,0,1,2:T(8,128)(2,1)} %maximum_select_fusion.22), channel_id=1, source_target_pairs={{0,2},{2,0},{1,3},{3,1},{4,6},{6,4},{5,7},{7,5},{8,10},{10,8},{9,1... | collective-permute-start | bytes 1179656 | tf_op jit(solution)/shard_map/ppermute | solution.py:31
  107.9 6.5 %collective-permute-start.12 = (bf16[256,256]{1,0:T(8,128)(2,1)S(1)}, bf16[256,256]{1,0:T(8,128)(2,1)S(1)}, u32[]{:S(2)}, u32[]{:S(2)}) collective-permute-start(bf16[256,256]{1,0:T(8,128)(2,1)S(1)} %shard_map.265), channel_id=1, source_target_pairs={{0,16},{16,0},{1,17},{17,1},{2,18},{18,2},{3,19},{19,3},{4,20},{20... | collective-permute-start | bytes 393224 | tf_op jit(solution)/shard_map/ppermute | solution.py:31
  115.9 7.4 %collective-permute-done.12 = bf16[256,256]{1,0:T(8,128)(2,1)S(1)} collective-permute-done((bf16[256,256]{1,0:T(8,128)(2,1)S(1)}, bf16[256,256]{1,0:T(8,128)(2,1)S(1)}, u32[]{:S(2)}, u32[]{:S(2)}) %collective-permute-start.12) | collective-permute-done | bytes 131104 | tf_op jit(solution)/shard_map/ppermute | solution.py:31
  123.4 18.3 %collective-permute-done.13 = bf16[2,96,768]{2,1,0:T(8,128)(2,1)S(1)} collective-permute-done((bf16[2,96,768]{2,1,0:T(8,128)(2,1)S(1)}, bf16[2,96,768]{2,1,0:T(8,128)(2,1)S(1)}, u32[]{:S(2)}, u32[]{:S(2)}) %collective-permute-start.13) | collective-permute-done | bytes 294944 | tf_op jit(solution)/shard_map/ppermute | solution.py:31
  142.1 9.2 %collective-permute-done.15 = bf16[2,256,256]{2,1,0:T(8,128)(2,1)S(1)} collective-permute-done((bf16[2,256,256]{2,1,0:T(8,128)(2,1)S(1)}, bf16[2,256,256]{2,1,0:T(8,128)(2,1)S(1)}, u32[]{:S(2)}, u32[]{:S(2)}) %collective-permute-start.15) | collective-permute-done | bytes 262176 | tf_op jit(solution)/shard_map/ppermute | solution.py:31
  167.5 7.7 %collective-permute-done.20 = bf16[2,2,2,256,128]{4,3,0,1,2:T(8,128)(2,1)S(1)} collective-permute-done((bf16[2,2,2,256,128]{4,3,0,1,2:T(8,128)(2,1)S(1)}, bf16[2,2,2,256,128]{4,3,0,1,2:T(8,128)(2,1)S(1)}, u32[]{:S(2)}, u32[]{:S(2)}) %collective-permute-start.20) | collective-permute-done | bytes 524320 | tf_op jit(solution)/shard_map/ppermute | solution.py:31
  188.6 40.0 %all-gather.3.cloned.1.call-done = bf16[1536,1280]{1,0:T(8,128)(2,1)} async-done(((bf16[768,1280]{1,0:T(8,128)(2,1)}), bf16[1536,1280]{1,0:T(8,128)(2,1)}) %all-gather.3.cloned.1.call-update) | async-done | bytes 3932176 | tf_op jit(solution)/shard_map/all_gather | solution.py:537
  256.5 7.8 %collective-permute-done.31 = bf16[160,1536]{1,0:T(8,128)(2,1)S(1)} collective-permute-done((bf16[160,1536]{1,0:T(8,128)(2,1)S(1)}, bf16[160,1536]{1,0:T(8,128)(2,1)S(1)}, u32[]{:S(2)}, u32[]{:S(2)}) %collective-permute-start.31) | collective-permute-done | bytes 491552 | tf_op jit(solution)/shard_map/ppermute | solution.py:31
  274.7 6.7 %fusion.67 = f32[1024,1536]{1,0:T(8,128)} fusion(bf16[1536,1280]{1,0:T(8,128)(2,1)S(1)} %copy-done.54, bf16[1024,640]{1,0:T(8,128)(2,1)S(1)} %get-tuple-element.197, bf16[1024,640]{1,0:T(8,128)(2,1)S(1)} %get-tuple-element.196), kind=kOutput, calls=%fused_computation.351 | convolution fusion | flops 4031774720 | bytes 12845056 | tf_op jit(solution)/shard_map/dot_general | solution.py:226
  291.7 7.6 %add_convert_fusion.1 = bf16[1024,1536]{1,0:T(8,128)(2,1)S(1)} fusion(f32[1024,1536]{1,0:T(8,128)} %fusion.67, bf16[1536,1280]{1,0:T(8,128)(2,1)} %copy-done.55, bf16[1024,640]{1,0:T(8,128)(2,1)S(1)} %get-tuple-element.195, bf16[1024,640]{1,0:T(8,128)(2,1)S(1)} %get-tuple-element.194), kind=kOutput, calls=%fused_computation.2 | convolution fusion | flops 4034920448 | bytes 15990784 | tf_op jit(solution)/shard_map/dot_general | solution.py:226
  305.5 6.1 convolution_convert_fusion
  312.1 6.5 %fusion.82 = f32[1536,1280]{1,0:T(8,128)} fusion(bf16[1024,1536]{1,0:T(8,128)(2,1)S(1)} %constant_dynamic-update-slice_fusion.2, bf16[1024,1280]{1,0:T(8,128)(2,1)S(1)} %pad_maximum_fusion.1), kind=kOutput, calls=%fused_computation.365 | convolution fusion | flops 4026531840 | bytes 13631488 | tf_op jit(solution)/shard_map/dot_general | solution.py:226
  359.0 6.1 fusion
  390.8 25.7 %collective-permute-done.44 = bf16[512,1536]{1,0:T(8,128)(2,1)} collective-permute-done((bf16[512,1536]{1,0:T(8,128)(2,1)}, bf16[512,1536]{1,0:T(8,128)(2,1)}, u32[]{:S(2)}, u32[]{:S(2)}) %collective-permute-start.44) | collective-permute-done | bytes 1572896 | tf_op jit(solution)/shard_map/ppermute | solution.py:31
  434.2 10.1 %collective-permute-done.56 = bf16[2,2,2,96,384]{4,3,0,1,2:T(8,128)(2,1)S(1)} collective-permute-done((bf16[2,2,2,96,384]{4,3,0,1,2:T(8,128)(2,1)S(1)}, bf16[2,2,2,96,384]{4,3,0,1,2:T(8,128)(2,1)S(1)}, u32[]{:S(2)}, u32[]{:S(2)}) %collective-permute-start.56) | collective-permute-done | bytes 589856 | tf_op jit(solution)/shard_map/ppermute | solution.py:31
  459.5 13.2 %collective-permute-done.60 = bf16[2,96,768]{2,1,0:T(8,128)(2,1)S(1)} collective-permute-done((bf16[2,96,768]{2,1,0:T(8,128)(2,1)S(1)}, bf16[2,96,768]{2,1,0:T(8,128)(2,1)S(1)}, u32[]{:S(2)}, u32[]{:S(2)}) %collective-permute-start.60) | collective-permute-done | bytes 294944 | tf_op jit(solution)/shard_map/ppermute | solution.py:31
  473.3 7.7 %collective-permute-done.53 = bf16[2,256,256]{2,1,0:T(8,128)(2,1)S(1)} collective-permute-done((bf16[2,256,256]{2,1,0:T(8,128)(2,1)S(1)}, bf16[2,256,256]{2,1,0:T(8,128)(2,1)S(1)}, u32[]{:S(2)}, u32[]{:S(2)}) %collective-permute-start.53) | collective-permute-done | bytes 262176 | tf_op jit(solution)/shard_map/ppermute | solution.py:31
  483.4 16.4 %collective-permute-done.79 = bf16[96,768]{1,0:T(8,128)(2,1)S(1)} collective-permute-done((bf16[96,768]{1,0:T(8,128)(2,1)S(1)}, bf16[96,768]{1,0:T(8,128)(2,1)S(1)}, u32[]{:S(2)}, u32[]{:S(2)}) %collective-permute-start.79) | collective-permute-done | bytes 147488 | tf_op jit(solution)/shard_map/ppermute | solution.py:31
  501.1 9.6 %collective-permute-done.61 = bf16[256,256]{1,0:T(8,128)(2,1)S(1)} collective-permute-done((bf16[256,256]{1,0:T(8,128)(2,1)S(1)}, bf16[256,256]{1,0:T(8,128)(2,1)S(1)}, u32[]{:S(2)}, u32[]{:S(2)}) %collective-permute-start.61) | collective-permute-done | bytes 131104 | tf_op jit(solution)/shard_map/ppermute | solution.py:31
  530.6 14.0 %collective-permute-done.75 = bf16[2,2,2,96,256]{4,3,0,1,2:T(8,128)(2,1)S(1)} collective-permute-done((bf16[2,2,2,96,256]{4,3,0,1,2:T(8,128)(2,1)}, bf16[2,2,2,96,256]{4,3,0,1,2:T(8,128)(2,1)S(1)}, u32[]{:S(2)}, u32[]{:S(2)}) %collective-permute-start.75) | collective-permute-done | bytes 393248 | tf_op jit(solution)/shard_map/ppermute | solution.py:31
  544.9 9.3 %collective-permute-done.62 = bf16[128,1536]{1,0:T(8,128)(2,1)S(1)} collective-permute-done((bf16[128,1536]{1,0:T(8,128)(2,1)S(1)}, bf16[128,1536]{1,0:T(8,128)(2,1)S(1)}, u32[]{:S(2)}, u32[]{:S(2)}) %collective-permute-start.62) | collective-permute-done | bytes 393248 | tf_op jit(solution)/shard_map/ppermute | solution.py:31
  564.2 11.8 %collective-permute-done.67 = f32[32,128]{1,0:T(8,128)S(1)} collective-permute-done((f32[32,128]{1,0:T(8,128)S(1)}, f32[32,128]{1,0:T(8,128)S(1)}, u32[]{:S(2)}, u32[]{:S(2)}) %collective-permute-start.67) | collective-permute-done | bytes 16416 | tf_op jit(solution)/shard_map/ppermute | solution.py:31
  598.3 8.5 %collective-permute-done.77 = bf16[2,96,256]{2,1,0:T(8,128)(2,1)S(1)} collective-permute-done((bf16[2,96,256]{2,1,0:T(8,128)(2,1)S(1)}, bf16[2,96,256]{2,1,0:T(8,128)(2,1)S(1)}, u32[]{:S(2)}, u32[]{:S(2)}) %collective-permute-start.77) | collective-permute-done | bytes 98336 | tf_op jit(solution)/shard_map/ppermute | solution.py:31
  (530 shorter events, 322.2 us)
Async XLA Ops:
  20.6 31.4 %all-to-all-start = ((bf16[8,96,1280]{2,1,0:T(8,128)(2,1)}), bf16[8,96,1280]{2,1,0:T(8,128)(2,1)}, u32[]{:S(2)}, u32[]{:S(2)}) async-start(bf16[8,96,1280]{2,1,0:T(8,128)(2,1)} %get-tuple-element.81), calls=%async_computation | async-start | bytes 3932160 | tf_op jit(solution)/shard_map/all_to_all | solution.py:48
  25.3 49.7 %collective-permute-start.7 = (bf16[128,1536]{1,0:T(8,128)(2,1)S(1)}, bf16[128,1536]{1,0:T(8,128)(2,1)}, u32[]{:S(2)}, u32[]{:S(2)}) collective-permute-start(bf16[128,1536]{1,0:T(8,128)(2,1)S(1)} %dynamic-slice_bitcast_fusion.1), channel_id=1, source_target_pairs={{0,4},{4,0},{1,5},{5,1},{2,6},{6,2},{3,7},{7,3},{8,12},{12,8},{9,1... | collective-permute-start | bytes 1179656 | tf_op jit(solution)/shard_map/ppermute | solution.py:31
  27.2 47.8 %collective-permute-start.8 = (bf16[96,768]{1,0:T(8,128)(2,1)}, bf16[96,768]{1,0:T(8,128)(2,1)}, u32[]{:S(2)}, u32[]{:S(2)}) collective-permute-start(bf16[96,768]{1,0:T(8,128)(2,1)} %bitcast.24), channel_id=1, source_target_pairs={{0,16},{16,0},{1,17},{17,1},{2,18},{18,2},{3,19},{19,3},{4,20},{20... | collective-permute-start | bytes 442376 | tf_op jit(solution)/shard_map/ppermute | solution.py:31
  56.6 132.0 %all-gather.5.cloned.1.call-start = ((), (), s32[]{:S(2)}) async-start(), calls=%async_computation.9 | async-start | bytes 2949120 | tf_op jit(solution)/shard_map/all_gather | solution.py:538
  70.0 158.5 %all-gather.3.cloned.1.call-start = ((), (), s32[]{:S(2)}) async-start(), calls=%async_computation.8 | async-start | bytes 5898240 | tf_op jit(solution)/shard_map/all_gather | solution.py:537
  96.7 422.2 %reduce-scatter.6.cloned.1.call-start = ((), (), s32[]{:S(2)}) async-start(), calls=%async_computation.11 | async-start | bytes 2949120 | tf_op jit(solution)/shard_map/reduce_scatter | solution.py:609
  96.9 44.9 %collective-permute-start.14 = (bf16[256,1536]{1,0:T(8,128)(2,1)S(1)}, bf16[256,1536]{1,0:T(8,128)(2,1)S(1)}, u32[]{:S(2)}, u32[]{:S(2)}) collective-permute-start(bf16[256,1536]{1,0:T(8,128)(2,1)S(1)} %pad_maximum_fusion.6), channel_id=1, source_target_pairs={{0,8},{8,0},{1,9},{9,1},{2,10},{10,2},{3,11},{11,3},{4,12},{12,4},... | collective-permute-start | bytes 2359304 | tf_op jit(solution)/shard_map/ppermute | solution.py:31
  100.8 65.9 %collective-permute-start.6 = (bf16[2,2,2,96,384]{4,3,0,1,2:T(8,128)(2,1)S(1)}, bf16[2,2,2,96,384]{4,3,0,1,2:T(8,128)(2,1)S(1)}, u32[]{:S(2)}, u32[]{:S(2)}) collective-permute-start(bf16[2,2,2,96,384]{4,3,0,1,2:T(8,128)(2,1)S(1)} %maximum_select_fusion.14), channel_id=1, source_target_pairs={{0,2},{2,0},{1,3},{3,1},{4,6},{6,4},{5,7},{7,5},{8,10},{10,8},{9,1... | collective-permute-start | bytes 1769480 | tf_op jit(solution)/shard_map/ppermute | solution.py:31
  115.1 52.0 %collective-permute-start.4 = (bf16[2,2,2,96,384]{4,3,0,1,2:T(8,128)(2,1)S(1)}, bf16[2,2,2,96,384]{4,3,0,1,2:T(8,128)(2,1)S(1)}, u32[]{:S(2)}, u32[]{:S(2)}) collective-permute-start(bf16[2,2,2,96,384]{4,3,0,1,2:T(8,128)(2,1)S(1)} %maximum_select_fusion.12), channel_id=1, source_target_pairs={{0,4},{4,0},{1,5},{5,1},{2,6},{6,2},{3,7},{7,3},{8,12},{12,8},{9,1... | collective-permute-start | bytes 1769480 | tf_op jit(solution)/shard_map/ppermute | solution.py:31
  179.4 52.1 %collective-permute-start.21 = (bf16[512,1536]{1,0:T(8,128)(2,1)}, bf16[512,1536]{1,0:T(8,128)(2,1)}, u32[]{:S(2)}, u32[]{:S(2)}) collective-permute-start(bf16[512,1536]{1,0:T(8,128)(2,1)} %pad_maximum_fusion.5), channel_id=1, source_target_pairs={{0,2},{2,0},{1,3},{3,1},{4,6},{6,4},{5,7},{7,5},{8,10},{10,8},{9,1... | collective-permute-start | bytes 4718600 | tf_op jit(solution)/shard_map/ppermute | solution.py:31
  180.5 48.1 %collective-permute-start.22 = (bf16[2,2,2,96,768]{4,3,2,1,0:T(8,128)(2,1)}, bf16[2,2,2,96,768]{4,3,2,1,0:T(8,128)(2,1)}, u32[]{:S(2)}, u32[]{:S(2)}) collective-permute-start(bf16[2,2,2,96,768]{4,3,2,1,0:T(8,128)(2,1)} %maximum_select_fusion.4), channel_id=1, source_target_pairs={{0,4},{4,0},{1,5},{5,1},{2,6},{6,2},{3,7},{7,3},{8,12},{12,8},{9,1... | collective-permute-start | bytes 3538952 | tf_op jit(solution)/shard_map/ppermute | solution.py:31
  188.6 97.1 %collective-permute-start.33 = (bf16[1536,640]{1,0:T(8,128)(2,1)}, bf16[1536,640]{1,0:T(8,128)(2,1)}, u32[]{:S(2)}, u32[]{:S(2)}) collective-permute-start(bf16[1536,640]{1,0:T(8,128)(2,1)} %all-gather.5.cloned.1.call-done), channel_id=1, source_target_pairs={{0,1},{1,0},{2,3},{3,2},{4,5},{5,4},{6,7},{7,6},{8,9},{9,8},{10,11... | collective-permute-start | bytes 5898248 | tf_op jit(solution)/shard_map/ppermute | solution.py:40
  228.5 52.9 %collective-permute-start.34 = (bf16[1536,1280]{1,0:T(8,128)(2,1)}, bf16[1536,1280]{1,0:T(8,128)(2,1)S(1)}, u32[]{:S(2)}, u32[]{:S(2)}) collective-permute-start(bf16[1536,1280]{1,0:T(8,128)(2,1)} %all-gather.3.cloned.1.call-done), channel_id=1, source_target_pairs={{0,1},{1,0},{2,3},{3,2},{4,5},{5,4},{6,7},{7,6},{8,9},{9,8},{10,11... | collective-permute-start | bytes 11796488 | tf_op jit(solution)/shard_map/ppermute | solution.py:40
  305.4 33.7 %collective-permute-start.45 = (bf16[1536,640]{1,0:T(8,128)(2,1)S(1)}, bf16[1536,640]{1,0:T(8,128)(2,1)S(1)}, u32[]{:S(2)}, u32[]{:S(2)}) collective-permute-start(bf16[1536,640]{1,0:T(8,128)(2,1)S(1)} %convolution_convert_fusion.3), channel_id=1, source_target_pairs={{0,1},{1,0},{2,3},{3,2},{4,5},{5,4},{6,7},{7,6},{8,9},{9,8},{10,11... | collective-permute-start | bytes 5898248 | tf_op jit(solution)/shard_map/ppermute | solution.py:40
  311.6 44.7 %collective-permute-start.46 = (bf16[1536,1280]{1,0:T(8,128)(2,1)}, bf16[1536,1280]{1,0:T(8,128)(2,1)}, u32[]{:S(2)}, u32[]{:S(2)}) collective-permute-start(bf16[1536,1280]{1,0:T(8,128)(2,1)} %convolution_convert_fusion), channel_id=1, source_target_pairs={{0,1},{1,0},{2,3},{3,2},{4,5},{5,4},{6,7},{7,6},{8,9},{9,8},{10,11... | collective-permute-start | bytes 11796488 | tf_op jit(solution)/shard_map/ppermute | solution.py:40
  343.0 214.8 %reduce-scatter.4.cloned.1.call-start = ((), (), s32[]{:S(2)}) async-start(), calls=%async_computation.10 | async-start | bytes 2949120 | tf_op jit(solution)/shard_map/reduce_scatter | solution.py:609
  365.1 225.4 %reduce-scatter.8.cloned.1.call-start = ((), (), s32[]{:S(2)}) async-start(), calls=%async_computation.12 | async-start | bytes 2949120 | tf_op jit(solution)/shard_map/reduce_scatter | solution.py:609
  379.4 37.1 %collective-permute-start.44 = (bf16[512,1536]{1,0:T(8,128)(2,1)}, bf16[512,1536]{1,0:T(8,128)(2,1)}, u32[]{:S(2)}, u32[]{:S(2)}) collective-permute-start(bf16[512,1536]{1,0:T(8,128)(2,1)} %get-tuple-element.201), channel_id=1, source_target_pairs={{0,4},{4,0},{1,5},{5,1},{2,6},{6,2},{3,7},{7,3},{8,12},{12,8},{9,1... | collective-permute-start | bytes 4718600 | tf_op jit(solution)/shard_map/ppermute | solution.py:31
  380.1 201.3 %collective-permute-start.64 = (f32[128,1536]{1,0:T(8,128)}, f32[128,1536]{1,0:T(8,128)}, u32[]{:S(2)}, u32[]{:S(2)}) collective-permute-start(f32[128,1536]{1,0:T(8,128)} %get-tuple-element.189), channel_id=1, source_target_pairs={{0,1},{1,0},{2,3},{3,2},{4,5},{5,4},{6,7},{7,6},{8,9},{9,8},{10,11... | collective-permute-start | bytes 2359304 | tf_op jit(solution)/shard_map/ppermute | solution.py:40
  451.6 77.0 %collective-permute-start.50 = (bf16[256,1536]{1,0:T(8,128)(2,1)}, bf16[256,1536]{1,0:T(8,128)(2,1)}, u32[]{:S(2)}, u32[]{:S(2)}) collective-permute-start(bf16[256,1536]{1,0:T(8,128)(2,1)} %slice.408), channel_id=1, source_target_pairs={{0,2},{2,0},{1,3},{3,1},{4,6},{6,4},{5,7},{7,5},{8,10},{10,8},{9,1... | collective-permute-start | bytes 2359304 | tf_op jit(solution)/shard_map/ppermute | solution.py:31
  458.6 42.0 %collective-permute-start.54 = (bf16[2,2,2,96,384]{4,3,0,1,2:T(8,128)(2,1)S(1)}, bf16[2,2,2,96,384]{4,3,0,1,2:T(8,128)(2,1)S(1)}, u32[]{:S(2)}, u32[]{:S(2)}) collective-permute-start(bf16[2,2,2,96,384]{4,3,0,1,2:T(8,128)(2,1)S(1)} %copy_bitcast_fusion.5), channel_id=1, source_target_pairs={{0,2},{2,0},{1,3},{3,1},{4,6},{6,4},{5,7},{7,5},{8,10},{10,8},{9,1... | collective-permute-start | bytes 1769480 | tf_op jit(solution)/shard_map/ppermute | solution.py:31
  514.7 41.1 %collective-permute-start.65 = (bf16[256,1536]{1,0:T(8,128)(2,1)}, bf16[256,1536]{1,0:T(8,128)(2,1)}, u32[]{:S(2)}, u32[]{:S(2)}) collective-permute-start(bf16[256,1536]{1,0:T(8,128)(2,1)} %fusion.4), channel_id=1, source_target_pairs={{0,1},{1,0},{2,3},{3,2},{4,5},{5,4},{6,7},{7,6},{8,9},{9,8},{10,11... | collective-permute-start | bytes 2359304 | tf_op jit(solution)/shard_map/ppermute | solution.py:40
  518.9 38.8 %all-to-all-start.2 = ((bf16[8,96,640]{2,1,0:T(8,128)(2,1)}), bf16[8,96,640]{2,1,0:T(8,128)(2,1)S(1)}, u32[]{:S(2)}, u32[]{:S(2)}) async-start(bf16[8,96,640]{2,1,0:T(8,128)(2,1)} %bitcast.442), calls=%async_computation.4 | async-start | bytes 1966080 | tf_op jit(solution)/shard_map/all_to_all | solution.py:48
  557.8 32.7 %all-to-all-start.3 = ((bf16[8,96,640]{2,1,0:T(8,128)(2,1)}), bf16[8,96,640]{2,1,0:T(8,128)(2,1)S(1)}, u32[]{:S(2)}, u32[]{:S(2)}) async-start(bf16[8,96,640]{2,1,0:T(8,128)(2,1)} %bitcast.441), calls=%async_computation.5 | async-start | bytes 1966080 | tf_op jit(solution)/shard_map/all_to_all | solution.py:48
  (126 other events, 1536.8 us)
Sparse Core Ops, SparseCore 0:
  70.2 60.8 all-gather.4
  132.6 95.8 all-gather.2
  343.1 50.2 reduce-scatter.5
  395.6 51.3 reduce-scatter.3
  449.1 63.3 reduce-scatter.7

commit v3 on v2

--- a/solution.py
+++ b/solution.py
@@ -49,6 +49,8 @@
 
 
 def after(value, *others):
+    if not others:
+        return value
     return lax.optimization_barrier((value,) + others)[0]
 
 
@@ -152,45 +154,30 @@
         return jnp.concatenate(pieces, 0)
 
 
-class CubeBack:
+class CubeSum:
     def __init__(self, value, rows):
-        have = [0]
-        for bit in (2, 0, 1):
-            have = have + [h ^ (1 << bit) for h in have]
-        pieces, at = {}, 0
-        for size, order in zip(cube_parts(rows), CUBE):
-            wanted = [0]
-            for bit in order:
-                wanted = wanted + [w ^ (1 << bit) for w in wanted]
-            for w in wanted:
-                pieces.setdefault(w, []).append(value[at : at + size])
-                at += size
-        self.value = jnp.concatenate([p for w in have for p in pieces[w]], 0)
-
-    def step(self, bit, *others):
-        half = self.value.shape[0] // 2
-        other = flip(self.value[half:], bit)
-        if others:
-            other = after(other, *others)
-        self.value = self.value[:half].astype(F32) + other.astype(F32)
-        if bit != 2:
-            self.value = self.value.astype(BF)
+        self.parts, self.number, at = [], 0, 0
+        for size in cube_parts(rows):
+            self.parts.append(value[at : at + 8 * size])
+            at += 8 * size
+
+    def step(self, *others):
+        half = [part.shape[0] // 2 for part in self.parts]
+        sent = [
+            flip(after(p[n:], *others), order[2 - self.number])
+            for p, n, order in zip(self.parts, half, CUBE)
+        ]
+        self.came = together(sent)
+        self.parts = [
+            p[:n].astype(F32) + v.astype(F32) for p, n, v in zip(self.parts, half, self.came)
+        ]
+        self.number += 1
+        if self.number < 3:
+            self.parts = [p.astype(BF) for p in self.parts]
         return self
 
-
-def cube_scatter(value, rows):
-    parts, at, came = [], 0, []
-    for size in cube_parts(rows):
-        parts.append(value[at : at + 8 * size])
-        at += 8 * size
-    for step in range(3):
-        half = [part.shape[0] // 2 for part in parts]
-        sent = [flip(p[n:], order[2 - step]) for p, n, order in zip(parts, half, CUBE)]
-        came.append(together(sent))
-        parts = [p[:n].astype(F32) + v.astype(F32) for p, n, v in zip(parts, half, came[-1])]
-        if step < 2:
-            parts = [p.astype(BF) for p in parts]
-    return jnp.concatenate(parts, 0), came
+    def total(self):
+        return jnp.concatenate(self.parts, 0)
 
 
 def rotate(value, cosine, sine):
@@ -437,7 +424,7 @@
 
     both_out[0, :, :part] = kept(gate_ref[:, cols])
     both_out[0, :, part:] = kept(up_ref[:, cols])
-    down_out[0] = kept(down_ref[cols, :].astype(F32).T)
+    down_out[0] = kept(down_ref[:, cols])
 
 
 def pack(w_gate, w_up, w_down, part):
@@ -466,7 +453,7 @@
         here, width = slice(at * 128, (at + size) * 128), size * 128
         gate_out[:, here] = gate_ref[c, :, :width].astype(F32)
         up_out[:, here] = up_ref[c, :, :width].astype(F32)
-        down_out[here, :] = down_ref[c, :, :width].astype(F32).T
+        down_out[:, here] = down_ref[c, :, :width].astype(F32)
 
 
 def unpack(gate, up, down, hidden):
@@ -477,7 +464,7 @@
         out_shape=(
             jax.ShapeDtypeStruct((slab, hidden), F32),
             jax.ShapeDtypeStruct((slab, hidden), F32),
-            jax.ShapeDtypeStruct((hidden, slab), F32),
+            jax.ShapeDtypeStruct((slab, hidden), F32),
         ),
         in_specs=[vmem] * 3,
         out_specs=(vmem,) * 3,
@@ -521,7 +508,7 @@
     bits = blocks.bit_length() - 1
     high = list(range(3, bits))[::-1]
 
-    both_send, down_send = pack(w_gate, w_up, w_down, part)
+    both_send, down_send = pack(w_gate, w_up, w_down.T, part)
     w_kv = Gather(jnp.concatenate([w_key, w_value], axis=1))
     w_q = Gather(w_query)
     w_out_all = Gather(w_out.T)
@@ -555,7 +542,7 @@
     gain_one = norm_gain.astype(F32)
     inverse_one = lax.rsqrt(jnp.mean(inputs * inputs, axis=-1, keepdims=True) + epsilon)
     normed = (inputs * inverse_one * gain_one).astype(BF)
-    w_kv.value = after(w_kv.value, both_cube, cosine, vis, normed, cot_cube.last, w_out_all.last)
+    w_kv.value = after(w_kv.value, both_cube, cosine, vis, normed)
     w_q.value = after(w_q.value, both_cube)
     w_kv.step(2)
     w_q.step(2)
@@ -599,11 +586,10 @@
     inverse_two = lax.rsqrt(jnp.mean(middle * middle, axis=-1, keepdims=True) + epsilon)
     normed_two = (middle * inverse_two * gain_two).astype(BF)
     cube_two, came = cube_gather(normed_two)
+    both_own = after(both_own, *came)
+    down_own = after(down_own, *came)
     both_w = (both_own, swap_mp(both_own))
     down_w = (down_own, swap_mp(down_own))
-
-    def collect(mine, theirs):
-        return (mine + swap_mp(theirs.astype(BF)).astype(F32)).astype(BF)
 
     def over_high_back(value):
         return lax.psum_scatter(value, "h", scatter_dimension=0, tiled=True)
@@ -616,8 +602,6 @@
         silu_gate = gate * sigmoid_gate
         hiddens.append((silu_gate * up).astype(BF))
         lins.append((gate, up, sigmoid_gate, silu_gate))
-    down_back = collect(dot(cot_cube, hiddens[0], TN), dot(cot_cube, hiddens[1], TN))
-    down_high = over_high_back(down_back)
     for (gate, up, sigmoid_gate, silu_gate), down in zip(lins, down_w):
         grad_hidden = dot(cot_cube, down)
         grad_gate = grad_hidden * up * sigmoid_gate * (1.0 + gate * (1.0 - sigmoid_gate))
@@ -626,17 +610,24 @@
     grad_two = dot(grads[0], both_w[0], NT) + dot(grads[1], both_w[1], NT)
     grad_two = grad_two.astype(BF)
     grads = [after(v, grad_two) for v in grads]
-    both_mine, both_theirs = dot(cube_two, grads[0], TN), dot(cube_two, grads[1], TN)
-    both_theirs = swap_mp(both_theirs.astype(BF)).astype(F32)
-    gate_back = (both_mine[:, :part] + both_theirs[:, :part]).astype(BF)
-    up_back = (both_mine[:, part:] + both_theirs[:, part:]).astype(BF)
+    hiddens = [after(v, grad_two) for v in hiddens]
+    grad_two = CubeSum(grad_two, low_rows).step()
+    gates, ups = [g[:, :part] for g in grads], [g[:, part:] for g in grads]
+    theirs = [
+        dot(cot_cube, hiddens[1], TN).astype(BF),
+        dot(cube_two, gates[1], TN).astype(BF),
+        dot(cube_two, ups[1], TN).astype(BF),
+    ]
+    came = [swap_mp(v) for v in theirs]
+    grad_two.step(*theirs)
+    down_back = (dot(cot_cube, hiddens[0], TN) + came[0].astype(F32)).astype(BF)
+    down_high = over_high_back(down_back)
+    gate_back = (dot(cube_two, gates[0], TN) + came[1].astype(F32)).astype(BF)
     gate_high = over_high_back(gate_back)
+    grad_two.step(down_back, gate_back)
+    up_back = (dot(cube_two, ups[0], TN) + came[2].astype(F32)).astype(BF)
     up_high = over_high_back(up_back)
-    kept = [after(v, grad_two) for v in hiddens]
-    grad_two, came = cube_scatter(grad_two, low_rows)
-    grad_two = after(grad_two, down_back, gate_back, up_back)
-    ffn = dot(kept[0], down_w[0], NT) + dot(kept[1], down_w[1], NT)
-    ffn = CubeBack(after(ffn.astype(BF), *came[2]), low_rows)
+    grad_two = after(grad_two.total(), up_back)
 
     def whole(own):
         other = swap_mp(own)
@@ -667,79 +658,87 @@
         for p in parts:
             p.value = after(p.value, *others)
 
-    ffn.step(1, grad_q)
+    def home(value, *others):
+        return trade(after(value, *others).reshape(8, slab, part), CUBE_AXES)
+
     out_sum = pair(out_grad)
-    out_sum[0].step(0, grad_q)
-    out_sum[1].step(1, grad_q)
+    out_sum[0].step(0)
+    out_sum[1].step(1)
     kv_sum = pair(grad_kv_all.reshape(blocks * rows, 2 * HD))
+    hold(kv_sum, out_sum[0].last, out_sum[1].last)
     kv_sum[0].step(0)
     kv_sum[1].step(1)
-    hold(out_sum, kv_sum[0].last, kv_sum[1].last)
+    hiddens = [after(v, kv_sum[0].last) for v in hiddens]
+    ffn = (dot(hiddens[0], down_w[0], NT) + dot(hiddens[1], down_w[1], NT)).astype(BF)
+    query_grad = dot(normed, after(grad_q, kv_sum[0].last), TN).astype(BF)
     kv_sum[0].step(1)
     kv_sum[1].step(0)
+    hold(out_sum, kv_sum[0].last, kv_sum[1].last)
     kv_sum = merge(kv_sum)
+    kv_sum.step(2)
+    hold(out_sum, kv_sum.last)
+    query_sum = pair(query_grad)
+    hold(query_sum, kv_sum.last)
     out_sum[0].step(1)
     out_sum[1].step(0)
-    out_sum = merge(out_sum)
-    query_sum = pair(dot(normed, grad_q, TN).astype(BF))
-    hold(query_sum, kv_sum.last)
-    hold([ffn], kv_sum.last)
     query_sum[0].step(0)
     query_sum[1].step(1)
-    ffn.step(0)
-    kv_sum.step(2)
-    out_sum.step(2)
-    hold([kv_sum], query_sum[0].last, query_sum[1].last, out_sum.last)
+    down_back = home(down_high, kv_sum.last)
+    ffn = CubeSum(ffn, low_rows)
     for bit in high[::-1]:
         kv_sum.step(bit)
-        out_sum.step(bit)
-    kv_mine = kv_sum.value
-    hold(query_sum, kv_sum.last)
-    hold([ffn], kv_sum.last)
+    out_sum = merge(out_sum)
+    hold([out_sum], kv_sum.last)
+    grad_k = rotate(kv_sum.value[:, :HD], cosine, -sine).astype(BF)
+    grad_v = kv_sum.value[:, HD:].astype(BF)
+    grad_kv = jnp.concatenate([grad_k, grad_v], axis=1)
+    last = Scatter(dot(normed, grad_kv, TN).astype(BF), bits)
+    last.step(1)
+    grad_normed = (dot(grad_q, w_q, NT) + dot(grad_kv, w_kv, NT)).astype(BF)
+    other_normed = swap_mp(grad_normed)
+    hold([last], other_normed, query_sum[0].last, query_sum[1].last)
+    last.step(0)
+    hold([out_sum], last.last)
+    hold(query_sum, last.last)
     query_sum[0].step(1)
     query_sum[1].step(0)
     query_sum = merge(query_sum)
-    ffn.step(2)
-    mixed = whole((middle + ffn.value).astype(BF))
-    grad_k = rotate(kv_mine[:, :HD], cosine, -sine).astype(BF)
-    grad_v = kv_mine[:, HD:].astype(BF)
-    grad_kv = jnp.concatenate([grad_k, grad_v], axis=1)
-    last = Scatter(dot(normed, grad_kv, TN).astype(BF), bits)
-    grad_normed = (dot(grad_q, w_q, NT) + dot(grad_kv, w_kv, NT)).astype(BF)
-    other_normed = swap_mp(grad_normed)
-    last.step(1)
+    last.step(2)
+    hold([out_sum], last.last)
+    hold([query_sum], last.last)
+    for bit in high[::-1]:
+        last.step(bit)
+    gate_back = home(gate_high, down_back, last.last)
+    out_sum.step(2)
+    query_sum.step(2)
     grad_normed = grad_normed.astype(F32) + other_normed.astype(F32)
     grad_input_norm, grad_gain_one = norm_back(grad_normed, inputs, inverse_one, gain_one)
+    grad_tokens = grad_middle + grad_input_norm
     bias_query = jnp.sum(grad_q.astype(F32), axis=0)
     bias_kv = jnp.sum(grad_kv.astype(F32), axis=0)
     gain_two_sum = grad_gain_two + swap_mp(grad_gain_two)
     small = jnp.concatenate([grad_gain_one, gain_two_sum, bias_query, bias_kv]).reshape(-1, 128)
-    hold([last], query_sum.last, other_normed)
-    last.step(0)
-    query_sum.step(2)
-    came = flip(small, 0)
+    came = flip(after(small, last.last), 0)
     small = small + came
-    hold([last], came)
-    last.step(2)
-    came = flip(small, 1)
+    hold([out_sum], query_sum.last, came)
+    hold([query_sum], out_sum.last, came)
+    ffn.step(last.last)
+    for bit in high[::-1]:
+        out_sum.step(bit)
+        query_sum.step(bit)
+    came = flip(after(small, out_sum.last, query_sum.last), 1)
     small = small + came
-    hold([last], came)
-    for bit in high[::-1]:
-        query_sum.step(bit)
-        last.step(bit)
-    for bit in range(2, bits):
+    up_back = home(up_high, gate_back, *ffn.came)
+    ffn.step(came)
+    small = small + flip(after(small, *ffn.came), 2)
+    for bit in high:
         small = small + flip(small, bit)
+    ffn.step()
+    mixed = whole((middle + ffn.total()).astype(BF))
     small = small.reshape(-1)
     out_part, query_part, kv_part = out_sum.value, query_sum.value, last.value
 
-    def home(value, *others):
-        return trade(after(value, *others).reshape(8, slab, part), CUBE_AXES)
-
-    down_back = home(down_high)
-    gate_back = home(gate_high, down_back)
-    up_back = home(up_high, gate_back)
     gate_part, up_part, down_part = unpack(gate_back, up_back, down_back, w_gate.shape[1])
-    grad_tokens = grad_middle + grad_input_norm
     gain_one_sum = small[:model]
     gain_two_sum = small[model : 2 * model]
     bias_query_sum = small[2 * model : 2 * model + width]
@@ -759,7 +758,7 @@
         gain_two_sum,
         gate_part,
         up_part,
-        down_part,
+        down_part.T,
     )
 
 

time: 636 us -> 608 us (0.956)
  waiting for transfers between devices: 302 us -> 262 us
  starting transfers between devices: 113 us -> 128 us
    all_gather x1, waiting for transfers between devices: 40 us -> 0.01 us  [shards(): lax.all_gather(both_cube.reshape(8 * slab, -1), 'h', axis=0, tiled=True)]
    ppermute x70 -> x76, starting transfers between devices: 90.2 us -> 103 us  [flip(): lax.ppermute(value, axis, [(i, i ^ mask) for i in range(lax.axis_size(axi...]
    all_to_all x5, waiting for transfers between devices: 24.5 us -> 14.8 us  [trade(): return lax.all_to_all(value, axes, dim, dim, tiled=True)]
    unnamed x167 -> x222, local copies, waits for them, and re-layouts: 31.2 us -> 23.5 us
    select_n x27, other arithmetic: 12.4 us -> 19.9 us  [step(): jnp.where(mine(bit) == 0, jnp.stack([self.value, other], at), jnp.stack([...]
    ppermute x70 -> x76, waiting for transfers between devices: 237 us -> 245 us  [flip(): lax.ppermute(value, axis, [(i, i ^ mask) for i in range(lax.axis_size(axi...]
    convert_element_type x20 -> x18, other arithmetic: 8.37 us -> 1.86 us  [step(): self.value = self.value.astype(BF)]
    dot_general x19 -> x21, matrix products: 70 us -> 73.2 us  [dot(): return lax.dot_general(left, right, dims, preferred_element_type=F32)]
  transfers between devices with their start and end apart: 90 -> 97, of which waited for: 43 -> 47; matrix products, arithmetic and copies ran while one was open for 24% -> 25% of each run, Pallas kernels for 2% -> 2%
where the time goes in v3:
time: 608 us; the launch traced here: 600 us
  waiting for transfers between devices  262 us (43%)
  starting transfers between devices  128 us (21%)
  matrix products  73.2 us (12%)
  other arithmetic  61.9 us (10%)
  local copies, waits for them, and re-layouts  39.4 us (6%)
  between operations  20.5 us (3%)
  Pallas kernels  14.6 us (2%)
    ppermute x76, waiting for transfers between devices, flip(): lax.ppermute(value, axis, [(i, i ^ mask) for i in range(lax.axis_size(axi...  245 us
    ppermute x76, starting transfers between devices, flip(): lax.ppermute(value, axis, [(i, i ^ mask) for i in range(lax.axis_size(axi...  103 us
    dot_general x21, matrix products, dot(): return lax.dot_general(left, right, dims, preferred_element_type=F32)  73.2 us
    unnamed x222, local copies, waits for them, and re-layouts  23.5 us
    all_to_all x5, starting transfers between devices, trade(): return lax.all_to_all(value, axes, dim, dim, tiled=True)  22.4 us
    select_n x27, other arithmetic, step(): jnp.where(mine(bit) == 0, jnp.stack([self.value, other], at), jnp.stack([...  19.9 us
    all_to_all x5, waiting for transfers between devices, trade(): return lax.all_to_all(value, axes, dim, dim, tiled=True)  14.8 us
  transfers between devices with their start and end apart: 97, of which 47 were waited for; matrix products, arithmetic and copies ran while one was open for 25% of the time, Pallas kernels for 2%

profile of v3, /device:TPU:0, one launch (start us, length us, event | category | flops | bytes accessed | tf_op | source)
XLA Modules:
  0.0 599.8 jit_solution(5140848686357767123)
XLA Ops:
  41.2 10.8 %all-to-all-done = bf16[8,96,1280]{2,1,0:T(8,128)(2,1)} async-done(((bf16[8,96,1280]{2,1,0:T(8,128)(2,1)}), bf16[8,96,1280]{2,1,0:T(8,128)(2,1)}, u32[]{:S(2)}, u32[]{:S(2)}) %all-to-all-start) | async-done | bytes 1966112 | tf_op jit(solution)/shard_map/all_to_all | solution.py:48
  54.7 6.4 %all-to-all-start.1 = ((bf16[8,96,640]{2,1,0:T(8,128)(2,1)}), bf16[8,96,640]{2,1,0:T(8,128)(2,1)S(1)}, u32[]{:S(2)}, u32[]{:S(2)}) async-start(bf16[8,96,640]{2,1,0:T(8,128)(2,1)} %get-tuple-element.116), calls=%async_computation.1 | async-start | bytes 1966080 | tf_op jit(solution)/shard_map/all_to_all | solution.py:48
  66.5 13.3 %collective-permute-done.8 = bf16[2,2,96,256]{3,2,0,1:T(8,128)(2,1)S(1)} collective-permute-done((bf16[2,2,96,256]{3,2,0,1:T(8,128)(2,1)S(1)}, bf16[2,2,96,256]{3,2,0,1:T(8,128)(2,1)S(1)}, u32[]{:S(2)}, u32[]{:S(2)}) %collective-permute-start.8) | collective-permute-done | bytes 196640 | tf_op jit(solution)/shard_map/ppermute | solution.py:31
  86.0 5.9 collective-permute-done.9
  100.1 23.9 %collective-permute-done.10 = bf16[256,256]{1,0:T(8,128)(2,1)S(1)} collective-permute-done((bf16[256,256]{1,0:T(8,128)(2,1)S(1)}, bf16[256,256]{1,0:T(8,128)(2,1)S(1)}, u32[]{:S(2)}, u32[]{:S(2)}) %collective-permute-start.10) | collective-permute-done | bytes 131104 | tf_op jit(solution)/shard_map/ppermute | solution.py:31
  124.8 10.9 %collective-permute-done.12 = bf16[2,96,768]{2,1,0:T(8,128)(2,1)S(1)} collective-permute-done((bf16[2,96,768]{2,1,0:T(8,128)(2,1)S(1)}, bf16[2,96,768]{2,1,0:T(8,128)(2,1)S(1)}, u32[]{:S(2)}, u32[]{:S(2)}) %collective-permute-start.12) | collective-permute-done | bytes 294944 | tf_op jit(solution)/shard_map/ppermute | solution.py:31
  142.5 5.9 collective-permute-done.15
  180.9 17.4 %collective-permute-done.22 = bf16[2,2,2,96,768]{4,3,2,1,0:T(8,128)(2,1)} collective-permute-done((bf16[2,2,2,96,768]{4,3,2,1,0:T(8,128)(2,1)}, bf16[2,2,2,96,768]{4,3,2,1,0:T(8,128)(2,1)}, u32[]{:S(2)}, u32[]{:S(2)}) %collective-permute-start.22) | collective-permute-done | bytes 1179680 | tf_op jit(solution)/shard_map/ppermute | solution.py:31
  214.8 16.9 %collective-permute-done.26 = bf16[40,1536]{1,0:T(8,128)(2,1)S(1)} collective-permute-done((bf16[40,1536]{1,0:T(8,128)(2,1)S(1)}, bf16[40,1536]{1,0:T(8,128)(2,1)S(1)}, u32[]{:S(2)}, u32[]{:S(2)}) %collective-permute-start.26) | collective-permute-done | bytes 122912 | tf_op jit(solution)/shard_map/ppermute | solution.py:31
  234.9 6.0 %collective-permute-done.28 = bf16[80,1536]{1,0:T(8,128)(2,1)S(1)} collective-permute-done((bf16[80,1536]{1,0:T(8,128)(2,1)S(1)}, bf16[80,1536]{1,0:T(8,128)(2,1)S(1)}, u32[]{:S(2)}, u32[]{:S(2)}) %collective-permute-start.28) | collective-permute-done | bytes 245792 | tf_op jit(solution)/shard_map/ppermute | solution.py:31
  247.0 7.5 %collective-permute-done.31 = bf16[160,1536]{1,0:T(8,128)(2,1)S(1)} collective-permute-done((bf16[160,1536]{1,0:T(8,128)(2,1)S(1)}, bf16[160,1536]{1,0:T(8,128)(2,1)S(1)}, u32[]{:S(2)}, u32[]{:S(2)}) %collective-permute-start.31) | collective-permute-done | bytes 491552 | tf_op jit(solution)/shard_map/ppermute | solution.py:31
  269.5 7.4 %fusion.91 = f32[1024,1280]{1,0:T(8,128)S(1)} fusion(bf16[1024,1536]{1,0:T(8,128)(2,1)} %constant_dynamic-update-slice_fusion.2, bf16[1536,1280]{1,0:T(8,128)(2,1)} %all-gather.3.cloned.1.call-done), kind=kOutput, calls=%fused_computation.334 | convolution fusion | flops 4026531840 | bytes 12320768 | tf_op jit(solution)/shard_map/dot_general | solution.py:213
  280.3 6.7 %fusion.78 = f32[1024,1536]{1,0:T(8,128)} fusion(bf16[1536,1280]{1,0:T(8,128)(2,1)S(1)} %copy-done.83, bf16[1024,640]{1,0:T(8,128)(2,1)S(1)} %get-tuple-element.215, bf16[1024,640]{1,0:T(8,128)(2,1)S(1)} %get-tuple-element.214), kind=kOutput, calls=%fused_computation.322 | convolution fusion | flops 4031774720 | bytes 12845056 | tf_op jit(solution)/shard_map/dot_general | solution.py:213
  287.0 6.3 %fusion.92 = f32[1024,1280]{1,0:T(8,128)S(1)} fusion(bf16[1024,1536]{1,0:T(8,128)(2,1)S(1)} %copy-done.71, bf16[1536,1280]{1,0:T(8,128)(2,1)} %collective-permute-done.34), kind=kOutput, calls=%fused_computation.335 | convolution fusion | flops 4026531840 | bytes 12320768 | tf_op jit(solution)/shard_map/dot_general | solution.py:213
  296.6 9.0 %add_convert_fusion.1 = bf16[1024,1536]{1,0:T(8,128)(2,1)S(1)} fusion(f32[1024,1536]{1,0:T(8,128)} %fusion.78, bf16[1536,1280]{1,0:T(8,128)(2,1)} %collective-permute-done.34, bf16[1024,640]{1,0:T(8,128)(2,1)S(1)} %get-tuple-element.213, bf16[1024,640]{1,0:T(8,128)(2,1)S(1)} %get-tuple-element.212), kind=kOutput, calls=%fused_computation.1 | convolution fusion | flops 4034920448 | bytes 15990784 | tf_op jit(solution)/shard_map/dot_general | solution.py:213
  333.6 10.0 %collective-permute-done.39 = bf16[80,1536]{1,0:T(8,128)(2,1)S(1)} collective-permute-done((bf16[80,1536]{1,0:T(8,128)(2,1)S(1)}, bf16[80,1536]{1,0:T(8,128)(2,1)S(1)}, u32[]{:S(2)}, u32[]{:S(2)}) %collective-permute-start.39) | collective-permute-done | bytes 245792 | tf_op jit(solution)/shard_map/ppermute | solution.py:31
  356.1 6.9 %add_convert_fusion.2 = bf16[1536,640]{1,0:T(8,128)(2,1)} fusion(bf16[1536,640]{1,0:T(8,128)(2,1)} %collective-permute-done.46, bf16[1024,1536]{1,0:T(8,128)(2,1)} %constant_dynamic-update-slice_fusion.2, bf16[1024,1280]{1,0:T(8,128)(2,1)} %copy-done.26), kind=kOutput, calls=%fused_computation.2 | convolution fusion | flops 2016215040 | bytes 8388608 | tf_op jit(solution)/shard_map/dot_general | solution.py:213
  363.0 6.0 %collective-permute-done.45 = bf16[40,1536]{1,0:T(8,128)(2,1)} collective-permute-done((bf16[40,1536]{1,0:T(8,128)(2,1)S(1)}, bf16[40,1536]{1,0:T(8,128)(2,1)}, u32[]{:S(2)}, u32[]{:S(2)}) %collective-permute-start.45) | collective-permute-done | bytes 122912 | tf_op jit(solution)/shard_map/ppermute | solution.py:31
  400.7 8.8 %collective-permute-done.50 = bf16[2,2,2,256,128]{4,3,0,1,2:T(8,128)(2,1)S(1)} collective-permute-done((bf16[2,2,2,256,128]{4,3,0,1,2:T(8,128)(2,1)S(1)}, bf16[2,2,2,256,128]{4,3,0,1,2:T(8,128)(2,1)S(1)}, u32[]{:S(2)}, u32[]{:S(2)}) %collective-permute-start.50) | collective-permute-done | bytes 524320 | tf_op jit(solution)/shard_map/ppermute | solution.py:31
  431.7 13.4 %collective-permute-start.55 = (bf16[256,256]{1,0:T(8,128)(2,1)S(1)}, bf16[256,256]{1,0:T(8,128)(2,1)S(1)}, u32[]{:S(2)}, u32[]{:S(2)}) collective-permute-start(bf16[256,256]{1,0:T(8,128)(2,1)S(1)} %dynamic-slice_bitcast_fusion.13), channel_id=1, source_target_pairs={{0,16},{16,0},{1,17},{17,1},{2,18},{18,2},{3,19},{19,3},{4,20},{20... | collective-permute-start | bytes 393224 | tf_op jit(solution)/shard_map/ppermute | solution.py:31
  447.6 18.7 %collective-permute-done.55 = bf16[256,256]{1,0:T(8,128)(2,1)S(1)} collective-permute-done((bf16[256,256]{1,0:T(8,128)(2,1)S(1)}, bf16[256,256]{1,0:T(8,128)(2,1)S(1)}, u32[]{:S(2)}, u32[]{:S(2)}) %collective-permute-start.55) | collective-permute-done | bytes 131104 | tf_op jit(solution)/shard_map/ppermute | solution.py:31
  469.8 6.4 %collective-permute-done.68 = bf16[2,2,96,384]{3,2,0,1:T(8,128)(2,1)S(1)} collective-permute-done((bf16[2,2,96,384]{3,2,0,1:T(8,128)(2,1)S(1)}, bf16[2,2,96,384]{3,2,0,1:T(8,128)(2,1)S(1)}, u32[]{:S(2)}, u32[]{:S(2)}) %collective-permute-start.68) | collective-permute-done | bytes 294944 | tf_op jit(solution)/shard_map/ppermute | solution.py:31
  476.4 6.7 %collective-permute-done.56 = bf16[2,2,2,96,256]{4,3,0,1,2:T(8,128)(2,1)S(1)} collective-permute-done((bf16[2,2,2,96,256]{4,3,0,1,2:T(8,128)(2,1)S(1)}, bf16[2,2,2,96,256]{4,3,0,1,2:T(8,128)(2,1)S(1)}, u32[]{:S(2)}, u32[]{:S(2)}) %collective-permute-start.56) | collective-permute-done | bytes 393248 | tf_op jit(solution)/shard_map/ppermute | solution.py:31
  510.1 11.5 %collective-permute-done.73 = bf16[2,96,768]{2,1,0:T(8,128)(2,1)S(1)} collective-permute-done((bf16[2,96,768]{2,1,0:T(8,128)(2,1)S(1)}, bf16[2,96,768]{2,1,0:T(8,128)(2,1)S(1)}, u32[]{:S(2)}, u32[]{:S(2)}) %collective-permute-start.73) | collective-permute-done | bytes 294944 | tf_op jit(solution)/shard_map/ppermute | solution.py:31
  (610 shorter events, 336.5 us)
Async XLA Ops:
  20.6 31.4 %all-to-all-start = ((bf16[8,96,1280]{2,1,0:T(8,128)(2,1)}), bf16[8,96,1280]{2,1,0:T(8,128)(2,1)}, u32[]{:S(2)}, u32[]{:S(2)}) async-start(bf16[8,96,1280]{2,1,0:T(8,128)(2,1)} %get-tuple-element.112), calls=%async_computation | async-start | bytes 3932160 | tf_op jit(solution)/shard_map/all_to_all | solution.py:48
  25.1 28.9 %collective-permute-start.11 = (bf16[96,768]{1,0:T(8,128)(2,1)S(1)}, bf16[96,768]{1,0:T(8,128)(2,1)S(1)}, u32[]{:S(2)}, u32[]{:S(2)}) collective-permute-start(bf16[96,768]{1,0:T(8,128)(2,1)S(1)} %bitcast.454), channel_id=1, source_target_pairs={{0,16},{16,0},{1,17},{17,1},{2,18},{18,2},{3,19},{19,3},{4,20},{20... | collective-permute-start | bytes 442376 | tf_op jit(solution)/shard_map/ppermute | solution.py:31
  28.9 51.0 %collective-permute-start.13 = (bf16[128,1536]{1,0:T(8,128)(2,1)}, bf16[128,1536]{1,0:T(8,128)(2,1)}, u32[]{:S(2)}, u32[]{:S(2)}) collective-permute-start(bf16[128,1536]{1,0:T(8,128)(2,1)} %dynamic-slice_bitcast_fusion.1), channel_id=1, source_target_pairs={{0,4},{4,0},{1,5},{5,1},{2,6},{6,2},{3,7},{7,3},{8,12},{12,8},{9,1... | collective-permute-start | bytes 1179656 | tf_op jit(solution)/shard_map/ppermute | solution.py:31
  54.7 82.5 %all-to-all-start.1 = ((bf16[8,96,640]{2,1,0:T(8,128)(2,1)}), bf16[8,96,640]{2,1,0:T(8,128)(2,1)S(1)}, u32[]{:S(2)}, u32[]{:S(2)}) async-start(bf16[8,96,640]{2,1,0:T(8,128)(2,1)} %get-tuple-element.116), calls=%async_computation.1 | async-start | bytes 1966080 | tf_op jit(solution)/shard_map/all_to_all | solution.py:48
  61.2 195.3 %all-gather.3.cloned.1.call-start = ((), (), s32[]{:S(2)}) async-start(), calls=%async_computation.8 | async-start | bytes 5898240 | tf_op jit(solution)/shard_map/all_gather | solution.py:524
  61.9 202.2 %all-gather.5.cloned.1.call-start = ((), (), s32[]{:S(2)}) async-start(), calls=%async_computation.9 | async-start | bytes 2949120 | tf_op jit(solution)/shard_map/all_gather | solution.py:525
  83.2 54.1 %collective-permute-start.14 = (bf16[256,1536]{1,0:T(8,128)(2,1)S(1)}, bf16[256,1536]{1,0:T(8,128)(2,1)}, u32[]{:S(2)}, u32[]{:S(2)}) collective-permute-start(bf16[256,1536]{1,0:T(8,128)(2,1)S(1)} %pad_maximum_fusion.6), channel_id=1, source_target_pairs={{0,8},{8,0},{1,9},{9,1},{2,10},{10,2},{3,11},{11,3},{4,12},{12,4},... | collective-permute-start | bytes 2359304 | tf_op jit(solution)/shard_map/ppermute | solution.py:31
  84.7 76.6 %collective-permute-start.6 = (bf16[2,2,2,96,384]{4,3,0,1,2:T(8,128)(2,1)}, bf16[2,2,2,96,384]{4,3,0,1,2:T(8,128)(2,1)}, u32[]{:S(2)}, u32[]{:S(2)}) collective-permute-start(bf16[2,2,2,96,384]{4,3,0,1,2:T(8,128)(2,1)} %maximum_select_fusion.14), channel_id=1, source_target_pairs={{0,2},{2,0},{1,3},{3,1},{4,6},{6,4},{5,7},{7,5},{8,10},{10,8},{9,1... | collective-permute-start | bytes 1769480 | tf_op jit(solution)/shard_map/ppermute | solution.py:31
  92.6 31.5 %collective-permute-start.10 = (bf16[256,256]{1,0:T(8,128)(2,1)S(1)}, bf16[256,256]{1,0:T(8,128)(2,1)S(1)}, u32[]{:S(2)}, u32[]{:S(2)}) collective-permute-start(bf16[256,256]{1,0:T(8,128)(2,1)S(1)} %shard_map.265), channel_id=1, source_target_pairs={{0,16},{16,0},{1,17},{17,1},{2,18},{18,2},{3,19},{19,3},{4,20},{20... | collective-permute-start | bytes 393224 | tf_op jit(solution)/shard_map/ppermute | solution.py:31
  94.5 41.2 %collective-permute-start.12 = (bf16[2,96,768]{2,1,0:T(8,128)(2,1)S(1)}, bf16[2,96,768]{2,1,0:T(8,128)(2,1)S(1)}, u32[]{:S(2)}, u32[]{:S(2)}) collective-permute-start(bf16[2,96,768]{2,1,0:T(8,128)(2,1)S(1)} %copy-done.25), channel_id=1, source_target_pairs={{0,8},{8,0},{1,9},{9,1},{2,10},{10,2},{3,11},{11,3},{4,12},{12,4},... | collective-permute-start | bytes 884744 | tf_op jit(solution)/shard_map/ppermute | solution.py:31
  99.2 63.7 %collective-permute-start.4 = (bf16[2,2,2,96,384]{4,3,0,1,2:T(8,128)(2,1)}, bf16[2,2,2,96,384]{4,3,0,1,2:T(8,128)(2,1)}, u32[]{:S(2)}, u32[]{:S(2)}) collective-permute-start(bf16[2,2,2,96,384]{4,3,0,1,2:T(8,128)(2,1)} %maximum_select_fusion.12), channel_id=1, source_target_pairs={{0,4},{4,0},{1,5},{5,1},{2,6},{6,2},{3,7},{7,3},{8,12},{12,8},{9,1... | collective-permute-start | bytes 1769480 | tf_op jit(solution)/shard_map/ppermute | solution.py:31
  170.0 33.7 %collective-permute-start.21 = (bf16[512,1536]{1,0:T(8,128)(2,1)}, bf16[512,1536]{1,0:T(8,128)(2,1)}, u32[]{:S(2)}, u32[]{:S(2)}) collective-permute-start(bf16[512,1536]{1,0:T(8,128)(2,1)} %pad_maximum_fusion.5), channel_id=1, source_target_pairs={{0,2},{2,0},{1,3},{3,1},{4,6},{6,4},{5,7},{7,5},{8,10},{10,8},{9,1... | collective-permute-start | bytes 4718600 | tf_op jit(solution)/shard_map/ppermute | solution.py:31
  176.1 348.7 %reduce-scatter.6.cloned.1.call-start = ((), (), s32[]{:S(2)}) async-start(), calls=%async_computation.11 | async-start | bytes 2949120 | tf_op jit(solution)/shard_map/reduce_scatter | solution.py:595
  256.5 30.5 %collective-permute-start.34 = (bf16[1536,1280]{1,0:T(8,128)(2,1)}, bf16[1536,1280]{1,0:T(8,128)(2,1)}, u32[]{:S(2)}, u32[]{:S(2)}) collective-permute-start(bf16[1536,1280]{1,0:T(8,128)(2,1)} %all-gather.3.cloned.1.call-done), channel_id=1, source_target_pairs={{0,1},{1,0},{2,3},{3,2},{4,5},{5,4},{6,7},{7,6},{8,9},{9,8},{10,11... | collective-permute-start | bytes 11796488 | tf_op jit(solution)/shard_map/ppermute | solution.py:40
  264.2 29.2 %collective-permute-start.33 = (bf16[1536,640]{1,0:T(8,128)(2,1)}, bf16[1536,640]{1,0:T(8,128)(2,1)S(1)}, u32[]{:S(2)}, u32[]{:S(2)}) collective-permute-start(bf16[1536,640]{1,0:T(8,128)(2,1)} %all-gather.5.cloned.1.call-done), channel_id=1, source_target_pairs={{0,1},{1,0},{2,3},{3,2},{4,5},{5,4},{6,7},{7,6},{8,9},{9,8},{10,11... | collective-permute-start | bytes 5898248 | tf_op jit(solution)/shard_map/ppermute | solution.py:40
  317.3 230.1 %reduce-scatter.4.cloned.1.call-start = ((), (), s32[]{:S(2)}) async-start(), calls=%async_computation.10 | async-start | bytes 2949120 | tf_op jit(solution)/shard_map/reduce_scatter | solution.py:595
  326.8 29.3 %collective-permute-start.46 = (bf16[1536,640]{1,0:T(8,128)(2,1)}, bf16[1536,640]{1,0:T(8,128)(2,1)}, u32[]{:S(2)}, u32[]{:S(2)}) collective-permute-start(bf16[1536,640]{1,0:T(8,128)(2,1)} %convolution_convert_fusion.2), channel_id=1, source_target_pairs={{0,1},{1,0},{2,3},{3,2},{4,5},{5,4},{6,7},{7,6},{8,9},{9,8},{10,11... | collective-permute-start | bytes 5898248 | tf_op jit(solution)/shard_map/ppermute | solution.py:40
  348.9 227.4 %reduce-scatter.8.cloned.1.call-start = ((), (), s32[]{:S(2)}) async-start(), calls=%async_computation.12 | async-start | bytes 2949120 | tf_op jit(solution)/shard_map/reduce_scatter | solution.py:595
  374.2 110.4 %collective-permute-start.84 = (f32[128,1536]{1,0:T(8,128)}, f32[128,1536]{1,0:T(8,128)S(1)}, u32[]{:S(2)}, u32[]{:S(2)}) collective-permute-start(f32[128,1536]{1,0:T(8,128)} %get-tuple-element.209), channel_id=1, source_target_pairs={{0,1},{1,0},{2,3},{3,2},{4,5},{5,4},{6,7},{7,6},{8,9},{9,8},{10,11... | collective-permute-start | bytes 2359304 | tf_op jit(solution)/shard_map/ppermute | solution.py:40
  431.7 34.6 %collective-permute-start.55 = (bf16[256,256]{1,0:T(8,128)(2,1)S(1)}, bf16[256,256]{1,0:T(8,128)(2,1)S(1)}, u32[]{:S(2)}, u32[]{:S(2)}) collective-permute-start(bf16[256,256]{1,0:T(8,128)(2,1)S(1)} %dynamic-slice_bitcast_fusion.13), channel_id=1, source_target_pairs={{0,16},{16,0},{1,17},{17,1},{2,18},{18,2},{3,19},{19,3},{4,20},{20... | collective-permute-start | bytes 393224 | tf_op jit(solution)/shard_map/ppermute | solution.py:31
  445.2 38.3 %collective-permute-start.58 = (bf16[2,2,2,96,384]{4,3,0,1,2:T(8,128)(2,1)S(1)}, bf16[2,2,2,96,384]{4,3,0,1,2:T(8,128)(2,1)S(1)}, u32[]{:S(2)}, u32[]{:S(2)}) collective-permute-start(bf16[2,2,2,96,384]{4,3,0,1,2:T(8,128)(2,1)S(1)} %copy_bitcast_fusion.3), channel_id=1, source_target_pairs={{0,2},{2,0},{1,3},{3,1},{4,6},{6,4},{5,7},{7,5},{8,10},{10,8},{9,1... | collective-permute-start | bytes 1769480 | tf_op jit(solution)/shard_map/ppermute | solution.py:31
  445.4 37.9 %collective-permute-start.59 = (bf16[2,2,2,96,384]{4,3,0,1,2:T(8,128)(2,1)S(1)}, bf16[2,2,2,96,384]{4,3,0,1,2:T(8,128)(2,1)S(1)}, u32[]{:S(2)}, u32[]{:S(2)}) collective-permute-start(bf16[2,2,2,96,384]{4,3,0,1,2:T(8,128)(2,1)S(1)} %copy_bitcast_fusion.2), channel_id=1, source_target_pairs={{0,4},{4,0},{1,5},{5,1},{2,6},{6,2},{3,7},{7,3},{8,12},{12,8},{9,1... | collective-permute-start | bytes 1769480 | tf_op jit(solution)/shard_map/ppermute | solution.py:31
  500.8 27.6 %collective-permute-start.63 = (bf16[192,1536]{1,0:T(8,128)(2,1)S(1)}, bf16[192,1536]{1,0:T(8,128)(2,1)S(1)}, u32[]{:S(2)}, u32[]{:S(2)}) collective-permute-start(bf16[192,1536]{1,0:T(8,128)(2,1)S(1)} %slice.450), channel_id=1, source_target_pairs={{0,8},{8,0},{1,9},{9,1},{2,10},{10,2},{3,11},{11,3},{4,12},{12,4},... | collective-permute-start | bytes 1769480 | tf_op jit(solution)/shard_map/ppermute | solution.py:31
  548.2 28.1 %all-to-all-start.3 = ((bf16[8,96,640]{2,1,0:T(8,128)(2,1)}), bf16[8,96,640]{2,1,0:T(8,128)(2,1)S(1)}, u32[]{:S(2)}, u32[]{:S(2)}) async-start(bf16[8,96,640]{2,1,0:T(8,128)(2,1)} %bitcast.436), calls=%async_computation.5 | async-start | bytes 1966080 | tf_op jit(solution)/shard_map/all_to_all | solution.py:48
  (167 other events, 1929.5 us)
Sparse Core Ops, SparseCore 0:
  63.6 103.7 all-gather.2
  176.2 53.1 all-gather.4
  317.5 50.2 reduce-scatter.5
  370.0 51.3 reduce-scatter.3
  423.5 57.0 reduce-scatter.7

commit v4 on v3

--- a/solution.py
+++ b/solution.py
@@ -213,12 +213,6 @@
     return lax.dot_general(left, right, dims, preferred_element_type=F32)
 
 
-def own_mask(rows):
-    return lax.broadcasted_iota(jnp.int32, (rows, rows), 0) >= lax.broadcasted_iota(
-        jnp.int32, (rows, rows), 1
-    )
-
-
 def attend_kernel(vis, q_ref, kv_ref, o_ref, low_ref, lse_ref, acc, top, tot):
     rows, width = q_ref.shape
     heads = width // HD
@@ -227,25 +221,26 @@
 
     def block(place, first):
         key = kv_ref[place, :, :HD]
-        value = kv_ref[place, :, HD:]
+        value = kv_ref[place, :, HD:].astype(F32).T.astype(BF)
         if first:
-            mask = own_mask(rows)
+            mask = lax.broadcasted_iota(jnp.int32, (rows, rows), 0) <= lax.broadcasted_iota(
+                jnp.int32, (rows, rows), 1
+            )
         for h in range(heads):
-            cols = slice(h * HD, (h + 1) * HD)
-            scores = dot(q_ref[:, cols], key, NT) * factor
+            scores = dot(key, q_ref[:, h * HD : (h + 1) * HD], NT) * factor
             if first:
                 scores = jnp.where(mask, scores, BIG)
-                best = jnp.max(scores, axis=1, keepdims=True)
+                best = jnp.max(scores, axis=0, keepdims=True)
                 weights = jnp.exp2(scores - best)
-                tot[h] = jnp.sum(weights, axis=1, keepdims=True)
-                acc[:, cols] = dot(weights.astype(BF), value)
+                tot[h] = jnp.sum(weights, axis=0, keepdims=True)
+                acc[h] = dot(value, weights.astype(BF))
             else:
                 old = top[h]
-                best = jnp.maximum(old, jnp.max(scores, axis=1, keepdims=True))
+                best = jnp.maximum(old, jnp.max(scores, axis=0, keepdims=True))
                 weights = jnp.exp2(scores - best)
                 scale = jnp.exp2(old - best)
-                tot[h] = tot[h] * scale + jnp.sum(weights, axis=1, keepdims=True)
-                acc[:, cols] = acc[:, cols] * scale + dot(weights.astype(BF), value)
+                tot[h] = tot[h] * scale + jnp.sum(weights, axis=0, keepdims=True)
+                acc[h] = acc[h] * scale + dot(value, weights.astype(BF))
             top[h] = best
 
     block(vis[blocks], True)
@@ -261,10 +256,10 @@
     for h in range(heads):
         cols = slice(h * HD, (h + 1) * HD)
         total = tot[h]
-        out = acc[:, cols] / total
+        out = (acc[h] / total).T
         o_ref[:, cols] = out
         low_ref[:, cols] = out.astype(BF)
-        lse_ref[:, cols] = jnp.broadcast_to(top[h] + jnp.log(total) * LOG2E, (rows, HD))
+        lse_ref[h] = top[h] + jnp.log(total) * LOG2E
 
 
 def attend(vis, query, keyval):
@@ -277,14 +272,14 @@
         out_shape=(
             jax.ShapeDtypeStruct((rows, width), F32),
             jax.ShapeDtypeStruct((rows, width), BF),
-            jax.ShapeDtypeStruct((rows, width), F32),
+            jax.ShapeDtypeStruct((heads, 1, rows), F32),
         ),
         in_specs=[smem, vmem, vmem],
         out_specs=(vmem, vmem, vmem),
         scratch_shapes=[
-            pltpu.VMEM((rows, width), F32),
-            pltpu.VMEM((heads, rows, 1), F32),
-            pltpu.VMEM((heads, rows, 1), F32),
+            pltpu.VMEM((heads, HD, rows), F32),
+            pltpu.VMEM((heads, 1, rows), F32),
+            pltpu.VMEM((heads, 1, rows), F32),
         ],
         compiler_params=pltpu.CompilerParams(vmem_limit_bytes=40 * 2**20),
         cost_estimate=pl.CostEstimate(
@@ -302,29 +297,30 @@
     scale = HD ** (-0.5)
     for h in range(heads):
         cols = slice(h * HD, (h + 1) * HD)
-        delta[h] = jnp.sum(do_ref[:, cols].astype(F32) * o_ref[:, cols], axis=1, keepdims=True)
+        product = (do_ref[:, cols].astype(F32) * o_ref[:, cols]).T
+        delta[h] = jnp.sum(product, axis=0, keepdims=True)
 
     def block(place, first):
         key = kv_ref[place, :, :HD]
         value = kv_ref[place, :, HD:]
         if first:
-            mask = own_mask(rows)
+            mask = lax.broadcasted_iota(jnp.int32, (rows, rows), 0) <= lax.broadcasted_iota(
+                jnp.int32, (rows, rows), 1
+            )
         dk = jnp.zeros((rows, HD), F32)
         dv = jnp.zeros((rows, HD), F32)
         for h in range(heads):
             cols = slice(h * HD, (h + 1) * HD)
             query = q_ref[:, cols]
             grad = do_ref[:, cols]
-            probs = jnp.exp2(
-                dot(query, key, NT) * (scale * LOG2E) - lse_ref[:, h * HD : h * HD + 1]
-            )
+            probs = jnp.exp2(dot(key, query, NT) * (scale * LOG2E) - lse_ref[h])
             if first:
                 probs = jnp.where(mask, probs, 0.0)
-            dv = dv + dot(probs.astype(BF), grad, TN)
-            dprobs = dot(grad, value, NT)
+            dv = dv + dot(probs.astype(BF), grad)
+            dprobs = dot(value, grad, NT)
             dscores = (probs * (dprobs - delta[h])).astype(BF)
-            dk = dk + dot(dscores, query, TN)
-            dq = dot(dscores, key) * scale
+            dk = dk + dot(dscores, query)
+            dq = dot(dscores, key, TN) * scale
             if first:
                 dq_ref[:, cols] = dq
             else:
@@ -366,7 +362,7 @@
         out_specs=(vmem, vmem),
         scratch_shapes=[
             pltpu.VMEM((rows, width), F32),
-            pltpu.VMEM((heads, rows, 1), F32),
+            pltpu.VMEM((heads, 1, rows), F32),
         ],
         compiler_params=pltpu.CompilerParams(vmem_limit_bytes=48 * 2**20),
         cost_estimate=pl.CostEstimate(

time: 608 us -> 604 us (level)
  waiting for transfers between devices: 262 us -> 247 us
  starting transfers between devices: 128 us -> 136 us
    ppermute x76, waiting for transfers between devices: 245 us -> 229 us  [flip(): lax.ppermute(value, axis, [(i, i ^ mask) for i in range(lax.axis_size(axi...]
    ppermute x76, starting transfers between devices: 103 us -> 110 us  [flip(): lax.ppermute(value, axis, [(i, i ^ mask) for i in range(lax.axis_size(axi...]
    unnamed x222 -> x218, local copies, waits for them, and re-layouts: 23.5 us -> 23.5 us
  transfers between devices with their start and end apart: 97 -> 97, of which waited for: 47 -> 46; matrix products, arithmetic and copies ran while one was open for 25% -> 25% of each run, Pallas kernels for 2% -> 2%
where the time goes in v4:
time: 604 us; the launch traced here: 594 us
  waiting for transfers between devices  247 us (41%)
  starting transfers between devices  136 us (23%)
  matrix products  73.1 us (12%)
  other arithmetic  63.7 us (11%)
  local copies, waits for them, and re-layouts  39.3 us (7%)
  between operations  20.5 us (3%)
  Pallas kernels  14.6 us (2%)
    ppermute x76, waiting for transfers between devices, flip(): lax.ppermute(value, axis, [(i, i ^ mask) for i in range(lax.axis_size(axi...  229 us
    ppermute x76, starting transfers between devices, flip(): lax.ppermute(value, axis, [(i, i ^ mask) for i in range(lax.axis_size(axi...  110 us
    dot_general x21, matrix products, dot(): return lax.dot_general(left, right, dims, preferred_element_type=F32)  73.1 us
    all_to_all x5, starting transfers between devices, trade(): return lax.all_to_all(value, axes, dim, dim, tiled=True)  24.2 us
    unnamed x218, local copies, waits for them, and re-layouts  23.5 us
    select_n x27, other arithmetic, step(): jnp.where(mine(bit) == 0, jnp.stack([self.value, other], at), jnp.stack([...  20.4 us
    all_to_all x5, waiting for transfers between devices, trade(): return lax.all_to_all(value, axes, dim, dim, tiled=True)  15.1 us
  transfers between devices with their start and end apart: 97, of which 46 were waited for; matrix products, arithmetic and copies ran while one was open for 25% of the time, Pallas kernels for 2%

profile of v4, /device:TPU:0, one launch (start us, length us, event | category | flops | bytes accessed | tf_op | source)
XLA Modules:
  0.0 594.4 jit_solution(7818329250554316503)
XLA Ops:
  41.2 10.8 %all-to-all-done = bf16[8,96,1280]{2,1,0:T(8,128)(2,1)} async-done(((bf16[8,96,1280]{2,1,0:T(8,128)(2,1)}), bf16[8,96,1280]{2,1,0:T(8,128)(2,1)}, u32[]{:S(2)}, u32[]{:S(2)}) %all-to-all-start) | async-done | bytes 1966112 | tf_op jit(solution)/shard_map/all_to_all | solution.py:48
  54.8 6.4 %all-to-all-start.1 = ((bf16[8,96,640]{2,1,0:T(8,128)(2,1)}), bf16[8,96,640]{2,1,0:T(8,128)(2,1)S(1)}, u32[]{:S(2)}, u32[]{:S(2)}) async-start(bf16[8,96,640]{2,1,0:T(8,128)(2,1)} %get-tuple-element.116), calls=%async_computation.1 | async-start | bytes 1966080 | tf_op jit(solution)/shard_map/all_to_all | solution.py:48
  66.4 13.3 %collective-permute-done.8 = bf16[2,2,96,256]{3,2,0,1:T(8,128)(2,1)S(1)} collective-permute-done((bf16[2,2,96,256]{3,2,0,1:T(8,128)(2,1)S(1)}, bf16[2,2,96,256]{3,2,0,1:T(8,128)(2,1)S(1)}, u32[]{:S(2)}, u32[]{:S(2)}) %collective-permute-start.8) | collective-permute-done | bytes 196640 | tf_op jit(solution)/shard_map/ppermute | solution.py:31
  86.0 5.9 collective-permute-done.9
  100.1 23.9 %collective-permute-done.10 = bf16[256,256]{1,0:T(8,128)(2,1)S(1)} collective-permute-done((bf16[256,256]{1,0:T(8,128)(2,1)S(1)}, bf16[256,256]{1,0:T(8,128)(2,1)S(1)}, u32[]{:S(2)}, u32[]{:S(2)}) %collective-permute-start.10) | collective-permute-done | bytes 131104 | tf_op jit(solution)/shard_map/ppermute | solution.py:31
  124.8 10.8 %collective-permute-done.12 = bf16[2,96,768]{2,1,0:T(8,128)(2,1)S(1)} collective-permute-done((bf16[2,96,768]{2,1,0:T(8,128)(2,1)S(1)}, bf16[2,96,768]{2,1,0:T(8,128)(2,1)S(1)}, u32[]{:S(2)}, u32[]{:S(2)}) %collective-permute-start.12) | collective-permute-done | bytes 294944 | tf_op jit(solution)/shard_map/ppermute | solution.py:31
  142.5 5.8 collective-permute-done.15
  183.0 14.2 %collective-permute-done.22 = bf16[2,2,2,96,768]{4,3,2,1,0:T(8,128)(2,1)} collective-permute-done((bf16[2,2,2,96,768]{4,3,2,1,0:T(8,128)(2,1)S(1)}, bf16[2,2,2,96,768]{4,3,2,1,0:T(8,128)(2,1)}, u32[]{:S(2)}, u32[]{:S(2)}) %collective-permute-start.22) | collective-permute-done | bytes 1179680 | tf_op jit(solution)/shard_map/ppermute | solution.py:31
  215.2 15.5 %collective-permute-done.26 = bf16[40,1536]{1,0:T(8,128)(2,1)S(1)} collective-permute-done((bf16[40,1536]{1,0:T(8,128)(2,1)S(1)}, bf16[40,1536]{1,0:T(8,128)(2,1)S(1)}, u32[]{:S(2)}, u32[]{:S(2)}) %collective-permute-start.26) | collective-permute-done | bytes 122912 | tf_op jit(solution)/shard_map/ppermute | solution.py:31
  234.0 6.0 %collective-permute-done.28 = bf16[80,1536]{1,0:T(8,128)(2,1)S(1)} collective-permute-done((bf16[80,1536]{1,0:T(8,128)(2,1)S(1)}, bf16[80,1536]{1,0:T(8,128)(2,1)S(1)}, u32[]{:S(2)}, u32[]{:S(2)}) %collective-permute-start.28) | collective-permute-done | bytes 245792 | tf_op jit(solution)/shard_map/ppermute | solution.py:31
  246.0 7.5 %collective-permute-done.31 = bf16[160,1536]{1,0:T(8,128)(2,1)S(1)} collective-permute-done((bf16[160,1536]{1,0:T(8,128)(2,1)S(1)}, bf16[160,1536]{1,0:T(8,128)(2,1)S(1)}, u32[]{:S(2)}, u32[]{:S(2)}) %collective-permute-start.31) | collective-permute-done | bytes 491552 | tf_op jit(solution)/shard_map/ppermute | solution.py:31
  268.5 7.4 %fusion.91 = f32[1024,1280]{1,0:T(8,128)S(1)} fusion(bf16[1024,1536]{1,0:T(8,128)(2,1)} %constant_dynamic-update-slice_fusion.2, bf16[1536,1280]{1,0:T(8,128)(2,1)} %all-gather.3.cloned.1.call-done), kind=kOutput, calls=%fused_computation.334 | convolution fusion | flops 4026531840 | bytes 12320768 | tf_op jit(solution)/shard_map/dot_general | solution.py:213
  279.4 6.8 %fusion.78 = f32[1024,1536]{1,0:T(8,128)} fusion(bf16[1536,1280]{1,0:T(8,128)(2,1)S(1)} %copy-done.81, bf16[1024,640]{1,0:T(8,128)(2,1)S(1)} %get-tuple-element.215, bf16[1024,640]{1,0:T(8,128)(2,1)S(1)} %get-tuple-element.214), kind=kOutput, calls=%fused_computation.322 | convolution fusion | flops 4031774720 | bytes 12845056 | tf_op jit(solution)/shard_map/dot_general | solution.py:213
  286.3 6.3 %fusion.92 = f32[1024,1280]{1,0:T(8,128)S(1)} fusion(bf16[1024,1536]{1,0:T(8,128)(2,1)S(1)} %copy-done.69, bf16[1536,1280]{1,0:T(8,128)(2,1)} %collective-permute-done.34), kind=kOutput, calls=%fused_computation.335 | convolution fusion | flops 4026531840 | bytes 12320768 | tf_op jit(solution)/shard_map/dot_general | solution.py:213
  295.9 9.0 %add_convert_fusion.1 = bf16[1024,1536]{1,0:T(8,128)(2,1)S(1)} fusion(f32[1024,1536]{1,0:T(8,128)} %fusion.78, bf16[1536,1280]{1,0:T(8,128)(2,1)} %collective-permute-done.34, bf16[1024,640]{1,0:T(8,128)(2,1)S(1)} %get-tuple-element.213, bf16[1024,640]{1,0:T(8,128)(2,1)S(1)} %get-tuple-element.212), kind=kOutput, calls=%fused_computation.1 | convolution fusion | flops 4034920448 | bytes 15990784 | tf_op jit(solution)/shard_map/dot_general | solution.py:213
  332.8 10.2 %collective-permute-done.39 = bf16[80,1536]{1,0:T(8,128)(2,1)S(1)} collective-permute-done((bf16[80,1536]{1,0:T(8,128)(2,1)S(1)}, bf16[80,1536]{1,0:T(8,128)(2,1)S(1)}, u32[]{:S(2)}, u32[]{:S(2)}) %collective-permute-start.39) | collective-permute-done | bytes 245792 | tf_op jit(solution)/shard_map/ppermute | solution.py:31
  355.5 6.9 %add_convert_fusion.2 = bf16[1536,640]{1,0:T(8,128)(2,1)} fusion(bf16[1536,640]{1,0:T(8,128)(2,1)} %collective-permute-done.46, bf16[1024,1536]{1,0:T(8,128)(2,1)} %constant_dynamic-update-slice_fusion.2, bf16[1024,1280]{1,0:T(8,128)(2,1)} %copy-done.24), kind=kOutput, calls=%fused_computation.2 | convolution fusion | flops 2016215040 | bytes 8388608 | tf_op jit(solution)/shard_map/dot_general | solution.py:213
  398.8 10.4 %collective-permute-done.50 = bf16[2,2,2,256,128]{4,3,0,1,2:T(8,128)(2,1)S(1)} collective-permute-done((bf16[2,2,2,256,128]{4,3,0,1,2:T(8,128)(2,1)S(1)}, bf16[2,2,2,256,128]{4,3,0,1,2:T(8,128)(2,1)S(1)}, u32[]{:S(2)}, u32[]{:S(2)}) %collective-permute-start.50) | collective-permute-done | bytes 524320 | tf_op jit(solution)/shard_map/ppermute | solution.py:31
  428.0 12.6 %collective-permute-start.55 = (bf16[256,256]{1,0:T(8,128)(2,1)S(1)}, bf16[256,256]{1,0:T(8,128)(2,1)S(1)}, u32[]{:S(2)}, u32[]{:S(2)}) collective-permute-start(bf16[256,256]{1,0:T(8,128)(2,1)S(1)} %dynamic-slice_bitcast_fusion.13), channel_id=1, source_target_pairs={{0,16},{16,0},{1,17},{17,1},{2,18},{18,2},{3,19},{19,3},{4,20},{20... | collective-permute-start | bytes 393224 | tf_op jit(solution)/shard_map/ppermute | solution.py:31
  443.1 19.6 %collective-permute-done.55 = bf16[256,256]{1,0:T(8,128)(2,1)S(1)} collective-permute-done((bf16[256,256]{1,0:T(8,128)(2,1)S(1)}, bf16[256,256]{1,0:T(8,128)(2,1)S(1)}, u32[]{:S(2)}, u32[]{:S(2)}) %collective-permute-start.55) | collective-permute-done | bytes 131104 | tf_op jit(solution)/shard_map/ppermute | solution.py:31
  466.2 6.4 %collective-permute-done.68 = bf16[2,2,96,384]{3,2,0,1:T(8,128)(2,1)S(1)} collective-permute-done((bf16[2,2,96,384]{3,2,0,1:T(8,128)(2,1)S(1)}, bf16[2,2,96,384]{3,2,0,1:T(8,128)(2,1)S(1)}, u32[]{:S(2)}, u32[]{:S(2)}) %collective-permute-start.68) | collective-permute-done | bytes 294944 | tf_op jit(solution)/shard_map/ppermute | solution.py:31
  472.8 5.7 collective-permute-done.56
  504.6 12.1 %collective-permute-done.73 = bf16[2,96,768]{2,1,0:T(8,128)(2,1)S(1)} collective-permute-done((bf16[2,96,768]{2,1,0:T(8,128)(2,1)S(1)}, bf16[2,96,768]{2,1,0:T(8,128)(2,1)S(1)}, u32[]{:S(2)}, u32[]{:S(2)}) %collective-permute-start.73) | collective-permute-done | bytes 294944 | tf_op jit(solution)/shard_map/ppermute | solution.py:31
  552.8 7.5 %collective-permute-done.85 = f32[32,128]{1,0:T(8,128)S(1)} collective-permute-done((f32[32,128]{1,0:T(8,128)S(1)}, f32[32,128]{1,0:T(8,128)S(1)}, u32[]{:S(2)}, u32[]{:S(2)}) %collective-permute-start.85) | collective-permute-done | bytes 16416 | tf_op jit(solution)/shard_map/ppermute | solution.py:31
  (606 shorter events, 332.7 us)
Async XLA Ops:
  20.6 31.4 %all-to-all-start = ((bf16[8,96,1280]{2,1,0:T(8,128)(2,1)}), bf16[8,96,1280]{2,1,0:T(8,128)(2,1)}, u32[]{:S(2)}, u32[]{:S(2)}) async-start(bf16[8,96,1280]{2,1,0:T(8,128)(2,1)} %get-tuple-element.112), calls=%async_computation | async-start | bytes 3932160 | tf_op jit(solution)/shard_map/all_to_all | solution.py:48
  25.1 28.9 %collective-permute-start.11 = (bf16[96,768]{1,0:T(8,128)(2,1)S(1)}, bf16[96,768]{1,0:T(8,128)(2,1)S(1)}, u32[]{:S(2)}, u32[]{:S(2)}) collective-permute-start(bf16[96,768]{1,0:T(8,128)(2,1)S(1)} %bitcast.455), channel_id=1, source_target_pairs={{0,16},{16,0},{1,17},{17,1},{2,18},{18,2},{3,19},{19,3},{4,20},{20... | collective-permute-start | bytes 442376 | tf_op jit(solution)/shard_map/ppermute | solution.py:31
  28.9 51.0 %collective-permute-start.13 = (bf16[128,1536]{1,0:T(8,128)(2,1)}, bf16[128,1536]{1,0:T(8,128)(2,1)}, u32[]{:S(2)}, u32[]{:S(2)}) collective-permute-start(bf16[128,1536]{1,0:T(8,128)(2,1)} %dynamic-slice_bitcast_fusion.1), channel_id=1, source_target_pairs={{0,4},{4,0},{1,5},{5,1},{2,6},{6,2},{3,7},{7,3},{8,12},{12,8},{9,1... | collective-permute-start | bytes 1179656 | tf_op jit(solution)/shard_map/ppermute | solution.py:31
  54.8 82.5 %all-to-all-start.1 = ((bf16[8,96,640]{2,1,0:T(8,128)(2,1)}), bf16[8,96,640]{2,1,0:T(8,128)(2,1)S(1)}, u32[]{:S(2)}, u32[]{:S(2)}) async-start(bf16[8,96,640]{2,1,0:T(8,128)(2,1)} %get-tuple-element.116), calls=%async_computation.1 | async-start | bytes 1966080 | tf_op jit(solution)/shard_map/all_to_all | solution.py:48
  61.2 194.4 %all-gather.3.cloned.1.call-start = ((), (), s32[]{:S(2)}) async-start(), calls=%async_computation.8 | async-start | bytes 5898240 | tf_op jit(solution)/shard_map/all_gather | solution.py:520
  61.9 201.3 %all-gather.5.cloned.1.call-start = ((), (), s32[]{:S(2)}) async-start(), calls=%async_computation.9 | async-start | bytes 2949120 | tf_op jit(solution)/shard_map/all_gather | solution.py:521
  83.2 54.1 %collective-permute-start.14 = (bf16[256,1536]{1,0:T(8,128)(2,1)S(1)}, bf16[256,1536]{1,0:T(8,128)(2,1)}, u32[]{:S(2)}, u32[]{:S(2)}) collective-permute-start(bf16[256,1536]{1,0:T(8,128)(2,1)S(1)} %pad_maximum_fusion.6), channel_id=1, source_target_pairs={{0,8},{8,0},{1,9},{9,1},{2,10},{10,2},{3,11},{11,3},{4,12},{12,4},... | collective-permute-start | bytes 2359304 | tf_op jit(solution)/shard_map/ppermute | solution.py:31
  84.7 76.6 %collective-permute-start.6 = (bf16[2,2,2,96,384]{4,3,0,1,2:T(8,128)(2,1)}, bf16[2,2,2,96,384]{4,3,0,1,2:T(8,128)(2,1)}, u32[]{:S(2)}, u32[]{:S(2)}) collective-permute-start(bf16[2,2,2,96,384]{4,3,0,1,2:T(8,128)(2,1)} %maximum_select_fusion.14), channel_id=1, source_target_pairs={{0,2},{2,0},{1,3},{3,1},{4,6},{6,4},{5,7},{7,5},{8,10},{10,8},{9,1... | collective-permute-start | bytes 1769480 | tf_op jit(solution)/shard_map/ppermute | solution.py:31
  92.6 31.5 %collective-permute-start.10 = (bf16[256,256]{1,0:T(8,128)(2,1)S(1)}, bf16[256,256]{1,0:T(8,128)(2,1)S(1)}, u32[]{:S(2)}, u32[]{:S(2)}) collective-permute-start(bf16[256,256]{1,0:T(8,128)(2,1)S(1)} %shard_map.265), channel_id=1, source_target_pairs={{0,16},{16,0},{1,17},{17,1},{2,18},{18,2},{3,19},{19,3},{4,20},{20... | collective-permute-start | bytes 393224 | tf_op jit(solution)/shard_map/ppermute | solution.py:31
  94.5 41.2 %collective-permute-start.12 = (bf16[2,96,768]{2,1,0:T(8,128)(2,1)S(1)}, bf16[2,96,768]{2,1,0:T(8,128)(2,1)S(1)}, u32[]{:S(2)}, u32[]{:S(2)}) collective-permute-start(bf16[2,96,768]{2,1,0:T(8,128)(2,1)S(1)} %copy-done.23), channel_id=1, source_target_pairs={{0,8},{8,0},{1,9},{9,1},{2,10},{10,2},{3,11},{11,3},{4,12},{12,4},... | collective-permute-start | bytes 884744 | tf_op jit(solution)/shard_map/ppermute | solution.py:31
  99.2 63.7 %collective-permute-start.4 = (bf16[2,2,2,96,384]{4,3,0,1,2:T(8,128)(2,1)}, bf16[2,2,2,96,384]{4,3,0,1,2:T(8,128)(2,1)}, u32[]{:S(2)}, u32[]{:S(2)}) collective-permute-start(bf16[2,2,2,96,384]{4,3,0,1,2:T(8,128)(2,1)} %maximum_select_fusion.12), channel_id=1, source_target_pairs={{0,4},{4,0},{1,5},{5,1},{2,6},{6,2},{3,7},{7,3},{8,12},{12,8},{9,1... | collective-permute-start | bytes 1769480 | tf_op jit(solution)/shard_map/ppermute | solution.py:31
  170.0 33.7 %collective-permute-start.21 = (bf16[512,1536]{1,0:T(8,128)(2,1)}, bf16[512,1536]{1,0:T(8,128)(2,1)}, u32[]{:S(2)}, u32[]{:S(2)}) collective-permute-start(bf16[512,1536]{1,0:T(8,128)(2,1)} %pad_maximum_fusion.5), channel_id=1, source_target_pairs={{0,2},{2,0},{1,3},{3,1},{4,6},{6,4},{5,7},{7,5},{8,10},{10,8},{9,1... | collective-permute-start | bytes 4718600 | tf_op jit(solution)/shard_map/ppermute | solution.py:31
  175.1 344.9 %reduce-scatter.6.cloned.1.call-start = ((), (), s32[]{:S(2)}) async-start(), calls=%async_computation.11 | async-start | bytes 2949120 | tf_op jit(solution)/shard_map/reduce_scatter | solution.py:591
  255.6 30.7 %collective-permute-start.34 = (bf16[1536,1280]{1,0:T(8,128)(2,1)}, bf16[1536,1280]{1,0:T(8,128)(2,1)}, u32[]{:S(2)}, u32[]{:S(2)}) collective-permute-start(bf16[1536,1280]{1,0:T(8,128)(2,1)} %all-gather.3.cloned.1.call-done), channel_id=1, source_target_pairs={{0,1},{1,0},{2,3},{3,2},{4,5},{5,4},{6,7},{7,6},{8,9},{9,8},{10,11... | collective-permute-start | bytes 11796488 | tf_op jit(solution)/shard_map/ppermute | solution.py:40
  263.2 29.4 %collective-permute-start.33 = (bf16[1536,640]{1,0:T(8,128)(2,1)}, bf16[1536,640]{1,0:T(8,128)(2,1)S(1)}, u32[]{:S(2)}, u32[]{:S(2)}) collective-permute-start(bf16[1536,640]{1,0:T(8,128)(2,1)} %all-gather.5.cloned.1.call-done), channel_id=1, source_target_pairs={{0,1},{1,0},{2,3},{3,2},{4,5},{5,4},{6,7},{7,6},{8,9},{9,8},{10,11... | collective-permute-start | bytes 5898248 | tf_op jit(solution)/shard_map/ppermute | solution.py:40
  316.4 226.9 %reduce-scatter.4.cloned.1.call-start = ((), (), s32[]{:S(2)}) async-start(), calls=%async_computation.10 | async-start | bytes 2949120 | tf_op jit(solution)/shard_map/reduce_scatter | solution.py:591
  326.0 29.5 %collective-permute-start.46 = (bf16[1536,640]{1,0:T(8,128)(2,1)}, bf16[1536,640]{1,0:T(8,128)(2,1)}, u32[]{:S(2)}, u32[]{:S(2)}) collective-permute-start(bf16[1536,640]{1,0:T(8,128)(2,1)} %convolution_convert_fusion.2), channel_id=1, source_target_pairs={{0,1},{1,0},{2,3},{3,2},{4,5},{5,4},{6,7},{7,6},{8,9},{9,8},{10,11... | collective-permute-start | bytes 5898248 | tf_op jit(solution)/shard_map/ppermute | solution.py:40
  348.3 222.6 %reduce-scatter.8.cloned.1.call-start = ((), (), s32[]{:S(2)}) async-start(), calls=%async_computation.12 | async-start | bytes 2949120 | tf_op jit(solution)/shard_map/reduce_scatter | solution.py:591
  373.9 107.5 %collective-permute-start.84 = (f32[128,1536]{1,0:T(8,128)}, f32[128,1536]{1,0:T(8,128)S(1)}, u32[]{:S(2)}, u32[]{:S(2)}) collective-permute-start(f32[128,1536]{1,0:T(8,128)} %get-tuple-element.209), channel_id=1, source_target_pairs={{0,1},{1,0},{2,3},{3,2},{4,5},{5,4},{6,7},{7,6},{8,9},{9,8},{10,11... | collective-permute-start | bytes 2359304 | tf_op jit(solution)/shard_map/ppermute | solution.py:40
  428.0 34.7 %collective-permute-start.55 = (bf16[256,256]{1,0:T(8,128)(2,1)S(1)}, bf16[256,256]{1,0:T(8,128)(2,1)S(1)}, u32[]{:S(2)}, u32[]{:S(2)}) collective-permute-start(bf16[256,256]{1,0:T(8,128)(2,1)S(1)} %dynamic-slice_bitcast_fusion.13), channel_id=1, source_target_pairs={{0,16},{16,0},{1,17},{17,1},{2,18},{18,2},{3,19},{19,3},{4,20},{20... | collective-permute-start | bytes 393224 | tf_op jit(solution)/shard_map/ppermute | solution.py:31
  440.7 38.1 %collective-permute-start.58 = (bf16[2,2,2,96,384]{4,3,0,1,2:T(8,128)(2,1)S(1)}, bf16[2,2,2,96,384]{4,3,0,1,2:T(8,128)(2,1)S(1)}, u32[]{:S(2)}, u32[]{:S(2)}) collective-permute-start(bf16[2,2,2,96,384]{4,3,0,1,2:T(8,128)(2,1)S(1)} %copy_bitcast_fusion.3), channel_id=1, source_target_pairs={{0,2},{2,0},{1,3},{3,1},{4,6},{6,4},{5,7},{7,5},{8,10},{10,8},{9,1... | collective-permute-start | bytes 1769480 | tf_op jit(solution)/shard_map/ppermute | solution.py:31
  440.8 37.8 %collective-permute-start.59 = (bf16[2,2,2,96,384]{4,3,0,1,2:T(8,128)(2,1)S(1)}, bf16[2,2,2,96,384]{4,3,0,1,2:T(8,128)(2,1)S(1)}, u32[]{:S(2)}, u32[]{:S(2)}) collective-permute-start(bf16[2,2,2,96,384]{4,3,0,1,2:T(8,128)(2,1)S(1)} %copy_bitcast_fusion.2), channel_id=1, source_target_pairs={{0,4},{4,0},{1,5},{5,1},{2,6},{6,2},{3,7},{7,3},{8,12},{12,8},{9,1... | collective-permute-start | bytes 1769480 | tf_op jit(solution)/shard_map/ppermute | solution.py:31
  495.4 29.8 %collective-permute-start.63 = (bf16[192,1536]{1,0:T(8,128)(2,1)S(1)}, bf16[192,1536]{1,0:T(8,128)(2,1)S(1)}, u32[]{:S(2)}, u32[]{:S(2)}) collective-permute-start(bf16[192,1536]{1,0:T(8,128)(2,1)S(1)} %slice.450), channel_id=1, source_target_pairs={{0,8},{8,0},{1,9},{9,1},{2,10},{10,2},{3,11},{11,3},{4,12},{12,4},... | collective-permute-start | bytes 1769480 | tf_op jit(solution)/shard_map/ppermute | solution.py:31
  495.4 29.8 %collective-permute-start.64 = (bf16[160,1536]{1,0:T(8,128)(2,1)}, bf16[160,1536]{1,0:T(8,128)(2,1)}, u32[]{:S(2)}, u32[]{:S(2)}) collective-permute-start(bf16[160,1536]{1,0:T(8,128)(2,1)} %get-tuple-element.169), channel_id=1, source_target_pairs={{0,2},{2,0},{1,3},{3,1},{4,6},{6,4},{5,7},{7,5},{8,10},{10,8},{9,1... | collective-permute-start | bytes 1474568 | tf_op jit(solution)/shard_map/ppermute | solution.py:31
  (165 other events, 1894.9 us)
Sparse Core Ops, SparseCore 0:
  63.6 103.7 all-gather.2
  175.2 53.2 all-gather.4
  316.5 50.2 reduce-scatter.5
  369.0 51.3 reduce-scatter.3
  422.5 57.0 reduce-scatter.7

commit v5 on v4

--- a/solution.py
+++ b/solution.py
@@ -116,9 +116,8 @@
 
 
 def cube_parts(rows):
-    units = rows // 8
-    sizes = [(units + 2 - i) // 3 * 8 for i in range(3)]
-    return sizes
+    units = rows // 16
+    return [(units + 2 - i) // 3 * 16 for i in range(3)]
 
 
 def cube_gather(value):
@@ -143,15 +142,29 @@
         return self
 
     def done(self):
-        slots = self.value.reshape((8, self.size) + self.value.shape[1:])
         pieces, at = [], 0
         for rows, order in zip(cube_parts(self.size), CUBE):
             wanted = [0]
             for bit in order:
                 wanted = wanted + [w ^ (1 << bit) for w in wanted]
-            pieces += [slots[self.have.index(w), at : at + rows] for w in wanted]
+            pieces += [(self.have.index(w) * self.size + at, rows) for w in wanted]
             at += rows
-        return jnp.concatenate(pieces, 0)
+
+        def kernel(value, out):
+            place = 0
+            for start, rows in pieces:
+                out[place : place + rows] = value[start : start + rows]
+                place += rows
+
+        vmem = pl.BlockSpec(memory_space=pltpu.VMEM)
+        return pl.pallas_call(
+            kernel,
+            out_shape=jax.ShapeDtypeStruct(self.value.shape, BF),
+            in_specs=[vmem],
+            out_specs=vmem,
+            compiler_params=pltpu.CompilerParams(vmem_limit_bytes=16 * 2**20),
+            cost_estimate=pl.CostEstimate(flops=0, bytes_accessed=2**23, transcendentals=0),
+        )(self.value)
 
 
 class CubeSum:
@@ -320,7 +333,7 @@
             dprobs = dot(value, grad, NT)
             dscores = (probs * (dprobs - delta[h])).astype(BF)
             dk = dk + dot(dscores, query)
-            dq = dot(dscores, key, TN) * scale
+            dq = dot(dscores, key, TN)
             if first:
                 dq_ref[:, cols] = dq
             else:
@@ -344,7 +357,7 @@
     lax.fori_loop(0, blocks, step, 0)
     for h in range(heads):
         cols = slice(h * HD, (h + 1) * HD)
-        out_ref[:, cols] = turn(dq_ref[:, cols], cos_ref[...], -sin_ref[...]).astype(BF)
+        out_ref[:, cols] = turn(dq_ref[:, cols] * scale, cos_ref[...], -sin_ref[...]).astype(BF)
 
 
 def attend_back(vis, query, keyval, grad, out, lse, cosine, sine):
@@ -501,6 +514,12 @@
     def my_half(value):
         return halves(value.reshape((2, low_rows) + value.shape[1:]), core)
 
+    def whole(own):
+        other = swap_mp(own)
+        return jnp.where(
+            core == 0, jnp.concatenate([own, other], 0), jnp.concatenate([other, own], 0)
+        )
+
     bits = blocks.bit_length() - 1
     high = list(range(3, bits))[::-1]
 
@@ -514,11 +533,15 @@
         w_kv.step(bit)
         w_q.step(bit)
         w_out_all.step(bit)
-    cot_cube.step(1)
-    both_cube = trade(after(both_send, w_kv.last, w_q.last), CUBE_AXES)
-    down_cube = trade(after(down_send, both_cube), CUBE_AXES)
+    cot_cube.step(2)
+    near = [after(my_half(tokens), w_kv.last)]
+    for bit in high[::-1]:
+        near = near + [flip(v, bit) for v in near]
+    both_cube = trade(after(both_send, w_kv.last), CUBE_AXES)
+    down_near = [after(down_send, w_kv.last)]
+    for bit in high[::-1]:
+        down_near = down_near + [flip(v, bit) for v in down_near]
     both_own = lax.all_gather(both_cube.reshape(8 * slab, -1), "h", axis=0, tiled=True)
-    down_own = lax.all_gather(down_cube.reshape(8 * slab, -1), "h", axis=0, tiled=True)
     block_map = after(block_map, both_send)
     inputs = after(tokens, both_send).astype(F32)
     per_unit = SEG // rows
@@ -531,14 +554,23 @@
     my_seq = jnp.sum(jnp.where(own_place, seqs, 0))
     vis = ((seqs == my_seq) & (block_map < my_block)).astype(jnp.int32)
     vis = jnp.concatenate([vis, me[None].astype(jnp.int32)])
-    begin = look(first_unit, (my_block // per_unit)[None])
-    position = my_block * rows - begin[0] * SEG + jnp.arange(rows, dtype=jnp.int32)
-    cosine, sine = rope_tables(position)
+    places = jnp.bitwise_xor(me, 8 * jnp.arange(blocks // 8, dtype=jnp.int32))
+    near_blocks = look(block_map, places)
+    begin = look(first_unit, near_blocks // per_unit)
+    position = (near_blocks * rows - begin * SEG)[:, None] + jnp.arange(rows, dtype=jnp.int32)
+    cosine_all, sine_all = rope_tables(position.reshape(-1))
+    cosine, sine = cosine_all[:rows], sine_all[:rows]
 
     gain_one = norm_gain.astype(F32)
-    inverse_one = lax.rsqrt(jnp.mean(inputs * inputs, axis=-1, keepdims=True) + epsilon)
-    normed = (inputs * inverse_one * gain_one).astype(BF)
-    w_kv.value = after(w_kv.value, both_cube, cosine, vis, normed)
+
+    def norm_one(value):
+        inverse = lax.rsqrt(jnp.mean(value * value, axis=-1, keepdims=True) + epsilon)
+        return inverse, (value * inverse * gain_one).astype(BF)
+
+    inverse_one, normed = norm_one(inputs)
+    normed_near = [norm_one(after(whole(v), both_send).astype(F32))[1] for v in near[1:]]
+    normed_near = jnp.concatenate([normed] + normed_near, 0)
+    w_kv.value = after(w_kv.value, both_cube, cosine, vis, normed_near)
     w_q.value = after(w_q.value, both_cube)
     w_kv.step(2)
     w_q.step(2)
@@ -546,26 +578,40 @@
     w_kv.step(1)
     one.step(0)
     two.step(1)
-    cot_cube.value = after(cot_cube.value, w_q.last)
-    cot_cube.step(2)
+    w_out_all.value = after(w_out_all.value, w_q.last)
+    w_out_all.step(2)
     w_kv = w_kv.step(0).rows()
     w_q = joined([one.step(1), two.step(0)]).rows()
-
-    keyval = Gather(project(normed, w_kv, jnp.concatenate([b_key, b_value]), cosine, sine, 1))
-
+    q_last = (one.last, two.last)
+
+    keyval = project(
+        normed_near, w_kv, jnp.concatenate([b_key, b_value]), cosine_all, sine_all, 1
+    )
+    keyval = list(keyval.reshape(blocks // 8, rows, 2 * HD))
+    for bit in high:
+        mask = 1 << (bit - 3)
+        keyval = [jnp.where(mine(bit) == 0, v, keyval[k ^ mask]) for k, v in enumerate(keyval)]
+    keyval = Gather(jnp.stack(keyval, 0).reshape((2,) * len(high) + (rows, 2 * HD)))
+    keyval.have = list(high)
+    keyval.value = after(keyval.value, w_out_all.last)
     w_out_all.value = after(w_out_all.value, w_kv)
-    for bit in high:
-        keyval.step(bit)
-    w_out_all.step(2)
-    keyval.value = after(keyval.value, down_cube, w_out_all.last, cot_cube.last)
+    cot_cube.value = after(cot_cube.value, w_kv)
     keyval.step(2)
     w_out_all.step(0)
+    cot_cube.step(1)
     key_part, value_part = keyval.split(2)
-    key_part.value = after(key_part.value, w_out_all.last)
+    key_part.value = after(key_part.value, w_out_all.last, cot_cube.last, *q_last)
     key_part.step(0)
     value_part.step(1)
     key_part.step(1)
     value_part.step(0)
+    for bit in high:
+        mask = 1 << (bit - 3)
+        down_near = [
+            jnp.where(mine(bit) == 0, v, down_near[k ^ mask]) for k, v in enumerate(down_near)
+        ]
+    down_near = after(jnp.stack(down_near, 0), key_part.last, value_part.last)
+    down_own = trade(down_near, CUBE_AXES, 1).reshape(model, part)
     w_out_all.value = after(w_out_all.value, key_part.last, value_part.last)
     cot_cube.value = after(cot_cube.value, key_part.last, value_part.last)
     keyval = joined([key_part, value_part]).value.reshape(blocks, rows, 2 * HD)
@@ -573,7 +619,7 @@
     cot_cube.step(0)
     query = project(normed, w_q, b_query, cosine, sine, heads)
     attended, attended_low, lse = attend(vis, query, keyval)
-    attended_low = after(attended_low, cot_cube.last)
+    attended_low = after(attended_low, cot_cube.last, down_own, both_own)
     cot_cube = cot_cube.done()
     attn = dot(attended_low, out_full, NT).astype(BF).reshape(2, low_rows, model)
     attn = halves(attn, core).astype(F32) + swap_mp(halves(attn, 1 - core)).astype(F32)
@@ -582,8 +628,6 @@
     inverse_two = lax.rsqrt(jnp.mean(middle * middle, axis=-1, keepdims=True) + epsilon)
     normed_two = (middle * inverse_two * gain_two).astype(BF)
     cube_two, came = cube_gather(normed_two)
-    both_own = after(both_own, *came)
-    down_own = after(down_own, *came)
     both_w = (both_own, swap_mp(both_own))
     down_w = (down_own, swap_mp(down_own))
 
@@ -624,12 +668,6 @@
     up_back = (dot(cube_two, ups[0], TN) + came[2].astype(F32)).astype(BF)
     up_high = over_high_back(up_back)
     grad_two = after(grad_two.total(), up_back)
-
-    def whole(own):
-        other = swap_mp(own)
-        return jnp.where(
-            core == 0, jnp.concatenate([own, other], 0), jnp.concatenate([other, own], 0)
-        )
 
     grad_middle_norm, grad_gain_two = norm_back(grad_two, middle, inverse_two, gain_two)
     grad_middle_half = cot_half.astype(F32) + grad_middle_norm

time: 604 us -> 602 us (level)
  waiting for transfers between devices: 247 us -> 269 us
  starting transfers between devices: 136 us -> 127 us
    all_gather x1, waiting for transfers between devices: 0.01 us -> 26.4 us  [shards(): lax.all_gather(both_cube.reshape(8 * slab, -1), 'h', axis=0, tiled=True)]
    all_to_all x5, waiting for transfers between devices: 15.1 us -> 4.14 us  [trade(): return lax.all_to_all(value, axes, dim, dim, tiled=True)]
    select_n x27 -> x25, other arithmetic: 20.4 us -> 13.3 us  [step(): jnp.where(mine(bit) == 0, jnp.stack([self.value, other], at), jnp.stack([...]
    unnamed x218 -> x226, local copies, waits for them, and re-layouts: 23.5 us -> 17.1 us
    ppermute x76 -> x77, waiting for transfers between devices: 229 us -> 235 us  [flip(): lax.ppermute(value, axis, [(i, i ^ mask) for i in range(lax.axis_size(axi...]
    ppermute x76 -> x77, starting transfers between devices: 110 us -> 106 us  [flip(): lax.ppermute(value, axis, [(i, i ^ mask) for i in range(lax.axis_size(axi...]
  transfers between devices with their start and end apart: 97 -> 98, of which waited for: 46 -> 48; matrix products, arithmetic and copies ran while one was open for 25% -> 22% of each run, Pallas kernels for 2% -> 2%
where the time goes in v5:
time: 602 us; the launch traced here: 594 us
  waiting for transfers between devices  269 us (45%)
  starting transfers between devices  127 us (21%)
  matrix products  71.7 us (12%)
  other arithmetic  59.8 us (10%)
  local copies, waits for them, and re-layouts  35.5 us (6%)
  between operations  16.7 us (3%)
  Pallas kernels  14.7 us (2%)
    ppermute x77, waiting for transfers between devices, flip(): lax.ppermute(value, axis, [(i, i ^ mask) for i in range(lax.axis_size(axi...  235 us
    ppermute x77, starting transfers between devices, flip(): lax.ppermute(value, axis, [(i, i ^ mask) for i in range(lax.axis_size(axi...  106 us
    dot_general x21, matrix products, dot(): return lax.dot_general(left, right, dims, preferred_element_type=F32)  71.7 us
    all_gather x1, waiting for transfers between devices, shards(): lax.all_gather(both_cube.reshape(8 * slab, -1), 'h', axis=0, tiled=True)  26.4 us
    all_to_all x5, starting transfers between devices, trade(): return lax.all_to_all(value, axes, dim, dim, tiled=True)  19.8 us
    unnamed x226, local copies, waits for them, and re-layouts  17.1 us
    select_n x25, other arithmetic, step(): jnp.where(mine(bit) == 0, jnp.stack([self.value, other], at), jnp.stack([...  13.3 us
  transfers between devices with their start and end apart: 98, of which 48 were waited for; matrix products, arithmetic and copies ran while one was open for 22% of the time, Pallas kernels for 2%

profile of v5, /device:TPU:0, one launch (start us, length us, event | category | flops | bytes accessed | tf_op | source)
XLA Modules:
  0.0 594.4 jit_solution(500141378231520279)
XLA Ops:
  36.4 24.1 %collective-permute-done.7 = bf16[128,1536]{1,0:T(8,128)(2,1)S(1)} collective-permute-done((bf16[128,1536]{1,0:T(8,128)(2,1)S(1)}, bf16[128,1536]{1,0:T(8,128)(2,1)S(1)}, u32[]{:S(2)}, u32[]{:S(2)}) %collective-permute-start.7) | collective-permute-done | bytes 393248 | tf_op jit(solution)/shard_map/ppermute | solution.py:31
  67.8 8.7 %collective-permute-done.9 = bf16[2,96,256]{2,1,0:T(8,128)(2,1)S(1)} collective-permute-done((bf16[2,96,256]{2,1,0:T(8,128)(2,1)S(1)}, bf16[2,96,256]{2,1,0:T(8,128)(2,1)S(1)}, u32[]{:S(2)}, u32[]{:S(2)}) %collective-permute-start.9) | collective-permute-done | bytes 98336 | tf_op jit(solution)/shard_map/ppermute | solution.py:31
  110.6 4.7 collective-permute-done.6
  117.1 11.3 %collective-permute-done.4 = bf16[2,2,2,96,384]{4,3,0,1,2:T(8,128)(2,1)S(1)} collective-permute-done((bf16[2,2,2,96,384]{4,3,0,1,2:T(8,128)(2,1)S(1)}, bf16[2,2,2,96,384]{4,3,0,1,2:T(8,128)(2,1)S(1)}, u32[]{:S(2)}, u32[]{:S(2)}) %collective-permute-start.4) | collective-permute-done | bytes 589856 | tf_op jit(solution)/shard_map/ppermute | solution.py:31
  139.2 6.8 %collective-permute-done.23 = bf16[8,96,640]{2,1,0:T(8,128)(2,1)} collective-permute-done((bf16[8,96,640]{2,1,0:T(8,128)(2,1)S(1)}, bf16[8,96,640]{2,1,0:T(8,128)(2,1)}, u32[]{:S(2)}, u32[]{:S(2)}) %collective-permute-start.23) | collective-permute-done | bytes 983072 | tf_op jit(solution)/shard_map/ppermute | solution.py:31
  172.0 29.9 %collective-permute-done.24 = bf16[2,2,2,96,768]{4,3,2,1,0:T(8,128)(2,1)S(1)} collective-permute-done((bf16[2,2,2,96,768]{4,3,2,1,0:T(8,128)(2,1)S(1)}, bf16[2,2,2,96,768]{4,3,2,1,0:T(8,128)(2,1)S(1)}, u32[]{:S(2)}, u32[]{:S(2)}) %collective-permute-start.24) | collective-permute-done | bytes 1179680 | tf_op jit(solution)/shard_map/ppermute | solution.py:31
  209.3 26.4 %all-gather.2.cloned.1.call-done = bf16[1536,1280]{1,0:T(8,128)(2,1)} async-done(((bf16[768,1280]{1,0:T(8,128)(2,1)}), bf16[1536,1280]{1,0:T(8,128)(2,1)}) %all-gather.2.cloned.1.call-update) | async-done | bytes 3932176 | tf_op jit(solution)/shard_map/all_gather | solution.py:544
  259.9 9.8 %collective-permute-done.34 = bf16[128,1536]{1,0:T(8,128)(2,1)S(1)} collective-permute-done((bf16[128,1536]{1,0:T(8,128)(2,1)S(1)}, bf16[128,1536]{1,0:T(8,128)(2,1)S(1)}, u32[]{:S(2)}, u32[]{:S(2)}) %collective-permute-start.34) | collective-permute-done | bytes 393248 | tf_op jit(solution)/shard_map/ppermute | solution.py:31
  280.4 6.6 %fusion.60 = f32[1024,1536]{1,0:T(8,128)} fusion(bf16[1536,1280]{1,0:T(8,128)(2,1)S(1)} %copy-done.100, bf16[1024,640]{1,0:T(8,128)(2,1)S(1)} %get-tuple-element.219, bf16[1024,640]{1,0:T(8,128)(2,1)S(1)} %get-tuple-element.218), kind=kOutput, calls=%fused_computation.299 | convolution fusion | flops 4031774720 | bytes 12845056 | tf_op jit(solution)/shard_map/dot_general | solution.py:226
  294.6 7.0 %add_convert_fusion.1 = bf16[1024,1536]{1,0:T(8,128)(2,1)S(1)} fusion(f32[1024,1536]{1,0:T(8,128)} %fusion.60, bf16[1536,1280]{1,0:T(8,128)(2,1)S(1)} %collective-permute-done.36, bf16[1024,640]{1,0:T(8,128)(2,1)S(1)} %get-tuple-element.217, bf16[1024,640]{1,0:T(8,128)(2,1)S(1)} %get-tuple-element.216), kind=kOutput, calls=%fused_computation.1 | convolution fusion | flops 4034920448 | bytes 15990784 | tf_op jit(solution)/shard_map/dot_general | solution.py:226
  315.1 5.1 convolution_convert_fusion.3
  337.3 4.7 collective-permute-done.41
  343.7 5.2 add_convert_fusion.3
  355.1 6.9 %add_convert_fusion.2 = bf16[1536,640]{1,0:T(8,128)(2,1)} fusion(bf16[1536,640]{1,0:T(8,128)(2,1)} %collective-permute-done.48, bf16[1024,1536]{1,0:T(8,128)(2,1)} %copy-done.90, bf16[1024,1280]{1,0:T(8,128)(2,1)} %pad_maximum_fusion.1), kind=kOutput, calls=%fused_computation.2 | convolution fusion | flops 2016215040 | bytes 8388608 | tf_op jit(solution)/shard_map/dot_general | solution.py:226
  395.7 10.1 %collective-permute-done.52 = bf16[2,2,2,256,128]{4,3,0,1,2:T(8,128)(2,1)S(1)} collective-permute-done((bf16[2,2,2,256,128]{4,3,0,1,2:T(8,128)(2,1)S(1)}, bf16[2,2,2,256,128]{4,3,0,1,2:T(8,128)(2,1)S(1)}, u32[]{:S(2)}, u32[]{:S(2)}) %collective-permute-start.52) | collective-permute-done | bytes 524320 | tf_op jit(solution)/shard_map/ppermute | solution.py:31
  419.4 4.9 collective-permute-done.56
  424.3 10.2 %collective-permute-start.57 = (bf16[256,256]{1,0:T(8,128)(2,1)S(1)}, bf16[256,256]{1,0:T(8,128)(2,1)S(1)}, u32[]{:S(2)}, u32[]{:S(2)}) collective-permute-start(bf16[256,256]{1,0:T(8,128)(2,1)S(1)} %dynamic-slice_bitcast_fusion.14), channel_id=1, source_target_pairs={{0,16},{16,0},{1,17},{17,1},{2,18},{18,2},{3,19},{19,3},{4,20},{20... | collective-permute-start | bytes 393224 | tf_op jit(solution)/shard_map/ppermute | solution.py:31
  437.0 23.4 %collective-permute-done.57 = bf16[256,256]{1,0:T(8,128)(2,1)S(1)} collective-permute-done((bf16[256,256]{1,0:T(8,128)(2,1)S(1)}, bf16[256,256]{1,0:T(8,128)(2,1)S(1)}, u32[]{:S(2)}, u32[]{:S(2)}) %collective-permute-start.57) | collective-permute-done | bytes 131104 | tf_op jit(solution)/shard_map/ppermute | solution.py:31
  463.9 6.4 %collective-permute-done.70 = bf16[2,2,96,384]{3,2,0,1:T(8,128)(2,1)S(1)} collective-permute-done((bf16[2,2,96,384]{3,2,0,1:T(8,128)(2,1)S(1)}, bf16[2,2,96,384]{3,2,0,1:T(8,128)(2,1)S(1)}, u32[]{:S(2)}, u32[]{:S(2)}) %collective-permute-start.70) | collective-permute-done | bytes 294944 | tf_op jit(solution)/shard_map/ppermute | solution.py:31
  470.5 6.7 %collective-permute-done.58 = bf16[2,2,2,96,256]{4,3,0,1,2:T(8,128)(2,1)S(1)} collective-permute-done((bf16[2,2,2,96,256]{4,3,0,1,2:T(8,128)(2,1)S(1)}, bf16[2,2,2,96,256]{4,3,0,1,2:T(8,128)(2,1)S(1)}, u32[]{:S(2)}, u32[]{:S(2)}) %collective-permute-start.58) | collective-permute-done | bytes 393248 | tf_op jit(solution)/shard_map/ppermute | solution.py:31
  500.6 5.1 collective-permute-done.69
  505.7 9.4 %collective-permute-done.75 = bf16[2,96,768]{2,1,0:T(8,128)(2,1)S(1)} collective-permute-done((bf16[2,96,768]{2,1,0:T(8,128)(2,1)S(1)}, bf16[2,96,768]{2,1,0:T(8,128)(2,1)S(1)}, u32[]{:S(2)}, u32[]{:S(2)}) %collective-permute-start.75) | collective-permute-done | bytes 294944 | tf_op jit(solution)/shard_map/ppermute | solution.py:31
  538.4 5.6 collective-permute-done.81
  553.2 7.6 %collective-permute-done.87 = f32[32,128]{1,0:T(8,128)S(1)} collective-permute-done((f32[32,128]{1,0:T(8,128)S(1)}, f32[32,128]{1,0:T(8,128)S(1)}, u32[]{:S(2)}, u32[]{:S(2)}) %collective-permute-start.87) | collective-permute-done | bytes 16416 | tf_op jit(solution)/shard_map/ppermute | solution.py:31
  (628 shorter events, 331.2 us)
Async XLA Ops:
  12.7 48.0 %collective-permute-start = (bf16[96,768]{1,0:T(8,128)(2,1)}, bf16[96,768]{1,0:T(8,128)(2,1)}, u32[]{:S(2)}, u32[]{:S(2)}) collective-permute-start(bf16[96,768]{1,0:T(8,128)(2,1)} %param.19), channel_id=1, source_target_pairs={{0,16},{16,0},{1,17},{17,1},{2,18},{18,2},{3,19},{19,3},{4,20},{20... | collective-permute-start | bytes 442376 | tf_op jit(solution)/shard_map/ppermute | solution.py:31
  12.8 53.8 %collective-permute-start.12 = (bf16[96,768]{1,0:T(8,128)(2,1)}, bf16[96,768]{1,0:T(8,128)(2,1)}, u32[]{:S(2)}, u32[]{:S(2)}) collective-permute-start(bf16[96,768]{1,0:T(8,128)(2,1)} %bitcast.350), channel_id=1, source_target_pairs={{0,16},{16,0},{1,17},{17,1},{2,18},{18,2},{3,19},{19,3},{4,20},{20... | collective-permute-start | bytes 442376 | tf_op jit(solution)/shard_map/ppermute | solution.py:31
  17.4 68.9 %collective-permute-start.16 = (bf16[128,1536]{1,0:T(8,128)(2,1)}, bf16[128,1536]{1,0:T(8,128)(2,1)}, u32[]{:S(2)}, u32[]{:S(2)}) collective-permute-start(bf16[128,1536]{1,0:T(8,128)(2,1)} %dynamic-slice_bitcast_fusion.1), channel_id=1, source_target_pairs={{0,8},{8,0},{1,9},{9,1},{2,10},{10,2},{3,11},{11,3},{4,12},{12,4},... | collective-permute-start | bytes 1179656 | tf_op jit(solution)/shard_map/ppermute | solution.py:31
  27.3 36.7 %all-to-all-start = ((bf16[8,96,1280]{2,1,0:T(8,128)(2,1)}), bf16[8,96,1280]{2,1,0:T(8,128)(2,1)}, u32[]{:S(2)}, u32[]{:S(2)}) async-start(bf16[8,96,1280]{2,1,0:T(8,128)(2,1)} %get-tuple-element.114), calls=%async_computation | async-start | bytes 3932160 | tf_op jit(solution)/shard_map/all_to_all | solution.py:48
  31.7 204.0 %all-gather.2.cloned.1.call-start = ((), (), s32[]{:S(2)}) async-start(), calls=%async_computation.8 | async-start | bytes 5898240 | tf_op jit(solution)/shard_map/all_gather | solution.py:544
  33.9 26.7 %collective-permute-start.7 = (bf16[128,1536]{1,0:T(8,128)(2,1)S(1)}, bf16[128,1536]{1,0:T(8,128)(2,1)S(1)}, u32[]{:S(2)}, u32[]{:S(2)}) collective-permute-start(bf16[128,1536]{1,0:T(8,128)(2,1)S(1)} %dynamic-slice_bitcast_fusion.2), channel_id=1, source_target_pairs={{0,16},{16,0},{1,17},{17,1},{2,18},{18,2},{3,19},{19,3},{4,20},{20... | collective-permute-start | bytes 1179656 | tf_op jit(solution)/shard_map/ppermute | solution.py:31
  99.0 29.5 %collective-permute-start.17 = (bf16[256,1536]{1,0:T(8,128)(2,1)S(1)}, bf16[256,1536]{1,0:T(8,128)(2,1)S(1)}, u32[]{:S(2)}, u32[]{:S(2)}) collective-permute-start(bf16[256,1536]{1,0:T(8,128)(2,1)S(1)} %pad_maximum_fusion.8), channel_id=1, source_target_pairs={{0,4},{4,0},{1,5},{5,1},{2,6},{6,2},{3,7},{7,3},{8,12},{12,8},{9,1... | collective-permute-start | bytes 2359304 | tf_op jit(solution)/shard_map/ppermute | solution.py:31
  106.8 39.2 %collective-permute-start.23 = (bf16[8,96,640]{2,1,0:T(8,128)(2,1)S(1)}, bf16[8,96,640]{2,1,0:T(8,128)(2,1)}, u32[]{:S(2)}, u32[]{:S(2)}) collective-permute-start(bf16[8,96,640]{2,1,0:T(8,128)(2,1)S(1)} %copy-done.4), channel_id=1, source_target_pairs={{0,16},{16,0},{1,17},{17,1},{2,18},{18,2},{3,19},{19,3},{4,20},{20... | collective-permute-start | bytes 2949128 | tf_op jit(solution)/shard_map/ppermute | solution.py:31
  149.3 54.3 %all-to-all-start.1 = ((bf16[2,8,96,640]{3,2,0,1:T(8,128)(2,1)}), bf16[2,8,96,640]{3,2,0,1:T(8,128)(2,1)}, u32[]{:S(2)}, u32[]{:S(2)}) async-start(bf16[2,8,96,640]{3,2,0,1:T(8,128)(2,1)} %copy.130), calls=%async_computation.1 | async-start | bytes 3932160 | tf_op jit(solution)/shard_map/all_to_all | solution.py:48
  153.8 365.1 %reduce-scatter.6.cloned.1.call-start = ((), (), s32[]{:S(2)}) async-start(), calls=%async_computation.10 | async-start | bytes 2949120 | tf_op jit(solution)/shard_map/reduce_scatter | solution.py:635
  159.3 50.0 %collective-permute-start.22 = (bf16[512,1536]{1,0:T(8,128)(2,1)}, bf16[512,1536]{1,0:T(8,128)(2,1)}, u32[]{:S(2)}, u32[]{:S(2)}) collective-permute-start(bf16[512,1536]{1,0:T(8,128)(2,1)} %pad_maximum_fusion.7), channel_id=1, source_target_pairs={{0,2},{2,0},{1,3},{3,1},{4,6},{6,4},{5,7},{7,5},{8,10},{10,8},{9,1... | collective-permute-start | bytes 4718600 | tf_op jit(solution)/shard_map/ppermute | solution.py:31
  161.2 40.6 %collective-permute-start.24 = (bf16[2,2,2,96,768]{4,3,2,1,0:T(8,128)(2,1)S(1)}, bf16[2,2,2,96,768]{4,3,2,1,0:T(8,128)(2,1)S(1)}, u32[]{:S(2)}, u32[]{:S(2)}) collective-permute-start(bf16[2,2,2,96,768]{4,3,2,1,0:T(8,128)(2,1)S(1)} %maximum_select_fusion.4), channel_id=1, source_target_pairs={{0,4},{4,0},{1,5},{5,1},{2,6},{6,2},{3,7},{7,3},{8,12},{12,8},{9,1... | collective-permute-start | bytes 3538952 | tf_op jit(solution)/shard_map/ppermute | solution.py:31
  254.3 32.8 %collective-permute-start.36 = (bf16[1536,1280]{1,0:T(8,128)(2,1)S(1)}, bf16[1536,1280]{1,0:T(8,128)(2,1)S(1)}, u32[]{:S(2)}, u32[]{:S(2)}) collective-permute-start(bf16[1536,1280]{1,0:T(8,128)(2,1)S(1)} %copy-done.100), channel_id=1, source_target_pairs={{0,1},{1,0},{2,3},{3,2},{4,5},{5,4},{6,7},{7,6},{8,9},{9,8},{10,11... | collective-permute-start | bytes 11796488 | tf_op jit(solution)/shard_map/ppermute | solution.py:40
  254.9 36.4 %collective-permute-start.35 = (bf16[1536,640]{1,0:T(8,128)(2,1)S(1)}, bf16[1536,640]{1,0:T(8,128)(2,1)S(1)}, u32[]{:S(2)}, u32[]{:S(2)}) collective-permute-start(bf16[1536,640]{1,0:T(8,128)(2,1)S(1)} %bitcast.309), channel_id=1, source_target_pairs={{0,1},{1,0},{2,3},{3,2},{4,5},{5,4},{6,7},{7,6},{8,9},{9,8},{10,11... | collective-permute-start | bytes 5898248 | tf_op jit(solution)/shard_map/ppermute | solution.py:40
  314.8 229.9 %reduce-scatter.4.cloned.1.call-start = ((), (), s32[]{:S(2)}) async-start(), calls=%async_computation.9 | async-start | bytes 2949120 | tf_op jit(solution)/shard_map/reduce_scatter | solution.py:635
  348.9 222.2 %reduce-scatter.8.cloned.1.call-start = ((), (), s32[]{:S(2)}) async-start(), calls=%async_computation.11 | async-start | bytes 2949120 | tf_op jit(solution)/shard_map/reduce_scatter | solution.py:635
  371.9 108.1 %collective-permute-start.86 = (f32[128,1536]{1,0:T(8,128)S(1)}, f32[128,1536]{1,0:T(8,128)}, u32[]{:S(2)}, u32[]{:S(2)}) collective-permute-start(f32[128,1536]{1,0:T(8,128)S(1)} %copy-done.26), channel_id=1, source_target_pairs={{0,1},{1,0},{2,3},{3,2},{4,5},{5,4},{6,7},{7,6},{8,9},{9,8},{10,11... | collective-permute-start | bytes 2359304 | tf_op jit(solution)/shard_map/ppermute | solution.py:40
  424.3 36.0 %collective-permute-start.57 = (bf16[256,256]{1,0:T(8,128)(2,1)S(1)}, bf16[256,256]{1,0:T(8,128)(2,1)S(1)}, u32[]{:S(2)}, u32[]{:S(2)}) collective-permute-start(bf16[256,256]{1,0:T(8,128)(2,1)S(1)} %dynamic-slice_bitcast_fusion.14), channel_id=1, source_target_pairs={{0,16},{16,0},{1,17},{17,1},{2,18},{18,2},{3,19},{19,3},{4,20},{20... | collective-permute-start | bytes 393224 | tf_op jit(solution)/shard_map/ppermute | solution.py:31
  434.6 42.9 %collective-permute-start.60 = (bf16[2,2,2,96,384]{4,3,0,1,2:T(8,128)(2,1)S(1)}, bf16[2,2,2,96,384]{4,3,0,1,2:T(8,128)(2,1)S(1)}, u32[]{:S(2)}, u32[]{:S(2)}) collective-permute-start(bf16[2,2,2,96,384]{4,3,0,1,2:T(8,128)(2,1)S(1)} %copy_bitcast_fusion.3), channel_id=1, source_target_pairs={{0,2},{2,0},{1,3},{3,1},{4,6},{6,4},{5,7},{7,5},{8,10},{10,8},{9,1... | collective-permute-start | bytes 1769480 | tf_op jit(solution)/shard_map/ppermute | solution.py:31
  435.1 42.2 %collective-permute-start.61 = (bf16[2,2,2,96,384]{4,3,0,1,2:T(8,128)(2,1)S(1)}, bf16[2,2,2,96,384]{4,3,0,1,2:T(8,128)(2,1)S(1)}, u32[]{:S(2)}, u32[]{:S(2)}) collective-permute-start(bf16[2,2,2,96,384]{4,3,0,1,2:T(8,128)(2,1)S(1)} %copy_bitcast_fusion.2), channel_id=1, source_target_pairs={{0,4},{4,0},{1,5},{5,1},{2,6},{6,2},{3,7},{7,3},{8,12},{12,8},{9,1... | collective-permute-start | bytes 1769480 | tf_op jit(solution)/shard_map/ppermute | solution.py:31
  435.2 27.3 %collective-permute-start.71 = (bf16[2,2,96,384]{3,2,0,1:T(8,128)(2,1)S(1)}, bf16[2,2,96,384]{3,2,0,1:T(8,128)(2,1)S(1)}, u32[]{:S(2)}, u32[]{:S(2)}) collective-permute-start(bf16[2,2,96,384]{3,2,0,1:T(8,128)(2,1)S(1)} %dynamic-slice_bitcast_fusion.7), channel_id=1, source_target_pairs={{0,2},{2,0},{1,3},{3,1},{4,6},{6,4},{5,7},{7,5},{8,10},{10,8},{9,1... | collective-permute-start | bytes 884744 | tf_op jit(solution)/shard_map/ppermute | solution.py:31
  493.7 29.0 %collective-permute-start.65 = (bf16[192,1536]{1,0:T(8,128)(2,1)}, bf16[192,1536]{1,0:T(8,128)(2,1)S(1)}, u32[]{:S(2)}, u32[]{:S(2)}) collective-permute-start(bf16[192,1536]{1,0:T(8,128)(2,1)} %get-tuple-element.172), channel_id=1, source_target_pairs={{0,8},{8,0},{1,9},{9,1},{2,10},{10,2},{3,11},{11,3},{4,12},{12,4},... | collective-permute-start | bytes 1769480 | tf_op jit(solution)/shard_map/ppermute | solution.py:31
  493.9 28.8 %collective-permute-start.66 = (bf16[192,1536]{1,0:T(8,128)(2,1)}, bf16[192,1536]{1,0:T(8,128)(2,1)S(1)}, u32[]{:S(2)}, u32[]{:S(2)}) collective-permute-start(bf16[192,1536]{1,0:T(8,128)(2,1)} %get-tuple-element.173), channel_id=1, source_target_pairs={{0,2},{2,0},{1,3},{3,1},{4,6},{6,4},{5,7},{7,5},{8,10},{10,8},{9,1... | collective-permute-start | bytes 1769480 | tf_op jit(solution)/shard_map/ppermute | solution.py:31
  495.5 27.3 %collective-permute-start.67 = (bf16[128,1536]{1,0:T(8,128)(2,1)S(1)}, bf16[128,1536]{1,0:T(8,128)(2,1)}, u32[]{:S(2)}, u32[]{:S(2)}) collective-permute-start(bf16[128,1536]{1,0:T(8,128)(2,1)S(1)} %slice.353), channel_id=1, source_target_pairs={{0,4},{4,0},{1,5},{5,1},{2,6},{6,2},{3,7},{7,3},{8,12},{12,8},{9,1... | collective-permute-start | bytes 1179656 | tf_op jit(solution)/shard_map/ppermute | solution.py:31
  (181 other events, 2144.6 us)
Sparse Core Ops, SparseCore 0:
  139.3 96.3 all-gather.1
  315.0 50.3 reduce-scatter.5
  367.7 51.3 reduce-scatter.3
  421.2 56.9 reduce-scatter.7
